TPU v7x, 32 devices: a whole 2x2x4 slice. The times are simulated.
32 devices in a mesh: gx: 4 (over y, x), gy: 8 (over z, core).
Axes of the slice: x: 2, y: 2, z: 4, core: 2. Of those that a mesh axis runs over, the one named last changes fastest.
Arguments:
- labels: float32 [131072, 256], P(('gx', 'gy')), may hold values from 0 to 24, as said below
- weights: bfloat16 [1024, 12, 128, 128], P(('gx', 'gy')), may hold values from 0.001 to 1, as said below
- column_index: int32 [1024, 12], P(('gx', 'gy')), may hold values from 0 to 47, as said below
- send_index: int32 [32, 4, 4], P(('gx', 'gy')), may hold values from 0 to 31, as said below
- seed_doc: int32 [8192], P(('gx', 'gy')), may hold values from 0 to 4095
- seed_topic: int32 [8192], P(('gx', 'gy')), may hold values from 0 to 255
Outputs:
- spread: float32 [131072, 256], P(('gx', 'gy'))
Inputs may be any that keep to these rules, and one draw needn't show every extreme that they name: `column_index`: slot 0 of a row block names the row block itself (its index within the partition). A value below 32 names a block of the partition's own labels; 32 + d * 4 + s names slot s of what neighbour d hands over; only existing neighbours are named, and only in the last 3 slots. `send_index`: the 4 entries of one partition and direction are distinct. `weights`: entries are positive. `labels`: entries are nonnegative.
All inputs are finite; a program needn't handle non-finite values.
Results may differ from a plain program's by a relative error of at most 0.0004.
Values may be sent and summed in bfloat16 or wider, within the bound.
No kernel may reach another device: no remote copies, remote signals or barrier semaphores. Data moves between devices by JAX's collectives and lax.ppermute only.
A program may use at most 128 MiB of HBM per device.

v0:
```python
import jax
import jax.numpy as jnp
from jax import lax
from jax.sharding import PartitionSpec as P

ITERS = 2


ALPHA = 0.99
GAIN = 1.0 / (1.0 - 0.99)


def shifted(value, axis, steps):
    count = lax.axis_size(axis)
    initial, last = (max(0, -steps), min(count, count - steps))
    return lax.ppermute(value, axis, [(source, source + steps) for source in range(initial, last)])


def local(labels, weights, column_index, send_index, seed_doc, seed_topic):
    blocks_dev, slots, block_size, _ = weights.shape
    documents = blocks_dev * block_size
    topics = labels.shape[1]
    ones_vector = jnp.ones((block_size,), jnp.bfloat16)
    degree = jnp.einsum("rkij,j->ri", weights, ones_vector, preferred_element_type=jnp.float32)
    scale = (1.0 / jnp.sqrt(degree)).reshape(documents, 1)
    doc_hot = (seed_doc[:, None] == jnp.arange(documents, dtype=jnp.int32)[None, :]).astype(
        jnp.bfloat16
    )
    topic_hot = (seed_topic[:, None] == jnp.arange(topics, dtype=jnp.int32)[None, :]).astype(
        jnp.bfloat16
    )
    counts = lax.dot_general(
        doc_hot, topic_hot, (((0,), (0,)), ((), ())), preferred_element_type=jnp.float32
    )
    seeds = counts * GAIN
    seed_term = (1.0 - ALPHA) * seeds
    lists = send_index[0]
    current = labels
    for iteration in range(ITERS):
        scaled = (scale * current).astype(jnp.bfloat16).reshape(blocks_dev, block_size, topics)
        outgoing = scaled[lists]
        lower_inner = shifted(outgoing[1], "gy", 1)
        upper_inner = shifted(outgoing[0], "gy", -1)
        lower_outer = shifted(outgoing[3], "gx", 1)
        upper_outer = shifted(outgoing[2], "gx", -1)
        extended = jnp.concatenate(
            [scaled, lower_inner, upper_inner, lower_outer, upper_outer], axis=0
        )
        picked = extended[column_index]
        product = jnp.einsum("rkij,rkjc->ric", weights, picked, preferred_element_type=jnp.float32)
        current = ALPHA * scale * product.reshape(documents, topics) + seed_term
    return current


def solution(mesh):
    in_specs = (
        P(("gx", "gy"), None),
        P(("gx", "gy"), None, None, None),
        P(("gx", "gy"), None),
        P(("gx", "gy"), None, None),
        P(("gx", "gy")),
        P(("gx", "gy")),
    )
    out_specs = P(("gx", "gy"), None)
    return jax.shard_map(local, mesh=mesh, in_specs=in_specs, out_specs=out_specs, check_vma=False)
```

profile of v0, /device:TPU:10, one launch (start us, length us, event | category | flops | bytes accessed | tf_op | source)
XLA Modules:
  0.0 123.2 jit_solution(14103561278274709737)
XLA Ops:
  0.0 0.7 compare_select_fusion.1
  0.7 0.1 reshape.60
  0.8 7.4 %convert_reduce_fusion = bf16[32,128,128]{2,1,0:T(8,128)(2,1)S(1)} fusion(bf16[32,12,128,128]{3,2,1,0:T(8,128)(2,1)} %param.7), kind=kLoop, calls=%fused_computation.4 | loop fusion | flops 12058624 | bytes 13631488 | tf_op jit(solution)/shard_map/rkij,j->ri/reduce_sum | solution.py:24
  8.2 0.4 fusion.7
  8.5 0.0 copy-start.2
  8.6 2.6 %multiply_convert_fusion = bf16[4096,256]{1,0:T(8,128)(2,1)S(1)} fusion(f32[4096,256]{1,0:T(8,128)} %param.6, f32[4096]{0:T(1024)S(1)} %rsqrt_bitcast_fusion), kind=kLoop, calls=%fused_computation.12 | loop fusion | flops 2097152 | bytes 6307840 | tf_op jit(solution)/shard_map/convert_element_type | solution.py:40
  11.2 0.0 copy-start
  11.2 0.6 gather_fusion
  11.8 1.0 fusion.11
  12.8 2.4 %collective-permute-start.3 = (bf16[4,128,256]{2,1,0:T(8,128)(2,1)}, bf16[4,128,256]{2,1,0:T(8,128)(2,1)S(1)}, u32[]{:S(2)}, u32[]{:S(2)}) collective-permute-start(bf16[4,128,256]{2,1,0:T(8,128)(2,1)} %get-tuple-element.9), channel_id=1, source_target_pairs={{8,0},{16,8},{24,16},{9,1},{17,9},{25,17},{10,2},{18,10},{26,18},{... | collective-permute-start | bytes 786440 | tf_op jit(solution)/shard_map/ppermute | solution.py:16
  15.3 4.3 %collective-permute-start.2 = (bf16[4,128,256]{2,1,0:T(8,128)(2,1)}, bf16[4,128,256]{2,1,0:T(8,128)(2,1)}, u32[]{:S(2)}, u32[]{:S(2)}) collective-permute-start(bf16[4,128,256]{2,1,0:T(8,128)(2,1)} %get-tuple-element.10), channel_id=1, source_target_pairs={{0,8},{8,16},{16,24},{1,9},{9,17},{17,25},{2,10},{10,18},{18,26},{... | collective-permute-start | bytes 786440 | tf_op jit(solution)/shard_map/ppermute | solution.py:16
  19.6 1.9 %collective-permute-start.1 = (bf16[4,128,256]{2,1,0:T(8,128)(2,1)}, bf16[4,128,256]{2,1,0:T(8,128)(2,1)}, u32[]{:S(2)}, u32[]{:S(2)}) collective-permute-start(bf16[4,128,256]{2,1,0:T(8,128)(2,1)} %get-tuple-element.11), channel_id=1, source_target_pairs={{1,0},{2,1},{3,2},{4,3},{5,4},{6,5},{7,6},{9,8},{10,9},{11,10},{12... | collective-permute-start | bytes 786440 | tf_op jit(solution)/shard_map/ppermute | solution.py:16
  21.5 2.4 %collective-permute-start = (bf16[4,128,256]{2,1,0:T(8,128)(2,1)}, bf16[4,128,256]{2,1,0:T(8,128)(2,1)}, u32[]{:S(2)}, u32[]{:S(2)}) collective-permute-start(bf16[4,128,256]{2,1,0:T(8,128)(2,1)} %get-tuple-element.12), channel_id=1, source_target_pairs={{0,1},{1,2},{2,3},{3,4},{4,5},{5,6},{6,7},{8,9},{9,10},{10,11},{11... | collective-permute-start | bytes 786440 | tf_op jit(solution)/shard_map/ppermute | solution.py:16
  23.9 0.0 copy-done
  24.0 0.0 copy-done.2
  24.0 1.7 %constant_dynamic-update-slice_fusion.4 = bf16[48,128,256]{2,1,0:T(8,128)(2,1)S(1)} fusion(bf16[32,128,256]{2,1,0:T(8,128)(2,1)} %bitcast.44), kind=kLoop, calls=%fused_computation.22 | loop fusion | bytes 4194304
  25.7 0.1 copy.7
  25.8 0.1 reshape.68
  25.9 3.6 %collective-permute-done = bf16[4,128,256]{2,1,0:T(8,128)(2,1)} collective-permute-done((bf16[4,128,256]{2,1,0:T(8,128)(2,1)}, bf16[4,128,256]{2,1,0:T(8,128)(2,1)}, u32[]{:S(2)}, u32[]{:S(2)}) %collective-permute-start) | collective-permute-done | bytes 262176 | tf_op jit(solution)/shard_map/ppermute | solution.py:16
  29.5 1.0 constant_dynamic-update-slice_fusion.3
  30.5 0.0 collective-permute-done.1
  30.5 1.0 constant_dynamic-update-slice_fusion.2
  31.5 0.0 collective-permute-done.2
  31.5 1.0 constant_dynamic-update-slice_fusion.1
  32.5 0.0 collective-permute-done.3
  32.5 12.9 %gather_fusion.1 = bf16[384,128,256]{2,1,0:T(8,128)(2,1)} fusion(bf16[48,128,256]{2,1,0:T(8,128)(2,1)S(1)} %constant_dynamic-update-slice_fusion, s32[1024]{0:T(1024)S(1)} %pad_clamp_fusion), kind=kCustom, calls=%fused_computation.1 | custom fusion | bytes 50333184 | tf_op jit(solution)/shard_map/gather | solution.py:49
  45.4 0.0 copy-start.3
  45.4 0.0 copy-start.4
  45.4 16.5 %fusion.12 = f32[32,256,128,1]{1,2,3,0:T(8,128)} fusion(bf16[32,12,128,128]{3,2,1,0:T(8,128)(2,1)} %param.7, bf16[32,12,128,256]{3,2,1,0:T(8,128)(2,1)} %bitcast.42), kind=kOutput, calls=%fused_computation.38 | convolution fusion | flops 3221225472 | bytes 41943040 | tf_op jit(solution)/shard_map/rkij,rkjc->ric/dot_general | solution.py:50
  62.0 0.0 copy-done.3
  62.0 0.0 copy-done.4
  62.0 5.4 %fusion.3 = (bf16[4096,256]{1,0:T(8,128)(2,1)S(1)}, f32[4096,256]{1,0:T(8,128)}) fusion(f32[32,256,128,1]{1,2,3,0:T(8,128)} %fusion.12, f32[4096]{0:T(1024)S(1)} %rsqrt_bitcast_fusion, f32[4096]{0:T(1024)S(1)} %broadcast_multiply_fusion, s32[256]{0:T(256)S(1)} %copy-done.3, s32[256]{0:T(256)S(1)} %copy-done.4), kind=kOutput, calls=%fused_computation.10 | convolution fusion | flops 542179328 | bytes 10520576 | tf_op jit(solution)/shard_map/dot_general | solution.py:32
  67.4 0.0 copy-start.1
  67.4 0.6 gather_fusion.2
  68.0 0.1 fusion.10
  68.1 1.9 %collective-permute-start.4 = (bf16[4,128,256]{2,1,0:T(8,128)(2,1)S(1)}, bf16[4,128,256]{2,1,0:T(8,128)(2,1)S(1)}, u32[]{:S(2)}, u32[]{:S(2)}) collective-permute-start(bf16[4,128,256]{2,1,0:T(8,128)(2,1)S(1)} %get-tuple-element.8), channel_id=1, source_target_pairs={{0,1},{1,2},{2,3},{3,4},{4,5},{5,6},{6,7},{8,9},{9,10},{10,11},{11... | collective-permute-start | bytes 786440 | tf_op jit(solution)/shard_map/ppermute | solution.py:16
  70.0 2.5 %collective-permute-start.6 = (bf16[4,128,256]{2,1,0:T(8,128)(2,1)S(1)}, bf16[4,128,256]{2,1,0:T(8,128)(2,1)S(1)}, u32[]{:S(2)}, u32[]{:S(2)}) collective-permute-start(bf16[4,128,256]{2,1,0:T(8,128)(2,1)S(1)} %get-tuple-element.6), channel_id=1, source_target_pairs={{0,8},{8,16},{16,24},{1,9},{9,17},{17,25},{2,10},{10,18},{18,26},{... | collective-permute-start | bytes 786440 | tf_op jit(solution)/shard_map/ppermute | solution.py:16
  72.5 0.0 copy-done.1
  72.5 3.4 %collective-permute-start.5 = (bf16[4,128,256]{2,1,0:T(8,128)(2,1)S(1)}, bf16[4,128,256]{2,1,0:T(8,128)(2,1)S(1)}, u32[]{:S(2)}, u32[]{:S(2)}) collective-permute-start(bf16[4,128,256]{2,1,0:T(8,128)(2,1)S(1)} %get-tuple-element.7), channel_id=1, source_target_pairs={{1,0},{2,1},{3,2},{4,3},{5,4},{6,5},{7,6},{9,8},{10,9},{11,10},{12... | collective-permute-start | bytes 786440 | tf_op jit(solution)/shard_map/ppermute | solution.py:16
  75.9 1.7 %constant_dynamic-update-slice_fusion.9 = bf16[48,128,256]{2,1,0:T(8,128)(2,1)S(1)} fusion(bf16[32,128,256]{2,1,0:T(8,128)(2,1)} %bitcast.46), kind=kLoop, calls=%fused_computation.27 | loop fusion | bytes 4194304
  77.6 3.5 %collective-permute-start.7 = (bf16[4,128,256]{2,1,0:T(8,128)(2,1)S(1)}, bf16[4,128,256]{2,1,0:T(8,128)(2,1)S(1)}, u32[]{:S(2)}, u32[]{:S(2)}) collective-permute-start(bf16[4,128,256]{2,1,0:T(8,128)(2,1)S(1)} %get-tuple-element.5), channel_id=1, source_target_pairs={{8,0},{16,8},{24,16},{9,1},{17,9},{25,17},{10,2},{18,10},{26,18},{... | collective-permute-start | bytes 786440 | tf_op jit(solution)/shard_map/ppermute | solution.py:16
  81.2 0.0 collective-permute-done.4
  81.2 0.0 collective-permute-done.5
  81.2 0.0 collective-permute-done.6
  81.3 7.3 %collective-permute-done.7 = bf16[4,128,256]{2,1,0:T(8,128)(2,1)S(1)} collective-permute-done((bf16[4,128,256]{2,1,0:T(8,128)(2,1)S(1)}, bf16[4,128,256]{2,1,0:T(8,128)(2,1)S(1)}, u32[]{:S(2)}, u32[]{:S(2)}) %collective-permute-start.7) | collective-permute-done | bytes 262176 | tf_op jit(solution)/shard_map/ppermute | solution.py:16
  88.6 12.9 %gather_fusion.3 = bf16[384,128,256]{2,1,0:T(8,128)(2,1)} fusion(bf16[48,128,256]{2,1,0:T(8,128)(2,1)S(1)} %constant_dynamic-update-slice_fusion.5, s32[1024]{0:T(1024)S(1)} %pad_clamp_fusion), kind=kCustom, calls=%fused_computation.3 | custom fusion | bytes 50333184 | tf_op jit(solution)/shard_map/gather | solution.py:49
  101.6 16.5 %fusion.13 = f32[32,256,128,1]{1,2,3,0:T(8,128)} fusion(bf16[32,12,128,128]{3,2,1,0:T(8,128)(2,1)} %param.7, bf16[32,12,128,256]{3,2,1,0:T(8,128)(2,1)} %bitcast.41), kind=kOutput, calls=%fused_computation.39 | convolution fusion | flops 3221225472 | bytes 41943040 | tf_op jit(solution)/shard_map/rkij,rkjc->ric/dot_general | solution.py:50
  118.1 5.1 %fusion = f32[4096,256]{1,0:T(8,128)} fusion(f32[4096,256]{1,0:T(8,128)} %get-tuple-element.14, f32[32,256,128,1]{1,2,3,0:T(8,128)} %fusion.13, f32[4096]{0:T(1024)S(1)} %broadcast_multiply_fusion), kind=kLoop, calls=%fused_computation.6 | loop fusion | flops 2097152 | bytes 12599296 | tf_op jit(solution)/shard_map/add | solution.py:51
  (10 shorter events, 0.1 us)
Async XLA Ops:
  8.5 15.4 %copy-start.2 = (s32[32,12]{0,1:T(8,128)S(1)}, s32[32,12]{0,1:T(8,128)}, u32[]{:S(2)}) copy-start(s32[32,12]{0,1:T(8,128)} %param.8) | copy-start | bytes 4612
  11.2 12.8 %copy-start = (bf16[4096,256]{1,0:T(8,128)(2,1)}, bf16[4096,256]{1,0:T(8,128)(2,1)S(1)}, u32[]{:S(2)}) copy-start(bf16[4096,256]{1,0:T(8,128)(2,1)S(1)} %multiply_convert_fusion) | copy-start | bytes 6291460
  12.8 19.6 %collective-permute-start.3 = (bf16[4,128,256]{2,1,0:T(8,128)(2,1)}, bf16[4,128,256]{2,1,0:T(8,128)(2,1)S(1)}, u32[]{:S(2)}, u32[]{:S(2)}) collective-permute-start(bf16[4,128,256]{2,1,0:T(8,128)(2,1)} %get-tuple-element.9), channel_id=1, source_target_pairs={{8,0},{16,8},{24,16},{9,1},{17,9},{25,17},{10,2},{18,10},{26,18},{... | collective-permute-start | bytes 786440 | tf_op jit(solution)/shard_map/ppermute | solution.py:16
  15.3 16.2 %collective-permute-start.2 = (bf16[4,128,256]{2,1,0:T(8,128)(2,1)}, bf16[4,128,256]{2,1,0:T(8,128)(2,1)}, u32[]{:S(2)}, u32[]{:S(2)}) collective-permute-start(bf16[4,128,256]{2,1,0:T(8,128)(2,1)} %get-tuple-element.10), channel_id=1, source_target_pairs={{0,8},{8,16},{16,24},{1,9},{9,17},{17,25},{2,10},{10,18},{18,26},{... | collective-permute-start | bytes 786440 | tf_op jit(solution)/shard_map/ppermute | solution.py:16
  19.6 10.9 %collective-permute-start.1 = (bf16[4,128,256]{2,1,0:T(8,128)(2,1)}, bf16[4,128,256]{2,1,0:T(8,128)(2,1)}, u32[]{:S(2)}, u32[]{:S(2)}) collective-permute-start(bf16[4,128,256]{2,1,0:T(8,128)(2,1)} %get-tuple-element.11), channel_id=1, source_target_pairs={{1,0},{2,1},{3,2},{4,3},{5,4},{6,5},{7,6},{9,8},{10,9},{11,10},{12... | collective-permute-start | bytes 786440 | tf_op jit(solution)/shard_map/ppermute | solution.py:16
  21.5 8.0 %collective-permute-start = (bf16[4,128,256]{2,1,0:T(8,128)(2,1)}, bf16[4,128,256]{2,1,0:T(8,128)(2,1)}, u32[]{:S(2)}, u32[]{:S(2)}) collective-permute-start(bf16[4,128,256]{2,1,0:T(8,128)(2,1)} %get-tuple-element.12), channel_id=1, source_target_pairs={{0,1},{1,2},{2,3},{3,4},{4,5},{5,6},{6,7},{8,9},{9,10},{10,11},{11... | collective-permute-start | bytes 786440 | tf_op jit(solution)/shard_map/ppermute | solution.py:16
  45.4 16.5 %copy-start.3 = (s32[256]{0:T(256)S(1)}, s32[256]{0:T(256)}, u32[]{:S(2)}) copy-start(s32[256]{0:T(256)} %param.11) | copy-start | bytes 3076
  45.4 16.5 %copy-start.4 = (s32[256]{0:T(256)S(1)}, s32[256]{0:T(256)}, u32[]{:S(2)}) copy-start(s32[256]{0:T(256)} %param.10) | copy-start | bytes 3076
  67.4 5.2 %copy-start.1 = (bf16[4096,256]{1,0:T(8,128)(2,1)}, bf16[4096,256]{1,0:T(8,128)(2,1)S(1)}, u32[]{:S(2)}) copy-start(bf16[4096,256]{1,0:T(8,128)(2,1)S(1)} %get-tuple-element.13) | copy-start | bytes 6291460
  68.1 13.1 %collective-permute-start.4 = (bf16[4,128,256]{2,1,0:T(8,128)(2,1)S(1)}, bf16[4,128,256]{2,1,0:T(8,128)(2,1)S(1)}, u32[]{:S(2)}, u32[]{:S(2)}) collective-permute-start(bf16[4,128,256]{2,1,0:T(8,128)(2,1)S(1)} %get-tuple-element.8), channel_id=1, source_target_pairs={{0,1},{1,2},{2,3},{3,4},{4,5},{5,6},{6,7},{8,9},{9,10},{10,11},{11... | collective-permute-start | bytes 786440 | tf_op jit(solution)/shard_map/ppermute | solution.py:16
  70.0 11.2 %collective-permute-start.6 = (bf16[4,128,256]{2,1,0:T(8,128)(2,1)S(1)}, bf16[4,128,256]{2,1,0:T(8,128)(2,1)S(1)}, u32[]{:S(2)}, u32[]{:S(2)}) collective-permute-start(bf16[4,128,256]{2,1,0:T(8,128)(2,1)S(1)} %get-tuple-element.6), channel_id=1, source_target_pairs={{0,8},{8,16},{16,24},{1,9},{9,17},{17,25},{2,10},{10,18},{18,26},{... | collective-permute-start | bytes 786440 | tf_op jit(solution)/shard_map/ppermute | solution.py:16
  72.5 8.7 %collective-permute-start.5 = (bf16[4,128,256]{2,1,0:T(8,128)(2,1)S(1)}, bf16[4,128,256]{2,1,0:T(8,128)(2,1)S(1)}, u32[]{:S(2)}, u32[]{:S(2)}) collective-permute-start(bf16[4,128,256]{2,1,0:T(8,128)(2,1)S(1)} %get-tuple-element.7), channel_id=1, source_target_pairs={{1,0},{2,1},{3,2},{4,3},{5,4},{6,5},{7,6},{9,8},{10,9},{11,10},{12... | collective-permute-start | bytes 786440 | tf_op jit(solution)/shard_map/ppermute | solution.py:16
  77.6 11.0 %collective-permute-start.7 = (bf16[4,128,256]{2,1,0:T(8,128)(2,1)S(1)}, bf16[4,128,256]{2,1,0:T(8,128)(2,1)S(1)}, u32[]{:S(2)}, u32[]{:S(2)}) collective-permute-start(bf16[4,128,256]{2,1,0:T(8,128)(2,1)S(1)} %get-tuple-element.5), channel_id=1, source_target_pairs={{8,0},{16,8},{24,16},{9,1},{17,9},{25,17},{10,2},{18,10},{26,18},{... | collective-permute-start | bytes 786440 | tf_op jit(solution)/shard_map/ppermute | solution.py:16
where the time goes:
time: 124 us; the launch traced here: 123 us
  matrix products  38.8 us (31%)
  local copies, waits for them, and re-layouts  35 us (28%)
  starting transfers between devices  22.4 us (18%)
  other arithmetic  15.8 us (13%)
  waiting for transfers between devices  11 us (9%)
    dot_general x2, matrix products, local(): jnp.einsum('rkij,rkjc->ric', weights, picked, preferred_element_type=jnp....  33 us
    gather x2, local copies, waits for them, and re-layouts, local(): picked = extended[column_index]  25.9 us
    ppermute x8, starting transfers between devices, shifted(): lax.ppermute(value, axis, [(source, source + steps) for source in range(i...  22.4 us
    ppermute x8, waiting for transfers between devices, shifted(): lax.ppermute(value, axis, [(source, source + steps) for source in range(i...  11 us
    reduce_sum x1, other arithmetic, local(): jnp.einsum('rkij,j->ri', weights, ones_vector, preferred_element_type=jnp...  7.38 us
    unnamed x18, local copies, waits for them, and re-layouts  6.45 us
    dot_general x1, matrix products, local(): lax.dot_general(doc_hot, topic_hot, (((0,), (0,)), ((), ())), preferred_e...  5.4 us
    add x1, other arithmetic, local(): current = ALPHA * scale * product.reshape(documents, topics) + seed_term  5.13 us
  transfers between devices with their start and end apart: 8, of which 2 were waited for; matrix products, arithmetic and copies ran while one was open for 5% of the time, Pallas kernels for 0%

commit v1 on v0

v1 whole, which is shorter than its diff:
```python
import functools

import jax
import jax.numpy as jnp
from jax import lax
from jax.experimental import pallas as pl
from jax.experimental.pallas import tpu as pltpu
from jax.sharding import PartitionSpec as P

ITERS = 2

ALPHA = 0.99
GAIN = 1.0 / (1.0 - 0.99)
SEED_WEIGHT = (1.0 - ALPHA) * GAIN

LOCAL = 8
VMEM = pltpu.VMEM
IN_VMEM = pl.BlockSpec(memory_space=pltpu.VMEM)
IN_SMEM = pl.BlockSpec(memory_space=pltpu.SMEM)
ANYWHERE = pl.BlockSpec(memory_space=pl.ANY)


def call(body, out_shape, out_specs, in_specs, scratch=(), aliases=None, limit=8):
    return pl.pallas_call(
        body,
        out_shape=out_shape,
        in_specs=in_specs,
        out_specs=out_specs,
        scratch_shapes=scratch,
        input_output_aliases=aliases or {},
        compiler_params=pltpu.CompilerParams(vmem_limit_bytes=limit * 2**20),
        cost_estimate=pl.CostEstimate(flops=1, bytes_accessed=1, transcendentals=0),
    )


def pinned(value):
    return pltpu.with_memory_space_constraint(value, pltpu.VMEM)


def unmoved(value):
    return pltpu.with_memory_space_constraint(value, pltpu.HBM)


def row_scale(weights, row):
    slots = weights.shape[1]
    total = weights[row, 0].astype(jnp.float32)
    for slot in range(1, slots):
        total = total + weights[row, slot].astype(jnp.float32)
    return lax.rsqrt(jnp.sum(total, axis=1, keepdims=True))


def spread_over(scale, width):
    return jnp.concatenate([scale] * (width // scale.shape[1]), axis=1)


def toward_x(odd):
    turn = odd[0]
    return (3 - turn, 2 + turn)


def toward_y(odd):
    turn = odd[0]
    return (1 - turn, turn)


def sent_row(send_index, order, sends, i):
    return send_index[0, order[i // sends], i % sends]


def weighted(weights, extended, columns, row, first, last):
    left = jnp.concatenate([weights[row, slot] for slot in range(first, last)], axis=1)
    right = jnp.concatenate([extended[columns[slot, row]] for slot in range(first, last)], axis=0)
    return jnp.dot(left, right, preferred_element_type=jnp.float32)


def first_send_body(send_index, odd_x, weights, labels, out_a, out_b, held, block, sem):
    sends = out_a.shape[0]
    order = toward_x(odd_x)

    def copies(i):
        row = sent_row(send_index, order, sends, i)
        return (
            pltpu.make_async_copy(weights.at[row], held.at[i], sem.at[i, 0]),
            pltpu.make_async_copy(labels.at[row], block.at[i], sem.at[i, 1]),
        )

    for i in range(2 * sends):
        for copy in copies(i):
            copy.start()
    for i in range(2 * sends):
        for copy in copies(i):
            copy.wait()
        out = out_a if i < sends else out_b
        out[i % sends] = (row_scale(held, i) * block[i]).astype(jnp.bfloat16)


def degree_body(send_index, odd_y, weights, labels, held, extended, scales, out_a, out_b, block, sem, *, chunk):
    blocks_dev = weights.shape[0]
    sends = out_a.shape[0]
    chunks = blocks_dev // chunk

    def copies(c):
        part = pl.ds(c * chunk, chunk)
        return (
            pltpu.make_async_copy(weights.at[part], held.at[part], sem.at[c, 0]),
            pltpu.make_async_copy(labels.at[part], block.at[part], sem.at[c, 1]),
        )

    for c in range(chunks):
        for copy in copies(c):
            copy.start()

    def step(c, carry):
        for copy in copies(c):
            copy.wait()
        for i in range(chunk):
            row = c * chunk + i
            scale = row_scale(held, row)
            scales[row] = jnp.broadcast_to(scale, scales.shape[1:])
            extended[row] = (scale * block[row]).astype(jnp.bfloat16)
        return carry

    lax.fori_loop(0, chunks, step, 0)
    order = toward_y(odd_y)
    for i in range(sends):
        out_a[i] = extended[sent_row(send_index, order, sends, i)]
        out_b[i] = extended[sent_row(send_index, order, sends, sends + i)]


def local_body(columns, seed_doc, seed_topic, weights, extended, scales, out, topic_hot, *, unroll):
    blocks_dev, block_size, topics = out.shape
    seeds = seed_doc.shape[1]
    topic = lax.broadcasted_iota(jnp.int32, (topics, seeds), 0)
    hot = jnp.where(topic == seed_topic[...], 1.0, 0.0).astype(jnp.float32)
    topic_hot[...] = hot.T.astype(jnp.bfloat16)

    def step(row, carry):
        product = weighted(weights, extended, columns, row, 0, LOCAL)
        document = lax.broadcasted_iota(jnp.int32, (block_size, seeds), 0) + row * block_size
        doc_hot = jnp.where(document == seed_doc[...], 1.0, 0.0).astype(jnp.bfloat16)
        counts = jnp.dot(doc_hot, topic_hot[...], preferred_element_type=jnp.float32)
        factor = spread_over(ALPHA * scales[row], topics)
        out[row] = factor * product + SEED_WEIGHT * counts
        return carry

    lax.fori_loop(0, blocks_dev, step, 0, unroll=unroll)


def arrivals(received, extended, odd_x, odd_y, sem):
    sends = received[0].shape[0]
    low = extended.shape[0] - 4 * sends
    order = toward_x(odd_x) + toward_y(odd_y)
    copies = [
        pltpu.make_async_copy(value, extended.at[pl.ds(low + order[i] * sends, sends)], sem.at[i])
        for i, value in enumerate(received)
    ]
    for copy in copies:
        copy.start()
    for copy in copies:
        copy.wait()


def finished(weights, extended, columns, scales, partial, row):
    topics = partial.shape[2]
    slots = weights.shape[1]
    product = weighted(weights, extended, columns, row, LOCAL, slots)
    return partial[row] + spread_over(ALPHA * scales[row], topics) * product


def second_send_body(
    columns, send_index, odd_x, odd_y, weights, extended_in, scales, partial, r0, r1, r2, r3, out_a, out_b, extended, sem
):
    sends = out_a.shape[0]
    topics = out_a.shape[2]
    arrivals((r0, r1, r2, r3), extended, odd_x, odd_y, sem)
    order = toward_x(odd_x)
    for i in range(2 * sends):
        row = sent_row(send_index, order, sends, i)
        value = finished(weights, extended, columns, scales, partial, row)
        out = out_a if i < sends else out_b
        out[i % sends] = (spread_over(scales[row], topics) * value).astype(jnp.bfloat16)


def rest_body(columns, send_index, odd_y, weights, extended, scales, partial, following, out_a, out_b, *, unroll):
    blocks_dev, _, topics = partial.shape
    sends = out_a.shape[0]

    def step(row, carry):
        value = finished(weights, extended, columns, scales, partial, row)
        following[row] = (spread_over(scales[row], topics) * value).astype(jnp.bfloat16)
        return carry

    lax.fori_loop(0, blocks_dev, step, 0, unroll=unroll)
    order = toward_y(odd_y)
    for i in range(sends):
        out_a[i] = following[sent_row(send_index, order, sends, i)]
        out_b[i] = following[sent_row(send_index, order, sends, sends + i)]


def last_body(
    columns, odd_x, odd_y, weights, extended_in, scales, partial, r0, r1, r2, r3, out, extended, block, sem, out_sem, *, chunk
):
    blocks_dev = partial.shape[0]
    chunks = blocks_dev // chunk
    arrivals((r0, r1, r2, r3), extended, odd_x, odd_y, sem)

    def leave(c):
        part = pl.ds(c * chunk, chunk)
        return pltpu.make_async_copy(block.at[part], out.at[part], out_sem.at[c])

    def step(c, carry):
        for i in range(chunk):
            row = c * chunk + i
            block[row] = finished(weights, extended, columns, scales, partial, row)
        leave(c).start()
        return carry

    lax.fori_loop(0, chunks, step, 0)
    for c in range(chunks):
        leave(c).wait()


def swapped(value, axis, first):
    count = lax.axis_size(axis)
    pairs = []
    for low in range(first, count - 1, 2):
        pairs += [(low, low + 1), (low + 1, low)]
    return lax.ppermute(value, axis, pairs)


def local(labels, weights, column_index, send_index, seed_doc, seed_topic):
    blocks_dev, slots, block_size, _ = weights.shape
    documents = blocks_dev * block_size
    topics = labels.shape[1]
    sends = send_index.shape[2]
    seeds = seed_doc.shape[0]
    chunk = 4
    labels = unmoved(labels.reshape(blocks_dev, block_size, topics))
    weights = unmoved(weights)
    seed_doc = seed_doc.reshape(1, seeds)
    seed_topic = seed_topic.reshape(1, seeds)
    columns = column_index.T
    odd_x = (lax.axis_index("gx") % 2).reshape(1)
    odd_y = (lax.axis_index("gy") % 2).reshape(1)

    sent = VMEM((sends, block_size, topics), jnp.bfloat16)
    extended_shape = VMEM((blocks_dev + 4 * sends, block_size, topics), jnp.bfloat16)
    partial_shape = VMEM((blocks_dev, block_size, topics), jnp.float32)

    xa, xb = call(
        first_send_body,
        (sent, sent),
        (IN_VMEM, IN_VMEM),
        (IN_SMEM, IN_SMEM, ANYWHERE, ANYWHERE),
        (
            pltpu.VMEM((2 * sends, slots, block_size, block_size), jnp.bfloat16),
            pltpu.VMEM((2 * sends, block_size, topics), jnp.float32),
            pltpu.SemaphoreType.DMA((2 * sends, 2)),
        ),
    )(send_index, odd_x, weights, labels)
    xa, xb = swapped(xa, "gx", 0), swapped(xb, "gx", 1)

    held, extended, scales, ya, yb = call(
        functools.partial(degree_body, chunk=chunk),
        (
            VMEM(weights.shape, jnp.bfloat16),
            extended_shape,
            VMEM((blocks_dev, block_size, block_size), jnp.float32),
            sent,
            sent,
        ),
        (IN_VMEM,) * 5,
        (IN_SMEM, IN_SMEM, ANYWHERE, ANYWHERE),
        (
            pltpu.VMEM((blocks_dev, block_size, topics), jnp.float32),
            pltpu.SemaphoreType.DMA((blocks_dev // chunk, 2)),
        ),
    )(send_index, odd_y, weights, labels)
    ya, yb = swapped(ya, "gy", 0), swapped(yb, "gy", 1)

    def near(extended):
        return call(
            functools.partial(local_body, unroll=4),
            partial_shape,
            IN_VMEM,
            (IN_SMEM, IN_VMEM, IN_VMEM, IN_VMEM, IN_VMEM, IN_VMEM),
            (pltpu.VMEM((seeds, topics), jnp.bfloat16),),
        )(columns, seed_doc, seed_topic, pinned(held), pinned(extended), pinned(scales))

    partial = near(extended)
    xa, xb, extended = call(
        second_send_body,
        (sent, sent, extended_shape),
        (IN_VMEM,) * 3,
        (IN_SMEM,) * 4 + (IN_VMEM,) * 4 + (ANYWHERE,) * 4,
        (pltpu.SemaphoreType.DMA((4,)),),
        aliases={5: 2},
    )(columns, send_index, odd_x, odd_y, pinned(held), pinned(extended), pinned(scales), pinned(partial), xa, xb, ya, yb)
    xa, xb = swapped(xa, "gx", 0), swapped(xb, "gx", 1)

    following, ya, yb = call(
        functools.partial(rest_body, unroll=4),
        (extended_shape, sent, sent),
        (IN_VMEM,) * 3,
        (IN_SMEM,) * 3 + (IN_VMEM,) * 4,
    )(columns, send_index, odd_y, pinned(held), pinned(extended), pinned(scales), pinned(partial))
    ya, yb = swapped(ya, "gy", 0), swapped(yb, "gy", 1)

    partial = near(following)
    out, _ = call(
        functools.partial(last_body, chunk=chunk),
        (jax.ShapeDtypeStruct((blocks_dev, block_size, topics), jnp.float32), extended_shape),
        (ANYWHERE, IN_VMEM),
        (IN_SMEM,) * 3 + (IN_VMEM,) * 4 + (ANYWHERE,) * 4,
        (
            pltpu.VMEM((blocks_dev, block_size, topics), jnp.float32),
            pltpu.SemaphoreType.DMA((4,)),
            pltpu.SemaphoreType.DMA((blocks_dev // chunk,)),
        ),
        aliases={4: 1},
    )(columns, odd_x, odd_y, pinned(held), pinned(following), pinned(scales), pinned(partial), xa, xb, ya, yb)
    return out.reshape(documents, topics)


def solution(mesh):
    in_specs = (
        P(("gx", "gy"), None),
        P(("gx", "gy"), None, None, None),
        P(("gx", "gy"), None),
        P(("gx", "gy"), None, None),
        P(("gx", "gy")),
        P(("gx", "gy")),
    )
    out_specs = P(("gx", "gy"), None)
    return jax.shard_map(local, mesh=mesh, in_specs=in_specs, out_specs=out_specs, check_vma=False)
```

time: 124 us -> 50.2 us (0.40)
  the two profiles are of different devices: /device:TPU:10 before, /device:TPU:13 now
where the time goes in v1:
time: 50.2 us; the launch traced here: 50.1 us
  Pallas kernels  29.3 us (58%)
  starting transfers between devices  15.6 us (31%)
  waiting for transfers between devices  4.34 us (9%)
  local copies, waits for them, and re-layouts  0.7 us (1%)
    ppermute x8, starting transfers between devices, swapped(): return lax.ppermute(value, axis, pairs)  15.6 us
    pallas_call x2, Pallas kernels, near(): call(functools.partial(local_body, unroll=4), partial_shape, IN_VMEM, (IN...  10.5 us
    pallas_call x1, Pallas kernels, local(): call(functools.partial(degree_body, chunk=chunk), (VMEM(weights.shape, jn...  6.78 us
    ppermute x8, waiting for transfers between devices, swapped(): return lax.ppermute(value, axis, pairs)  4.34 us
    pallas_call x1, Pallas kernels, local(): call(functools.partial(last_body, chunk=chunk), (jax.ShapeDtypeStruct((bl...  4.24 us
    pallas_call x1, Pallas kernels, local(): call(functools.partial(rest_body, unroll=4), (extended_shape, sent, sent)...  3.37 us
    pallas_call x1, Pallas kernels, local(): call(first_send_body, (sent, sent), (IN_VMEM, IN_VMEM), (IN_SMEM, IN_SMEM...  3 us
    pallas_call x1, Pallas kernels, local(): call(second_send_body, (sent, sent, extended_shape), (IN_VMEM,) * 3, (IN_...  1.39 us
  transfers between devices with their start and end apart: 8, of which 1 were waited for; matrix products, arithmetic and copies ran while one was open for 0% of the time, Pallas kernels for 34%

profile of v1, /device:TPU:13, one launch (start us, length us, event | category | flops | bytes accessed | tf_op | source)
XLA Modules:
  0.0 50.1 jit_solution(5883026585319596996)
XLA Ops:
  0.0 0.0 copy-start.1
  0.0 0.7 %copy-done.1 = s32[1,4,4]{2,1,0:T(4,128)S(1)} copy-done((s32[1,4,4]{2,1,0:T(4,128)S(1)}, s32[1,4,4]{2,1,0:T(4,128)}, u32[]{:S(2)}) %copy-start.1) | copy-done | bytes 88
  0.7 0.0 copy-start.2
  0.7 3.0 %shard_map.66 = (bf16[4,128,256]{2,1,0:T(8,128)(2,1)S(1)}, bf16[4,128,256]{2,1,0:T(8,128)(2,1)S(1)}) custom-call(s32[1,4,4]{2,1,0:T(4,128)S(1)} %copy-done.1, s32[1]{0:T(128)} %bitcast.1.odd_x, bf16[32,12,128,128]{3,2,1,0:T(8,128)(2,1)} %weights.3, f32[32,128,256]{2,1,0:T(8,128)} %bitcast.16), custom_call_target="tpu_custom_call" | custom-call | flops 1 | bytes 1 | tf_op jit(solution)/shard_map/pallas_call | solution.py:250
  3.7 1.3 %collective-permute-start = (bf16[4,128,256]{2,1,0:T(8,128)(2,1)S(1)}, bf16[4,128,256]{2,1,0:T(8,128)(2,1)S(1)}, u32[]{:S(2)}, u32[]{:S(2)}) collective-permute-start(bf16[4,128,256]{2,1,0:T(8,128)(2,1)S(1)} %get-tuple-element.22), channel_id=1, source_target_pairs={{0,8},{8,0},{16,24},{24,16},{1,9},{9,1},{17,25},{25,17},{2,10},{10... | collective-permute-start | bytes 786440 | tf_op jit(solution)/shard_map/ppermute | solution.py:228
  5.0 2.2 %collective-permute-start.1 = (bf16[4,128,256]{2,1,0:T(8,128)(2,1)S(1)}, bf16[4,128,256]{2,1,0:T(8,128)(2,1)S(1)}, u32[]{:S(2)}, u32[]{:S(2)}) collective-permute-start(bf16[4,128,256]{2,1,0:T(8,128)(2,1)S(1)} %get-tuple-element.23), channel_id=1, source_target_pairs={{8,16},{16,8},{9,17},{17,9},{10,18},{18,10},{11,19},{19,11},{12,20... | collective-permute-start | bytes 786440 | tf_op jit(solution)/shard_map/ppermute | solution.py:228
  7.1 0.0 copy-done.2
  7.2 0.0 copy-start
  7.2 0.0 copy-start.3
  7.2 0.0 copy-start.4
  7.2 6.8 %shard_map.64 = (bf16[32,12,128,128]{3,2,1,0:T(8,128)(2,1)S(1)}, bf16[48,128,256]{2,1,0:T(8,128)(2,1)S(1)}, f32[32,128,128]{2,1,0:T(8,128)S(1)}, bf16[4,128,256]...) custom-call(s32[1,4,4]{2,1,0:T(4,128)S(1)} %copy-done.2, s32[1]{0:T(128)} %bitcast.2.odd_y, bf16[32,12,128,128]{3,2,1,0:T(8,128)(2,1)} %weights.3, ...), custom_call_target="tpu_custom_call" | custom-call | flops 1 | bytes 1 | tf_op jit(solution)/shard_map/pallas_call | solution.py:263
  14.0 1.2 %collective-permute-start.2 = (bf16[4,128,256]{2,1,0:T(8,128)(2,1)S(1)}, bf16[4,128,256]{2,1,0:T(8,128)(2,1)S(1)}, u32[]{:S(2)}, u32[]{:S(2)}) collective-permute-start(bf16[4,128,256]{2,1,0:T(8,128)(2,1)S(1)} %get-tuple-element.24), channel_id=1, source_target_pairs={{0,1},{1,0},{2,3},{3,2},{4,5},{5,4},{6,7},{7,6},{8,9},{9,8},{10,11... | collective-permute-start | bytes 786440 | tf_op jit(solution)/shard_map/ppermute | solution.py:228
  15.2 3.1 %collective-permute-start.3 = (bf16[4,128,256]{2,1,0:T(8,128)(2,1)S(1)}, bf16[4,128,256]{2,1,0:T(8,128)(2,1)S(1)}, u32[]{:S(2)}, u32[]{:S(2)}) collective-permute-start(bf16[4,128,256]{2,1,0:T(8,128)(2,1)S(1)} %get-tuple-element.25), channel_id=1, source_target_pairs={{1,2},{2,1},{3,4},{4,3},{5,6},{6,5},{9,10},{10,9},{11,12},{12,11},... | collective-permute-start | bytes 786440 | tf_op jit(solution)/shard_map/ppermute | solution.py:228
  18.3 0.0 copy-done
  18.3 0.0 copy-done.3
  18.3 0.0 copy-done.4
  18.4 5.2 %shard_map.65.partial = f32[32,128,256]{2,1,0:T(8,128)S(1)} custom-call(s32[12,32]{1,0:T(8,128)S(1)} %bitcast.7, s32[1,256]{1,0:T(1,128)S(1)} %bitcast.12, s32[1,256]{1,0:T(1,128)S(1)} %bitcast.14, bf16[32,12,128,128]{3,2,1,0:T(8,128)(2,1)S(1)} %get-tuple-element.19.weights, bf16[48,128,256]{2,1,0:T(8,128)(2,1)S(1)} %get-tuple-element.20.extended.extended_in, ...), custom_call_target="tpu_custom_call" | custom-call | flops 1 | bytes 1 | tf_op jit(solution)/shard_map/pallas_call | solution.py:282
  23.6 0.0 collective-permute-done.r0
  23.6 0.0 collective-permute-done.1.r1
  23.6 0.0 collective-permute-done.2.r2
  23.6 0.0 collective-permute-done.3.r3
  23.6 1.4 %shard_map.67 = (bf16[4,128,256]{2,1,0:T(8,128)(2,1)S(1)}, bf16[4,128,256]{2,1,0:T(8,128)(2,1)S(1)}, bf16[48,128,256]{2,1,0:T(8,128)(2,1)S(1)}) custom-call(s32[12,32]{1,0:T(8,128)S(1)} %bitcast.8, s32[1,4,4]{2,1,0:T(4,128)S(1)} %copy-done.2, s32[1]{0:T(128)} %bitcast.1.odd_x, s32[1]{0:T(128)} %bitcast.2.odd_y, ...), custom_call_target="tpu_custom_call", output_to_operand_aliasing={{2}: (5, {})} | custom-call | flops 1 | bytes 1 | tf_op jit(solution)/shard_map/pallas_call | solution.py:291
  25.0 3.4 %shard_map.68 = (bf16[48,128,256]{2,1,0:T(8,128)(2,1)S(1)}, bf16[4,128,256]{2,1,0:T(8,128)(2,1)S(1)}, bf16[4,128,256]{2,1,0:T(8,128)(2,1)S(1)}) custom-call(s32[12,32]{1,0:T(8,128)S(1)} %bitcast.9, s32[1,4,4]{2,1,0:T(4,128)S(1)} %copy-done.2, s32[1]{0:T(128)} %bitcast.2.odd_y, bf16[32,12,128,128]{3,2,1,0:T(8,128)(2,1)S(1)} %get-tuple-element.19.weights, ...), custom_call_target="tpu_custom_call" | custom-call | flops 1 | bytes 1 | tf_op jit(solution)/shard_map/pallas_call | solution.py:301
  28.4 0.1 collective-permute-start.6
  28.5 3.6 %collective-permute-start.7 = (bf16[4,128,256]{2,1,0:T(8,128)(2,1)S(1)}, bf16[4,128,256]{2,1,0:T(8,128)(2,1)S(1)}, u32[]{:S(2)}, u32[]{:S(2)}) collective-permute-start(bf16[4,128,256]{2,1,0:T(8,128)(2,1)S(1)} %get-tuple-element.31), channel_id=1, source_target_pairs={{1,2},{2,1},{3,4},{4,3},{5,6},{6,5},{9,10},{10,9},{11,12},{12,11},... | collective-permute-start | bytes 786440 | tf_op jit(solution)/shard_map/ppermute | solution.py:228
  32.1 0.1 collective-permute-start.4
  32.2 4.1 %collective-permute-start.5 = (bf16[4,128,256]{2,1,0:T(8,128)(2,1)S(1)}, bf16[4,128,256]{2,1,0:T(8,128)(2,1)S(1)}, u32[]{:S(2)}, u32[]{:S(2)}) collective-permute-start(bf16[4,128,256]{2,1,0:T(8,128)(2,1)S(1)} %get-tuple-element.29), channel_id=1, source_target_pairs={{8,16},{16,8},{9,17},{17,9},{10,18},{18,10},{11,19},{19,11},{12,20... | collective-permute-start | bytes 786440 | tf_op jit(solution)/shard_map/ppermute | solution.py:228
  36.2 5.2 %shard_map.69.partial = f32[32,128,256]{2,1,0:T(8,128)S(1)} custom-call(s32[12,32]{1,0:T(8,128)S(1)} %bitcast.10, s32[1,256]{1,0:T(1,128)S(1)} %bitcast.13, s32[1,256]{1,0:T(1,128)S(1)} %bitcast.15, bf16[32,12,128,128]{3,2,1,0:T(8,128)(2,1)S(1)} %get-tuple-element.19.weights, bf16[48,128,256]{2,1,0:T(8,128)(2,1)S(1)} %get-tuple-element.27.extended.extended_in, ...), custom_call_target="tpu_custom_call" | custom-call | flops 1 | bytes 1 | tf_op jit(solution)/shard_map/pallas_call | solution.py:282
  41.5 0.0 collective-permute-done.6.r2
  41.5 0.0 collective-permute-done.7.r3
  41.5 0.0 collective-permute-done.4.r0
  41.5 4.3 %collective-permute-done.5.r1 = bf16[4,128,256]{2,1,0:T(8,128)(2,1)S(1)} collective-permute-done((bf16[4,128,256]{2,1,0:T(8,128)(2,1)S(1)}, bf16[4,128,256]{2,1,0:T(8,128)(2,1)S(1)}, u32[]{:S(2)}, u32[]{:S(2)}) %collective-permute-start.5) | collective-permute-done | bytes 262176 | tf_op jit(solution)/shard_map/ppermute | solution.py:228
  45.8 4.2 %shard_map.70 = (f32[32,128,256]{2,1,0:T(8,128)}, bf16[48,128,256]{2,1,0:T(8,128)(2,1)S(1)}) custom-call(s32[12,32]{1,0:T(8,128)S(1)} %bitcast.11, s32[1]{0:T(128)} %bitcast.1.odd_x, s32[1]{0:T(128)} %bitcast.2.odd_y, bf16[32,12,128,128]{3,2,1,0:T(8,128)(2,1)S(1)} %get-tuple-element.19.weights, ...), custom_call_target="tpu_custom_call", output_to_operand_aliasing={{1}: (4, {})} | custom-call | flops 1 | bytes 1 | tf_op jit(solution)/shard_map/pallas_call | solution.py:310
Async XLA Ops:
  0.0 0.7 %copy-start.1 = (s32[1,4,4]{2,1,0:T(4,128)S(1)}, s32[1,4,4]{2,1,0:T(4,128)}, u32[]{:S(2)}) copy-start(s32[1,4,4]{2,1,0:T(4,128)} %send_index.7) | copy-start | bytes 196
  0.7 6.5 %copy-start.2 = (s32[1,4,4]{2,1,0:T(4,128)S(1)}, s32[1,4,4]{2,1,0:T(4,128)}, u32[]{:S(2)}) copy-start(s32[1,4,4]{2,1,0:T(4,128)} %send_index.7) | copy-start | bytes 196
  3.7 19.9 %collective-permute-start = (bf16[4,128,256]{2,1,0:T(8,128)(2,1)S(1)}, bf16[4,128,256]{2,1,0:T(8,128)(2,1)S(1)}, u32[]{:S(2)}, u32[]{:S(2)}) collective-permute-start(bf16[4,128,256]{2,1,0:T(8,128)(2,1)S(1)} %get-tuple-element.22), channel_id=1, source_target_pairs={{0,8},{8,0},{16,24},{24,16},{1,9},{9,1},{17,25},{25,17},{2,10},{10... | collective-permute-start | bytes 786440 | tf_op jit(solution)/shard_map/ppermute | solution.py:228
  5.0 18.7 %collective-permute-start.1 = (bf16[4,128,256]{2,1,0:T(8,128)(2,1)S(1)}, bf16[4,128,256]{2,1,0:T(8,128)(2,1)S(1)}, u32[]{:S(2)}, u32[]{:S(2)}) collective-permute-start(bf16[4,128,256]{2,1,0:T(8,128)(2,1)S(1)} %get-tuple-element.23), channel_id=1, source_target_pairs={{8,16},{16,8},{9,17},{17,9},{10,18},{18,10},{11,19},{19,11},{12,20... | collective-permute-start | bytes 786440 | tf_op jit(solution)/shard_map/ppermute | solution.py:228
  7.2 11.2 %copy-start = (s32[32,12]{0,1:T(8,128)S(1)}, s32[32,12]{0,1:T(8,128)}, u32[]{:S(2)}) copy-start(s32[32,12]{0,1:T(8,128)} %param.8) | copy-start | bytes 4612
  7.2 11.2 %copy-start.3 = (s32[256]{0:T(256)S(1)}, s32[256]{0:T(256)}, u32[]{:S(2)}) copy-start(s32[256]{0:T(256)} %param.10) | copy-start | bytes 3076
  7.2 11.2 %copy-start.4 = (s32[256]{0:T(256)S(1)}, s32[256]{0:T(256)}, u32[]{:S(2)}) copy-start(s32[256]{0:T(256)} %param.11) | copy-start | bytes 3076
  14.0 9.7 %collective-permute-start.2 = (bf16[4,128,256]{2,1,0:T(8,128)(2,1)S(1)}, bf16[4,128,256]{2,1,0:T(8,128)(2,1)S(1)}, u32[]{:S(2)}, u32[]{:S(2)}) collective-permute-start(bf16[4,128,256]{2,1,0:T(8,128)(2,1)S(1)} %get-tuple-element.24), channel_id=1, source_target_pairs={{0,1},{1,0},{2,3},{3,2},{4,5},{5,4},{6,7},{7,6},{8,9},{9,8},{10,11... | collective-permute-start | bytes 786440 | tf_op jit(solution)/shard_map/ppermute | solution.py:228
  15.2 8.4 %collective-permute-start.3 = (bf16[4,128,256]{2,1,0:T(8,128)(2,1)S(1)}, bf16[4,128,256]{2,1,0:T(8,128)(2,1)S(1)}, u32[]{:S(2)}, u32[]{:S(2)}) collective-permute-start(bf16[4,128,256]{2,1,0:T(8,128)(2,1)S(1)} %get-tuple-element.25), channel_id=1, source_target_pairs={{1,2},{2,1},{3,4},{4,3},{5,6},{6,5},{9,10},{10,9},{11,12},{12,11},... | collective-permute-start | bytes 786440 | tf_op jit(solution)/shard_map/ppermute | solution.py:228
  28.4 13.1 %collective-permute-start.6 = (bf16[4,128,256]{2,1,0:T(8,128)(2,1)S(1)}, bf16[4,128,256]{2,1,0:T(8,128)(2,1)S(1)}, u32[]{:S(2)}, u32[]{:S(2)}) collective-permute-start(bf16[4,128,256]{2,1,0:T(8,128)(2,1)S(1)} %get-tuple-element.30), channel_id=1, source_target_pairs={{0,1},{1,0},{2,3},{3,2},{4,5},{5,4},{6,7},{7,6},{8,9},{9,8},{10,11... | collective-permute-start | bytes 786440 | tf_op jit(solution)/shard_map/ppermute | solution.py:228
  28.5 13.0 %collective-permute-start.7 = (bf16[4,128,256]{2,1,0:T(8,128)(2,1)S(1)}, bf16[4,128,256]{2,1,0:T(8,128)(2,1)S(1)}, u32[]{:S(2)}, u32[]{:S(2)}) collective-permute-start(bf16[4,128,256]{2,1,0:T(8,128)(2,1)S(1)} %get-tuple-element.31), channel_id=1, source_target_pairs={{1,2},{2,1},{3,4},{4,3},{5,6},{6,5},{9,10},{10,9},{11,12},{12,11},... | collective-permute-start | bytes 786440 | tf_op jit(solution)/shard_map/ppermute | solution.py:228
  32.1 9.4 %collective-permute-start.4 = (bf16[4,128,256]{2,1,0:T(8,128)(2,1)S(1)}, bf16[4,128,256]{2,1,0:T(8,128)(2,1)S(1)}, u32[]{:S(2)}, u32[]{:S(2)}) collective-permute-start(bf16[4,128,256]{2,1,0:T(8,128)(2,1)S(1)} %get-tuple-element.28), channel_id=1, source_target_pairs={{0,8},{8,0},{16,24},{24,16},{1,9},{9,1},{17,25},{25,17},{2,10},{10... | collective-permute-start | bytes 786440 | tf_op jit(solution)/shard_map/ppermute | solution.py:228
  32.2 13.7 %collective-permute-start.5 = (bf16[4,128,256]{2,1,0:T(8,128)(2,1)S(1)}, bf16[4,128,256]{2,1,0:T(8,128)(2,1)S(1)}, u32[]{:S(2)}, u32[]{:S(2)}) collective-permute-start(bf16[4,128,256]{2,1,0:T(8,128)(2,1)S(1)} %get-tuple-element.29), channel_id=1, source_target_pairs={{8,16},{16,8},{9,17},{17,9},{10,18},{18,10},{11,19},{19,11},{12,20... | collective-permute-start | bytes 786440 | tf_op jit(solution)/shard_map/ppermute | solution.py:228

commit v2 on v1

--- a/solution.py
+++ b/solution.py
@@ -94,8 +94,12 @@
         out[i % sends] = (row_scale(held, i) * block[i]).astype(jnp.bfloat16)
 
 
-def degree_body(send_index, odd_y, weights, labels, held, extended, scales, out_a, out_b, block, sem, *, chunk):
-    blocks_dev = weights.shape[0]
+def degree_body(
+    send_index, odd_y, seed_doc, seed_topic, weights, labels, held, extended, scales, counts, out_a, out_b,
+    block, topic_hot, sem, *, chunk,
+):
+    blocks_dev, block_size, topics = labels.shape
+    seeds = seed_doc.shape[1]
     sends = out_a.shape[0]
     chunks = blocks_dev // chunk
 
@@ -109,6 +113,9 @@
     for c in range(chunks):
         for copy in copies(c):
             copy.start()
+    topic = lax.broadcasted_iota(jnp.int32, (topics, seeds), 0)
+    hot = jnp.where(topic == seed_topic[...], 1.0, 0.0).astype(jnp.float32)
+    topic_hot[...] = hot.T.astype(jnp.bfloat16)
 
     def step(c, carry):
         for copy in copies(c):
@@ -118,6 +125,10 @@
             scale = row_scale(held, row)
             scales[row] = jnp.broadcast_to(scale, scales.shape[1:])
             extended[row] = (scale * block[row]).astype(jnp.bfloat16)
+            document = lax.broadcasted_iota(jnp.int32, (block_size, seeds), 0) + row * block_size
+            doc_hot = jnp.where(document == seed_doc[...], 1.0, 0.0).astype(jnp.bfloat16)
+            hits = jnp.dot(doc_hot, topic_hot[...], preferred_element_type=jnp.float32)
+            counts[row] = hits.astype(jnp.bfloat16)
         return carry
 
     lax.fori_loop(0, chunks, step, 0)
@@ -127,23 +138,18 @@
         out_b[i] = extended[sent_row(send_index, order, sends, sends + i)]
 
 
-def local_body(columns, seed_doc, seed_topic, weights, extended, scales, out, topic_hot, *, unroll):
-    blocks_dev, block_size, topics = out.shape
-    seeds = seed_doc.shape[1]
-    topic = lax.broadcasted_iota(jnp.int32, (topics, seeds), 0)
-    hot = jnp.where(topic == seed_topic[...], 1.0, 0.0).astype(jnp.float32)
-    topic_hot[...] = hot.T.astype(jnp.bfloat16)
-
+def near(weights, extended, columns, scales, counts, row):
+    topics = extended.shape[2]
+    product = weighted(weights, extended, columns, row, 0, LOCAL)
+    return spread_over(ALPHA * scales[row], topics) * product + SEED_WEIGHT * counts[row].astype(jnp.float32)
+
+
+def near_body(columns, weights, extended, scales, counts, partial, *, unroll):
     def step(row, carry):
-        product = weighted(weights, extended, columns, row, 0, LOCAL)
-        document = lax.broadcasted_iota(jnp.int32, (block_size, seeds), 0) + row * block_size
-        doc_hot = jnp.where(document == seed_doc[...], 1.0, 0.0).astype(jnp.bfloat16)
-        counts = jnp.dot(doc_hot, topic_hot[...], preferred_element_type=jnp.float32)
-        factor = spread_over(ALPHA * scales[row], topics)
-        out[row] = factor * product + SEED_WEIGHT * counts
-        return carry
-
-    lax.fori_loop(0, blocks_dev, step, 0, unroll=unroll)
+        partial[row] = near(weights, extended, columns, scales, counts, row)
+        return carry
+
+    lax.fori_loop(0, partial.shape[0], step, 0, unroll=unroll)
 
 
 def arrivals(received, extended, odd_x, odd_y, sem):
@@ -168,33 +174,34 @@
 
 
 def second_send_body(
-    columns, send_index, odd_x, odd_y, weights, extended_in, scales, partial, r0, r1, r2, r3, out_a, out_b, extended, sem
+    columns, send_index, odd_x, odd_y, weights, extended_in, scales, partial, r0, r1, r2, r3,
+    x_a, x_b, y_a, y_b, extended, sem,
 ):
-    sends = out_a.shape[0]
-    topics = out_a.shape[2]
+    sends = x_a.shape[0]
+    topics = x_a.shape[2]
     arrivals((r0, r1, r2, r3), extended, odd_x, odd_y, sem)
-    order = toward_x(odd_x)
-    for i in range(2 * sends):
+    outs = (x_a, x_b, y_a, y_b)
+    order = toward_x(odd_x) + toward_y(odd_y)
+    for i in range(len(outs) * sends):
         row = sent_row(send_index, order, sends, i)
         value = finished(weights, extended, columns, scales, partial, row)
-        out = out_a if i < sends else out_b
-        out[i % sends] = (spread_over(scales[row], topics) * value).astype(jnp.bfloat16)
-
-
-def rest_body(columns, send_index, odd_y, weights, extended, scales, partial, following, out_a, out_b, *, unroll):
+        outs[i // sends][i % sends] = (spread_over(scales[row], topics) * value).astype(jnp.bfloat16)
+
+
+def rest_body(columns, weights, extended, scales, counts, partial, following, next_partial, *, unroll):
     blocks_dev, _, topics = partial.shape
-    sends = out_a.shape[0]
-
-    def step(row, carry):
+
+    def finish(row, carry):
         value = finished(weights, extended, columns, scales, partial, row)
         following[row] = (spread_over(scales[row], topics) * value).astype(jnp.bfloat16)
         return carry
 
-    lax.fori_loop(0, blocks_dev, step, 0, unroll=unroll)
-    order = toward_y(odd_y)
-    for i in range(sends):
-        out_a[i] = following[sent_row(send_index, order, sends, i)]
-        out_b[i] = following[sent_row(send_index, order, sends, sends + i)]
+    def start(row, carry):
+        next_partial[row] = near(weights, following, columns, scales, counts, row)
+        return carry
+
+    lax.fori_loop(0, blocks_dev, finish, 0, unroll=unroll)
+    lax.fori_loop(0, blocks_dev, start, 0, unroll=unroll)
 
 
 def last_body(
@@ -220,12 +227,28 @@
         leave(c).wait()
 
 
+def swap_pairs(axis, first):
+    outer, inner = lax.axis_size("gx"), lax.axis_size("gy")
+    count, other = (outer, inner) if axis == "gx" else (inner, outer)
+    lines = []
+    for low in range(first, count - 1, 2):
+        lines += [((low, line), (low + 1, line)) for line in range(other)]
+    alone = [place for place in range(count) if all(place not in (p[0], q[0]) for p, q in lines)]
+    half = 1 if axis == "gx" else other // 2
+    for place in alone:
+        for line in range(other):
+            if line // half % 2 == 0 and line + half < other:
+                lines.append(((place, line), (place, line + half)))
+    number = (lambda place, line: place * inner + line) if axis == "gx" else (lambda place, line: line * inner + place)
+    pairs = []
+    for p, q in lines:
+        low, high = number(*p), number(*q)
+        pairs += [(low, high), (high, low)]
+    return sorted(pairs)
+
+
 def swapped(value, axis, first):
-    count = lax.axis_size(axis)
-    pairs = []
-    for low in range(first, count - 1, 2):
-        pairs += [(low, low + 1), (low + 1, low)]
-    return lax.ppermute(value, axis, pairs)
+    return lax.ppermute(value, ("gx", "gy"), swap_pairs(axis, first))
 
 
 def local(labels, weights, column_index, send_index, seed_doc, seed_topic):
@@ -234,9 +257,7 @@
     topics = labels.shape[1]
     sends = send_index.shape[2]
     seeds = seed_doc.shape[0]
-    chunk = 4
-    labels = unmoved(labels.reshape(blocks_dev, block_size, topics))
-    weights = unmoved(weights)
+    labels = labels.reshape(blocks_dev, block_size, topics)
     seed_doc = seed_doc.reshape(1, seeds)
     seed_topic = seed_topic.reshape(1, seeds)
     columns = column_index.T
@@ -245,6 +266,8 @@
 
     sent = VMEM((sends, block_size, topics), jnp.bfloat16)
     extended_shape = VMEM((blocks_dev + 4 * sends, block_size, topics), jnp.bfloat16)
+    scale_shape = VMEM((blocks_dev, block_size, block_size), jnp.float32)
+    count_shape = VMEM((blocks_dev, block_size, topics), jnp.bfloat16)
     partial_shape = VMEM((blocks_dev, block_size, topics), jnp.float32)
 
     xa, xb = call(
@@ -257,68 +280,59 @@
             pltpu.VMEM((2 * sends, block_size, topics), jnp.float32),
             pltpu.SemaphoreType.DMA((2 * sends, 2)),
         ),
-    )(send_index, odd_x, weights, labels)
+    )(send_index, odd_x, unmoved(weights), unmoved(labels))
     xa, xb = swapped(xa, "gx", 0), swapped(xb, "gx", 1)
 
-    held, extended, scales, ya, yb = call(
-        functools.partial(degree_body, chunk=chunk),
-        (
-            VMEM(weights.shape, jnp.bfloat16),
-            extended_shape,
-            VMEM((blocks_dev, block_size, block_size), jnp.float32),
-            sent,
-            sent,
-        ),
-        (IN_VMEM,) * 5,
-        (IN_SMEM, IN_SMEM, ANYWHERE, ANYWHERE),
+    held, extended, scales, counts, ya, yb = call(
+        functools.partial(degree_body, chunk=4),
+        (VMEM(weights.shape, jnp.bfloat16), extended_shape, scale_shape, count_shape, sent, sent),
+        (IN_VMEM,) * 6,
+        (IN_SMEM,) * 2 + (IN_VMEM,) * 2 + (ANYWHERE,) * 2,
         (
             pltpu.VMEM((blocks_dev, block_size, topics), jnp.float32),
-            pltpu.SemaphoreType.DMA((blocks_dev // chunk, 2)),
+            pltpu.VMEM((seeds, topics), jnp.bfloat16),
+            pltpu.SemaphoreType.DMA((blocks_dev // 4, 2)),
         ),
-    )(send_index, odd_y, weights, labels)
+    )(send_index, odd_y, seed_doc, seed_topic, unmoved(weights), unmoved(labels))
     ya, yb = swapped(ya, "gy", 0), swapped(yb, "gy", 1)
-
-    def near(extended):
-        return call(
-            functools.partial(local_body, unroll=4),
-            partial_shape,
-            IN_VMEM,
-            (IN_SMEM, IN_VMEM, IN_VMEM, IN_VMEM, IN_VMEM, IN_VMEM),
-            (pltpu.VMEM((seeds, topics), jnp.bfloat16),),
-        )(columns, seed_doc, seed_topic, pinned(held), pinned(extended), pinned(scales))
-
-    partial = near(extended)
-    xa, xb, extended = call(
+    held, scales, counts = pinned(held), pinned(scales), pinned(counts)
+
+    partial = call(
+        functools.partial(near_body, unroll=16),
+        partial_shape,
+        IN_VMEM,
+        (IN_SMEM,) + (IN_VMEM,) * 4,
+    )(columns, held, pinned(extended), scales, counts)
+    xa, xb, ya, yb, extended = call(
         second_send_body,
-        (sent, sent, extended_shape),
-        (IN_VMEM,) * 3,
+        (sent, sent, sent, sent, extended_shape),
+        (IN_VMEM,) * 5,
         (IN_SMEM,) * 4 + (IN_VMEM,) * 4 + (ANYWHERE,) * 4,
         (pltpu.SemaphoreType.DMA((4,)),),
-        aliases={5: 2},
-    )(columns, send_index, odd_x, odd_y, pinned(held), pinned(extended), pinned(scales), pinned(partial), xa, xb, ya, yb)
+        aliases={5: 4},
+    )(columns, send_index, odd_x, odd_y, held, pinned(extended), scales, pinned(partial), xa, xb, ya, yb)
     xa, xb = swapped(xa, "gx", 0), swapped(xb, "gx", 1)
-
-    following, ya, yb = call(
-        functools.partial(rest_body, unroll=4),
-        (extended_shape, sent, sent),
-        (IN_VMEM,) * 3,
-        (IN_SMEM,) * 3 + (IN_VMEM,) * 4,
-    )(columns, send_index, odd_y, pinned(held), pinned(extended), pinned(scales), pinned(partial))
     ya, yb = swapped(ya, "gy", 0), swapped(yb, "gy", 1)
 
-    partial = near(following)
+    following, partial = call(
+        functools.partial(rest_body, unroll=16),
+        (extended_shape, partial_shape),
+        (IN_VMEM,) * 2,
+        (IN_SMEM,) + (IN_VMEM,) * 5,
+    )(columns, held, pinned(extended), scales, counts, pinned(partial))
+
     out, _ = call(
-        functools.partial(last_body, chunk=chunk),
+        functools.partial(last_body, chunk=4),
         (jax.ShapeDtypeStruct((blocks_dev, block_size, topics), jnp.float32), extended_shape),
         (ANYWHERE, IN_VMEM),
         (IN_SMEM,) * 3 + (IN_VMEM,) * 4 + (ANYWHERE,) * 4,
         (
             pltpu.VMEM((blocks_dev, block_size, topics), jnp.float32),
             pltpu.SemaphoreType.DMA((4,)),
-            pltpu.SemaphoreType.DMA((blocks_dev // chunk,)),
+            pltpu.SemaphoreType.DMA((blocks_dev // 4,)),
         ),
         aliases={4: 1},
-    )(columns, odd_x, odd_y, pinned(held), pinned(following), pinned(scales), pinned(partial), xa, xb, ya, yb)
+    )(columns, odd_x, odd_y, held, pinned(following), scales, pinned(partial), xa, xb, ya, yb)
     return out.reshape(documents, topics)
 
 

time: 50.2 us -> 41.6 us (0.83)
  the two profiles are of different devices: /device:TPU:13 before, /device:TPU:4 now
where the time goes in v2:
time: 41.6 us; the launch traced here: 40.9 us
  Pallas kernels  25 us (60%)
  waiting for transfers between devices  8.52 us (20%)
  starting transfers between devices  6.58 us (16%)
  local copies, waits for them, and re-layouts  0.7 us (2%)
    ppermute x8, waiting for transfers between devices, swapped(): return lax.ppermute(value, ('gx', 'gy'), swap_pairs(axis, first))  8.52 us
    pallas_call x1, Pallas kernels, local(): call(functools.partial(degree_body, chunk=4), (VMEM(weights.shape, jnp.bf...  6.86 us
    ppermute x8, starting transfers between devices, swapped(): return lax.ppermute(value, ('gx', 'gy'), swap_pairs(axis, first))  6.58 us
    pallas_call x1, Pallas kernels, local(): call(functools.partial(rest_body, unroll=16), (extended_shape, partial_sh...  5.78 us
    pallas_call x1, Pallas kernels, local(): call(functools.partial(last_body, chunk=4), (jax.ShapeDtypeStruct((blocks...  4.21 us
    pallas_call x1, Pallas kernels, local(): call(functools.partial(near_body, unroll=16), partial_shape, IN_VMEM, (IN...  3.28 us
    pallas_call x1, Pallas kernels, local(): call(first_send_body, (sent, sent), (IN_VMEM, IN_VMEM), (IN_SMEM, IN_SMEM...  3.17 us
    pallas_call x1, Pallas kernels, local(): call(second_send_body, (sent, sent, sent, sent, extended_shape), (IN_VMEM...  1.74 us
  transfers between devices with their start and end apart: 8, of which 4 were waited for; matrix products, arithmetic and copies ran while one was open for 0% of the time, Pallas kernels for 39%

profile of v2, /device:TPU:4, one launch (start us, length us, event | category | flops | bytes accessed | tf_op | source)
XLA Modules:
  0.0 40.9 jit_solution(3405019397477134270)
XLA Ops:
  0.0 0.0 copy-start.1
  0.0 0.7 %copy-done.1 = s32[1,4,4]{2,1,0:T(4,128)S(1)} copy-done((s32[1,4,4]{2,1,0:T(4,128)S(1)}, s32[1,4,4]{2,1,0:T(4,128)}, u32[]{:S(2)}) %copy-start.1) | copy-done | bytes 88
  0.7 0.0 copy-start.2
  0.7 0.0 copy-start.3
  0.7 0.0 copy-start.4
  0.7 3.2 %shard_map.66 = (bf16[4,128,256]{2,1,0:T(8,128)(2,1)S(1)}, bf16[4,128,256]{2,1,0:T(8,128)(2,1)S(1)}) custom-call(s32[1,4,4]{2,1,0:T(4,128)S(1)} %copy-done.1, s32[1]{0:T(128)} %bitcast.1.odd_x, bf16[32,12,128,128]{3,2,1,0:T(8,128)(2,1)} %weights.3, f32[32,128,256]{2,1,0:T(8,128)} %bitcast.13), custom_call_target="tpu_custom_call" | custom-call | flops 1 | bytes 1 | tf_op jit(solution)/shard_map/pallas_call | solution.py:273
  3.9 1.5 %collective-permute-start = (bf16[4,128,256]{2,1,0:T(8,128)(2,1)S(1)}, bf16[4,128,256]{2,1,0:T(8,128)(2,1)S(1)}, u32[]{:S(2)}, u32[]{:S(2)}) collective-permute-start(bf16[4,128,256]{2,1,0:T(8,128)(2,1)S(1)} %get-tuple-element.25), channel_id=1, source_target_pairs={{0,8},{1,9},{2,10},{3,11},{4,12},{5,13},{6,14},{7,15},{8,0},{9,1},... | collective-permute-start | bytes 786440 | tf_op jit(solution)/shard_map/ppermute | solution.py:251
  5.3 0.0 collective-permute-start.1
  5.3 0.0 copy-done.2
  5.3 0.0 copy-done.3
  5.3 0.0 copy-done.4
  5.3 0.0 copy-start
  5.4 6.9 %shard_map.64 = (bf16[32,12,128,128]{3,2,1,0:T(8,128)(2,1)S(1)}, bf16[48,128,256]{2,1,0:T(8,128)(2,1)S(1)}, f32[32,128,128]{2,1,0:T(8,128)S(1)}, bf16[32,128,256...) custom-call(s32[1,4,4]{2,1,0:T(4,128)S(1)} %copy-done.2, s32[1]{0:T(128)} %bitcast.2.odd_y, ...), custom_call_target="tpu_custom_call" | custom-call | flops 1 | bytes 1 | tf_op jit(solution)/shard_map/pallas_call | solution.py:286
  12.2 0.1 collective-permute-start.2
  12.3 0.9 %collective-permute-start.3 = (bf16[4,128,256]{2,1,0:T(8,128)(2,1)S(1)}, bf16[4,128,256]{2,1,0:T(8,128)(2,1)S(1)}, u32[]{:S(2)}, u32[]{:S(2)}) collective-permute-start(bf16[4,128,256]{2,1,0:T(8,128)(2,1)S(1)} %get-tuple-element.28), channel_id=1, source_target_pairs={{0,16},{1,2},{2,1},{3,4},{4,3},{5,6},{6,5},{7,23},{8,24},{9,10},{1... | collective-permute-start | bytes 786440 | tf_op jit(solution)/shard_map/ppermute | solution.py:251
  13.2 0.0 copy-done
  13.2 3.3 %shard_map.65.partial = f32[32,128,256]{2,1,0:T(8,128)S(1)} custom-call(s32[12,32]{1,0:T(8,128)S(1)} %bitcast.7, bf16[32,12,128,128]{3,2,1,0:T(8,128)(2,1)S(1)} %get-tuple-element.21.weights, bf16[48,128,256]{2,1,0:T(8,128)(2,1)S(1)} %get-tuple-element.22.extended.extended_in, f32[32,128,128]{2,1,0:T(8,128)S(1)} %get-tuple-element.23.scales, ...), custom_call_target="tpu_custom_call" | custom-call | flops 1 | bytes 1 | tf_op jit(solution)/shard_map/pallas_call | solution.py:300
  16.5 0.0 collective-permute-done.r0
  16.5 0.7 %collective-permute-done.1.r1 = bf16[4,128,256]{2,1,0:T(8,128)(2,1)S(1)} collective-permute-done((bf16[4,128,256]{2,1,0:T(8,128)(2,1)S(1)}, bf16[4,128,256]{2,1,0:T(8,128)(2,1)S(1)}, u32[]{:S(2)}, u32[]{:S(2)}) %collective-permute-start.1) | collective-permute-done | bytes 262176 | tf_op jit(solution)/shard_map/ppermute | solution.py:251
  17.2 0.0 collective-permute-done.2.r2
  17.2 2.7 %collective-permute-done.3.r3 = bf16[4,128,256]{2,1,0:T(8,128)(2,1)S(1)} collective-permute-done((bf16[4,128,256]{2,1,0:T(8,128)(2,1)S(1)}, bf16[4,128,256]{2,1,0:T(8,128)(2,1)S(1)}, u32[]{:S(2)}, u32[]{:S(2)}) %collective-permute-start.3) | collective-permute-done | bytes 262176 | tf_op jit(solution)/shard_map/ppermute | solution.py:251
  19.9 1.7 %shard_map.67 = (bf16[4,128,256]{2,1,0:T(8,128)(2,1)S(1)}, bf16[4,128,256]{2,1,0:T(8,128)(2,1)S(1)}, bf16[4,128,256]{2,1,0:T(8,128)(2,1)S(1)}, bf16[4,128,256]{2,1,0:T(8,128)(2,1)S(1)}, bf16[48,128,256]{2,1,0:T(8,128)(2,1)S(1)}) custom-call(s32[12,32]{1,0:T(8,128)S(1)} %bitcast.8, s32[1,4,4]{2,1,0:T(4,128)S(1)} %copy-done.2, ...), custom_call_target="tpu_custom_call", output_to_operand_aliasing={{4}: (5, {})} | custom-call | flops 1 | bytes 1 | tf_op jit(solution)/shard_map/pallas_call | solution.py:306
  21.7 1.2 %collective-permute-start.4 = (bf16[4,128,256]{2,1,0:T(8,128)(2,1)S(1)}, bf16[4,128,256]{2,1,0:T(8,128)(2,1)S(1)}, u32[]{:S(2)}, u32[]{:S(2)}) collective-permute-start(bf16[4,128,256]{2,1,0:T(8,128)(2,1)S(1)} %get-tuple-element.32), channel_id=1, source_target_pairs={{0,8},{1,9},{2,10},{3,11},{4,12},{5,13},{6,14},{7,15},{8,0},{9,1},... | collective-permute-start | bytes 786440 | tf_op jit(solution)/shard_map/ppermute | solution.py:251
  22.8 2.0 %collective-permute-start.5 = (bf16[4,128,256]{2,1,0:T(8,128)(2,1)S(1)}, bf16[4,128,256]{2,1,0:T(8,128)(2,1)S(1)}, u32[]{:S(2)}, u32[]{:S(2)}) collective-permute-start(bf16[4,128,256]{2,1,0:T(8,128)(2,1)S(1)} %get-tuple-element.33), channel_id=1, source_target_pairs={{0,1},{1,0},{2,3},{3,2},{4,5},{5,4},{6,7},{7,6},{8,16},{9,17},{10,... | collective-permute-start | bytes 786440 | tf_op jit(solution)/shard_map/ppermute | solution.py:251
  24.8 0.0 collective-permute-start.6
  24.8 1.0 %collective-permute-start.7 = (bf16[4,128,256]{2,1,0:T(8,128)(2,1)S(1)}, bf16[4,128,256]{2,1,0:T(8,128)(2,1)S(1)}, u32[]{:S(2)}, u32[]{:S(2)}) collective-permute-start(bf16[4,128,256]{2,1,0:T(8,128)(2,1)S(1)} %get-tuple-element.35), channel_id=1, source_target_pairs={{0,16},{1,2},{2,1},{3,4},{4,3},{5,6},{6,5},{7,23},{8,24},{9,10},{1... | collective-permute-start | bytes 786440 | tf_op jit(solution)/shard_map/ppermute | solution.py:251
  25.8 5.8 %shard_map.68 = (bf16[48,128,256]{2,1,0:T(8,128)(2,1)S(1)}, f32[32,128,256]{2,1,0:T(8,128)S(1)}) custom-call(s32[12,32]{1,0:T(8,128)S(1)} %bitcast.9, bf16[32,12,128,128]{3,2,1,0:T(8,128)(2,1)S(1)} %get-tuple-element.21.weights, bf16[48,128,256]{2,1,0:T(8,128)(2,1)S(1)} %get-tuple-element.29.extended, f32[32,128,128]{2,1,0:T(8,128)S(1)} %get-tuple-element.23.scales, ...), custom_call_target="tpu_custom_call" | custom-call | flops 1 | bytes 1 | tf_op jit(solution)/shard_map/pallas_call | solution.py:317
  31.6 0.0 collective-permute-done.4.r0
  31.6 4.2 %collective-permute-done.5.r1 = bf16[4,128,256]{2,1,0:T(8,128)(2,1)S(1)} collective-permute-done((bf16[4,128,256]{2,1,0:T(8,128)(2,1)S(1)}, bf16[4,128,256]{2,1,0:T(8,128)(2,1)S(1)}, u32[]{:S(2)}, u32[]{:S(2)}) %collective-permute-start.5) | collective-permute-done | bytes 262176 | tf_op jit(solution)/shard_map/ppermute | solution.py:251
  35.8 0.0 collective-permute-done.6.r2
  35.8 0.9 %collective-permute-done.7.r3 = bf16[4,128,256]{2,1,0:T(8,128)(2,1)S(1)} collective-permute-done((bf16[4,128,256]{2,1,0:T(8,128)(2,1)S(1)}, bf16[4,128,256]{2,1,0:T(8,128)(2,1)S(1)}, u32[]{:S(2)}, u32[]{:S(2)}) %collective-permute-start.7) | collective-permute-done | bytes 262176 | tf_op jit(solution)/shard_map/ppermute | solution.py:251
  36.7 4.2 %shard_map.69 = (f32[32,128,256]{2,1,0:T(8,128)}, bf16[48,128,256]{2,1,0:T(8,128)(2,1)S(1)}) custom-call(s32[12,32]{1,0:T(8,128)S(1)} %bitcast.10, s32[1]{0:T(128)} %bitcast.1.odd_x, s32[1]{0:T(128)} %bitcast.2.odd_y, bf16[32,12,128,128]{3,2,1,0:T(8,128)(2,1)S(1)} %get-tuple-element.21.weights, ...), custom_call_target="tpu_custom_call", output_to_operand_aliasing={{1}: (4, {})} | custom-call | flops 1 | bytes 1 | tf_op jit(solution)/shard_map/pallas_call | solution.py:324
Async XLA Ops:
  0.0 0.7 %copy-start.1 = (s32[1,4,4]{2,1,0:T(4,128)S(1)}, s32[1,4,4]{2,1,0:T(4,128)}, u32[]{:S(2)}) copy-start(s32[1,4,4]{2,1,0:T(4,128)} %send_index.5) | copy-start | bytes 196
  0.7 4.7 %copy-start.2 = (s32[1,4,4]{2,1,0:T(4,128)S(1)}, s32[1,4,4]{2,1,0:T(4,128)}, u32[]{:S(2)}) copy-start(s32[1,4,4]{2,1,0:T(4,128)} %send_index.5) | copy-start | bytes 196
  0.7 4.7 %copy-start.3 = (s32[256]{0:T(256)S(1)}, s32[256]{0:T(256)}, u32[]{:S(2)}) copy-start(s32[256]{0:T(256)} %param.10) | copy-start | bytes 3076
  0.7 4.7 %copy-start.4 = (s32[256]{0:T(256)S(1)}, s32[256]{0:T(256)}, u32[]{:S(2)}) copy-start(s32[256]{0:T(256)} %param.11) | copy-start | bytes 3076
  3.9 12.6 %collective-permute-start = (bf16[4,128,256]{2,1,0:T(8,128)(2,1)S(1)}, bf16[4,128,256]{2,1,0:T(8,128)(2,1)S(1)}, u32[]{:S(2)}, u32[]{:S(2)}) collective-permute-start(bf16[4,128,256]{2,1,0:T(8,128)(2,1)S(1)} %get-tuple-element.25), channel_id=1, source_target_pairs={{0,8},{1,9},{2,10},{3,11},{4,12},{5,13},{6,14},{7,15},{8,0},{9,1},... | collective-permute-start | bytes 786440 | tf_op jit(solution)/shard_map/ppermute | solution.py:251
  5.3 11.9 %collective-permute-start.1 = (bf16[4,128,256]{2,1,0:T(8,128)(2,1)S(1)}, bf16[4,128,256]{2,1,0:T(8,128)(2,1)S(1)}, u32[]{:S(2)}, u32[]{:S(2)}) collective-permute-start(bf16[4,128,256]{2,1,0:T(8,128)(2,1)S(1)} %get-tuple-element.26), channel_id=1, source_target_pairs={{0,1},{1,0},{2,3},{3,2},{4,5},{5,4},{6,7},{7,6},{8,16},{9,17},{10,... | collective-permute-start | bytes 786440 | tf_op jit(solution)/shard_map/ppermute | solution.py:251
  5.3 7.9 %copy-start = (s32[32,12]{0,1:T(8,128)S(1)}, s32[32,12]{0,1:T(8,128)}, u32[]{:S(2)}) copy-start(s32[32,12]{0,1:T(8,128)} %param.8) | copy-start | bytes 4612
  12.2 5.0 %collective-permute-start.2 = (bf16[4,128,256]{2,1,0:T(8,128)(2,1)S(1)}, bf16[4,128,256]{2,1,0:T(8,128)(2,1)S(1)}, u32[]{:S(2)}, u32[]{:S(2)}) collective-permute-start(bf16[4,128,256]{2,1,0:T(8,128)(2,1)S(1)} %get-tuple-element.27), channel_id=1, source_target_pairs={{0,1},{1,0},{2,3},{3,2},{4,5},{5,4},{6,7},{7,6},{8,9},{9,8},{10,11... | collective-permute-start | bytes 786440 | tf_op jit(solution)/shard_map/ppermute | solution.py:251
  12.3 7.6 %collective-permute-start.3 = (bf16[4,128,256]{2,1,0:T(8,128)(2,1)S(1)}, bf16[4,128,256]{2,1,0:T(8,128)(2,1)S(1)}, u32[]{:S(2)}, u32[]{:S(2)}) collective-permute-start(bf16[4,128,256]{2,1,0:T(8,128)(2,1)S(1)} %get-tuple-element.28), channel_id=1, source_target_pairs={{0,16},{1,2},{2,1},{3,4},{4,3},{5,6},{6,5},{7,23},{8,24},{9,10},{1... | collective-permute-start | bytes 786440 | tf_op jit(solution)/shard_map/ppermute | solution.py:251
  21.7 9.9 %collective-permute-start.4 = (bf16[4,128,256]{2,1,0:T(8,128)(2,1)S(1)}, bf16[4,128,256]{2,1,0:T(8,128)(2,1)S(1)}, u32[]{:S(2)}, u32[]{:S(2)}) collective-permute-start(bf16[4,128,256]{2,1,0:T(8,128)(2,1)S(1)} %get-tuple-element.32), channel_id=1, source_target_pairs={{0,8},{1,9},{2,10},{3,11},{4,12},{5,13},{6,14},{7,15},{8,0},{9,1},... | collective-permute-start | bytes 786440 | tf_op jit(solution)/shard_map/ppermute | solution.py:251
  22.8 13.0 %collective-permute-start.5 = (bf16[4,128,256]{2,1,0:T(8,128)(2,1)S(1)}, bf16[4,128,256]{2,1,0:T(8,128)(2,1)S(1)}, u32[]{:S(2)}, u32[]{:S(2)}) collective-permute-start(bf16[4,128,256]{2,1,0:T(8,128)(2,1)S(1)} %get-tuple-element.33), channel_id=1, source_target_pairs={{0,1},{1,0},{2,3},{3,2},{4,5},{5,4},{6,7},{7,6},{8,16},{9,17},{10,... | collective-permute-start | bytes 786440 | tf_op jit(solution)/shard_map/ppermute | solution.py:251
  24.8 11.0 %collective-permute-start.6 = (bf16[4,128,256]{2,1,0:T(8,128)(2,1)S(1)}, bf16[4,128,256]{2,1,0:T(8,128)(2,1)S(1)}, u32[]{:S(2)}, u32[]{:S(2)}) collective-permute-start(bf16[4,128,256]{2,1,0:T(8,128)(2,1)S(1)} %get-tuple-element.34), channel_id=1, source_target_pairs={{0,1},{1,0},{2,3},{3,2},{4,5},{5,4},{6,7},{7,6},{8,9},{9,8},{10,11... | collective-permute-start | bytes 786440 | tf_op jit(solution)/shard_map/ppermute | solution.py:251
  24.8 11.9 %collective-permute-start.7 = (bf16[4,128,256]{2,1,0:T(8,128)(2,1)S(1)}, bf16[4,128,256]{2,1,0:T(8,128)(2,1)S(1)}, u32[]{:S(2)}, u32[]{:S(2)}) collective-permute-start(bf16[4,128,256]{2,1,0:T(8,128)(2,1)S(1)} %get-tuple-element.35), channel_id=1, source_target_pairs={{0,16},{1,2},{2,1},{3,4},{4,3},{5,6},{6,5},{7,23},{8,24},{9,10},{1... | collective-permute-start | bytes 786440 | tf_op jit(solution)/shard_map/ppermute | solution.py:251

commit v3 on v2

v3 whole, which is shorter than its diff:
```python
import functools

import jax
import jax.numpy as jnp
from jax import lax
from jax.experimental import pallas as pl
from jax.experimental.pallas import tpu as pltpu
from jax.sharding import PartitionSpec as P

ITERS = 2

ALPHA = 0.99
GAIN = 1.0 / (1.0 - 0.99)
SEED_WEIGHT = (1.0 - ALPHA) * GAIN

LOCAL = 8
VMEM = pltpu.VMEM
IN_VMEM = pl.BlockSpec(memory_space=pltpu.VMEM)
IN_SMEM = pl.BlockSpec(memory_space=pltpu.SMEM)
ANYWHERE = pl.BlockSpec(memory_space=pl.ANY)


def call(body, out_shape, out_specs, in_specs, scratch=(), aliases=None, limit=8):
    return pl.pallas_call(
        body,
        out_shape=out_shape,
        in_specs=in_specs,
        out_specs=out_specs,
        scratch_shapes=scratch,
        input_output_aliases=aliases or {},
        compiler_params=pltpu.CompilerParams(vmem_limit_bytes=limit * 2**20),
        cost_estimate=pl.CostEstimate(flops=1, bytes_accessed=1, transcendentals=0),
    )


def pinned(value):
    return pltpu.with_memory_space_constraint(value, pltpu.VMEM)


def unmoved(value):
    return pltpu.with_memory_space_constraint(value, pltpu.HBM)


def tabled(value):
    return pltpu.with_memory_space_constraint(value, pltpu.SMEM)


def row_scale(weights, row):
    slots = weights.shape[1]
    total = weights[row, 0].astype(jnp.float32)
    for slot in range(1, slots):
        total = total + weights[row, slot].astype(jnp.float32)
    return lax.rsqrt(jnp.sum(total, axis=1, keepdims=True))


def spread_over(scale, width):
    return jnp.concatenate([scale] * (width // scale.shape[1]), axis=1)


def toward_x():
    turn = lax.axis_index("gx") % 2
    return (3 - turn, 2 + turn)


def toward_y():
    turn = lax.axis_index("gy") % 2
    return (1 - turn, turn)


def sent_row(send_index, order, sends, i):
    return send_index[0, order[i // sends], i % sends]


def weighted(weights, extended, columns, row, first, last):
    left = jnp.concatenate([weights[row, slot] for slot in range(first, last)], axis=1)
    right = jnp.concatenate([extended[columns[slot, row]] for slot in range(first, last)], axis=0)
    return jnp.dot(left, right, preferred_element_type=jnp.float32)


def row_copies(weights, labels, held, block, sem, row, slot):
    return (
        pltpu.make_async_copy(weights.at[row], held.at[row], sem.at[slot, 0]),
        pltpu.make_async_copy(labels.at[row], block.at[slot], sem.at[slot, 1]),
    )


def scale_row(held, block, extended, scales, row, slot):
    scale = row_scale(held, row)
    scales[row] = jnp.broadcast_to(scale, scales.shape[1:])
    extended[row] = (scale * block[slot]).astype(jnp.bfloat16)


def copy_out(source, send_index, order, outs):
    sends = send_index.shape[2]
    i = 0
    for out in outs:
        for j in range(out.shape[0]):
            out[j] = source[sent_row(send_index, order, sends, i)]
            i += 1


def first_send_body(
    column_index, send_index, weights, labels, x_a, x_b, held, extended, scales, columns, lists,
    block, seen, fresh, sem, table_sem,
):
    blocks_dev = held.shape[0]
    get_lists = pltpu.make_async_copy(send_index, lists, table_sem.at[0])
    get_columns = pltpu.make_async_copy(column_index, columns, table_sem.at[1])
    get_lists.start()
    get_columns.start()

    def unseen(row, carry):
        seen[row] = 0
        return carry

    lax.fori_loop(0, blocks_dev, unseen, 0, unroll=8)
    get_lists.wait()
    sends = lists.shape[2]
    order = toward_x()
    rows = [sent_row(lists, order, sends, i) for i in range(len(order) * sends)]
    for i, row in enumerate(rows):
        fresh[i] = 1 - seen[row]
        seen[row] = 1

        @pl.when(fresh[i] == 1)
        def _():
            for copy in row_copies(weights, labels, held, block, sem, row, i):
                copy.start()

    for i, row in enumerate(rows):

        @pl.when(fresh[i] == 1)
        def _():
            for copy in row_copies(weights, labels, held, block, sem, row, i):
                copy.wait()
            scale_row(held, block, extended, scales, row, i)

    copy_out(extended, lists, order, (x_a, x_b))
    get_columns.wait()


def degree_body(
    lists, seed_doc, seed_topic, weights, labels, held_in, extended_in, scales_in,
    held, extended, scales, counts, y_a, y_b, block, topic_hot, seen, left, sem, *, chunk,
):
    blocks_dev, block_size, topics = block.shape
    seeds = seed_doc.shape[1]

    def unseen(row, carry):
        seen[row] = 0
        return carry

    lax.fori_loop(0, blocks_dev, unseen, 0, unroll=8)
    for direction in toward_x():
        for i in range(lists.shape[2]):
            seen[lists[0, direction, i]] = 1

    def fetch(row, number):
        @pl.when(seen[row] == 0)
        def _():
            left[number] = row
            for copy in row_copies(weights, labels, held, block, sem, row, number):
                copy.start()

        return number + 1 - seen[row]

    number = lax.fori_loop(0, blocks_dev, fetch, jnp.int32(0))
    topic = lax.broadcasted_iota(jnp.int32, (topics, seeds), 0)
    hot = jnp.where(topic == seed_topic[...], 1.0, 0.0).astype(jnp.float32)
    topic_hot[...] = hot.T.astype(jnp.bfloat16)

    def count(row, carry):
        document = lax.broadcasted_iota(jnp.int32, (block_size, seeds), 0) + row * block_size
        doc_hot = jnp.where(document == seed_doc[...], 1.0, 0.0).astype(jnp.bfloat16)
        hits = jnp.dot(doc_hot, topic_hot[...], preferred_element_type=jnp.float32)
        counts[row] = hits.astype(jnp.bfloat16)
        return carry

    lax.fori_loop(0, blocks_dev, count, 0, unroll=8)

    def step(c, carry):
        slots = [jnp.minimum(c * chunk + i, number - 1) for i in range(chunk)]
        for i, slot in enumerate(slots):

            @pl.when(c * chunk + i < number)
            def _():
                for copy in row_copies(weights, labels, held, block, sem, left[slot], slot):
                    copy.wait()

        for slot in slots:
            scale_row(held, block, extended, scales, left[slot], slot)
        return carry

    lax.fori_loop(0, lax.div(number + chunk - 1, jnp.int32(chunk)), step, 0)
    copy_out(extended, lists, toward_y(), (y_a, y_b))


def near(weights, extended, columns, scales, counts, row):
    topics = extended.shape[2]
    product = weighted(weights, extended, columns, row, 0, LOCAL)
    return spread_over(ALPHA * scales[row], topics) * product + SEED_WEIGHT * counts[row].astype(jnp.float32)


def near_body(columns, weights, extended, scales, counts, partial, *, unroll):
    def step(row, carry):
        partial[row] = near(weights, extended, columns, scales, counts, row)
        return carry

    lax.fori_loop(0, partial.shape[0], step, 0, unroll=unroll)


def arrivals(pieces, extended):
    sends = pieces[0].shape[0]
    low = extended.shape[0] - 4 * sends
    order = toward_x() + toward_y()
    i = 0
    for piece in pieces:
        extended[pl.ds(low + order[i // sends] * sends + i % sends, piece.shape[0])] = piece[...]
        i += piece.shape[0]


def finished(weights, extended, columns, scales, partial, row):
    topics = partial.shape[2]
    slots = weights.shape[1]
    product = weighted(weights, extended, columns, row, LOCAL, slots)
    return partial[row] + spread_over(ALPHA * scales[row], topics) * product


def second_send_body(
    columns, lists, weights, extended_in, scales, partial, r0, r1, r2, r3, x_a, x_b, x_c, y_a, y_b, extended
):
    sends = lists.shape[2]
    topics = x_a.shape[2]
    arrivals((r0, r1, r2, r3), extended)
    order = toward_x() + toward_y()
    i = 0
    for out in (x_a, x_b, x_c, y_a, y_b):
        for j in range(out.shape[0]):
            row = sent_row(lists, order, sends, i)
            value = finished(weights, extended, columns, scales, partial, row)
            out[j] = (spread_over(scales[row], topics) * value).astype(jnp.bfloat16)
            i += 1


def rest_body(columns, weights, extended, scales, partial, following, *, unroll):
    blocks_dev, _, topics = partial.shape

    def finish(row, carry):
        value = finished(weights, extended, columns, scales, partial, row)
        following[row] = (spread_over(scales[row], topics) * value).astype(jnp.bfloat16)
        return carry

    lax.fori_loop(0, blocks_dev, finish, 0, unroll=unroll)


def last_body(
    columns, weights, extended_in, scales, partial, r0, r1, r2, r3, r4, out, extended, block, sem, *, unroll
):
    blocks_dev = partial.shape[0]
    arrivals((r0, r1, r2, r3, r4), extended)

    def leave(row):
        return pltpu.make_async_copy(block.at[row], out.at[row], sem.at[row])

    def step(row, carry):
        block[row] = finished(weights, extended, columns, scales, partial, row)
        leave(row).start()
        return carry

    lax.fori_loop(0, blocks_dev, step, 0, unroll=unroll)

    def settle(row, carry):
        leave(row).wait()
        return carry

    lax.fori_loop(0, blocks_dev, settle, 0)


def swap_pairs(axis, first):
    outer, inner = lax.axis_size("gx"), lax.axis_size("gy")
    count, other = (outer, inner) if axis == "gx" else (inner, outer)
    lines = []
    for low in range(first, count - 1, 2):
        lines += [((low, line), (low + 1, line)) for line in range(other)]
    alone = [place for place in range(count) if all(place not in (p[0], q[0]) for p, q in lines)]
    half = 1 if axis == "gx" else other // 2
    for place in alone:
        for line in range(other):
            if line // half % 2 == 0 and line + half < other:
                lines.append(((place, line), (place, line + half)))
    number = (lambda place, line: place * inner + line) if axis == "gx" else (lambda place, line: line * inner + place)
    pairs = []
    for p, q in lines:
        low, high = number(*p), number(*q)
        pairs += [(low, high), (high, low)]
    return sorted(pairs)


def swapped(value, axis, first):
    return lax.ppermute(value, ("gx", "gy"), swap_pairs(axis, first))


def relayed(value):
    if lax.axis_size("gx") != 4:
        return swapped(value, "gx", 1)
    value = lax.ppermute(value, "gx", [(0, 2), (1, 3), (2, 0), (3, 1)])
    return lax.ppermute(value, "gx", [(0, 1), (1, 3), (3, 2), (2, 0)])


def local(labels, weights, column_index, send_index, seed_doc, seed_topic):
    blocks_dev, slots, block_size, _ = weights.shape
    documents = blocks_dev * block_size
    topics = labels.shape[1]
    sends = send_index.shape[2]
    seeds = seed_doc.shape[0]
    labels = unmoved(labels.reshape(blocks_dev, block_size, topics))
    weights = unmoved(weights)
    send_index = unmoved(send_index)
    seed_doc = seed_doc.reshape(1, seeds)
    seed_topic = seed_topic.reshape(1, seeds)
    half = sends // 2
    whole = VMEM((sends, block_size, topics), jnp.bfloat16)
    first_half = VMEM((half, block_size, topics), jnp.bfloat16)
    second_half = VMEM((sends - half, block_size, topics), jnp.bfloat16)
    held_shape = VMEM(weights.shape, jnp.bfloat16)
    extended_shape = VMEM((blocks_dev + 4 * sends, block_size, topics), jnp.bfloat16)
    scale_shape = VMEM((blocks_dev, block_size, block_size), jnp.float32)
    count_shape = VMEM((blocks_dev, block_size, topics), jnp.bfloat16)
    partial_shape = VMEM((blocks_dev, block_size, topics), jnp.float32)

    x_a, x_b, held, extended, scales, columns, lists = call(
        first_send_body,
        (whole, whole, held_shape, extended_shape, scale_shape)
        + (pltpu.SMEM((slots, blocks_dev), jnp.int32), pltpu.SMEM(send_index.shape, jnp.int32)),
        (IN_VMEM,) * 5 + (IN_SMEM,) * 2,
        (ANYWHERE,) * 4,
        (
            pltpu.VMEM((2 * sends, block_size, topics), jnp.float32),
            pltpu.SMEM((blocks_dev,), jnp.int32),
            pltpu.SMEM((2 * sends,), jnp.int32),
            pltpu.SemaphoreType.DMA((2 * sends, 2)),
            pltpu.SemaphoreType.DMA((2,)),
        ),
    )(unmoved(column_index.T), send_index, weights, labels)
    x_a, x_b = swapped(x_a, "gx", 0), swapped(x_b, "gx", 1)
    columns, lists = tabled(columns), tabled(lists)

    held, extended, scales, counts, y_a, y_b = call(
        functools.partial(degree_body, chunk=4),
        (held_shape, extended_shape, scale_shape, count_shape, whole, whole),
        (IN_VMEM,) * 6,
        (IN_SMEM,) + (IN_VMEM,) * 2 + (ANYWHERE,) * 2 + (IN_VMEM,) * 3,
        (
            pltpu.VMEM((blocks_dev, block_size, topics), jnp.float32),
            pltpu.VMEM((seeds, topics), jnp.bfloat16),
            pltpu.SMEM((blocks_dev,), jnp.int32),
            pltpu.SMEM((blocks_dev,), jnp.int32),
            pltpu.SemaphoreType.DMA((blocks_dev, 2)),
        ),
        aliases={5: 0, 6: 1, 7: 2},
    )(lists, seed_doc, seed_topic, weights, labels, pinned(held), pinned(extended), pinned(scales))
    y_b, y_a = swapped(y_b, "gy", 1), swapped(y_a, "gy", 0)
    held, scales, counts = pinned(held), pinned(scales), pinned(counts)

    def started(extended):
        return call(
            functools.partial(near_body, unroll=16),
            partial_shape,
            IN_VMEM,
            (IN_SMEM,) + (IN_VMEM,) * 4,
        )(columns, held, pinned(extended), scales, counts)

    partial = started(extended)
    x_a, x_b, x_c, y_a, y_b, extended = call(
        second_send_body,
        (whole, first_half, second_half, whole, whole, extended_shape),
        (IN_VMEM,) * 6,
        (IN_SMEM,) * 2 + (IN_VMEM,) * 8,
        aliases={3: 5},
    )(columns, lists, held, pinned(extended), scales, pinned(partial), *map(pinned, (x_a, x_b, y_a, y_b)))
    x_c, x_a, x_b = relayed(x_c), swapped(x_a, "gx", 0), swapped(x_b, "gx", 1)
    y_b, y_a = swapped(y_b, "gy", 1), swapped(y_a, "gy", 0)

    following = call(
        functools.partial(rest_body, unroll=16),
        extended_shape,
        IN_VMEM,
        (IN_SMEM,) + (IN_VMEM,) * 4,
    )(columns, held, pinned(extended), scales, pinned(partial))
    partial = started(following)

    out, _ = call(
        functools.partial(last_body, unroll=16),
        (jax.ShapeDtypeStruct((blocks_dev, block_size, topics), jnp.float32), extended_shape),
        (ANYWHERE, IN_VMEM),
        (IN_SMEM,) + (IN_VMEM,) * 9,
        (
            pltpu.VMEM((blocks_dev, block_size, topics), jnp.float32),
            pltpu.SemaphoreType.DMA((blocks_dev,)),
        ),
        aliases={2: 1},
    )(columns, held, pinned(following), scales, pinned(partial), *map(pinned, (x_a, x_b, x_c, y_a, y_b)))
    return out.reshape(documents, topics)


def solution(mesh):
    in_specs = (
        P(("gx", "gy"), None),
        P(("gx", "gy"), None, None, None),
        P(("gx", "gy"), None),
        P(("gx", "gy"), None, None),
        P(("gx", "gy")),
        P(("gx", "gy")),
    )
    out_specs = P(("gx", "gy"), None)
    return jax.shard_map(local, mesh=mesh, in_specs=in_specs, out_specs=out_specs, check_vma=False)
```

time: 41.6 us -> 37.5 us (0.901)
  the two profiles are of different devices: /device:TPU:4 before, /device:TPU:0 now
where the time goes in v3:
time: 37.5 us; the launch traced here: 37.4 us
  Pallas kernels  19.8 us (53%)
  starting transfers between devices  13.9 us (37%)
  waiting for transfers between devices  3.52 us (9%)
    ppermute x8, starting transfers between devices, swapped(): return lax.ppermute(value, ('gx', 'gy'), swap_pairs(axis, first))  8.2 us
    pallas_call x1, Pallas kernels, local(): call(functools.partial(degree_body, chunk=4), (held_shape, extended_shape...  5.63 us
    pallas_call x2, Pallas kernels, started(): call(functools.partial(near_body, unroll=16), partial_shape, IN_VMEM, (IN...  5.2 us
    ppermute x8, waiting for transfers between devices, swapped(): return lax.ppermute(value, ('gx', 'gy'), swap_pairs(axis, first))  3.51 us
    pallas_call x1, Pallas kernels, local(): call(first_send_body, (whole, whole, held_shape, extended_shape, scale_sh...  3.33 us
    ppermute x1, starting transfers between devices, relayed(): return lax.ppermute(value, 'gx', [(0, 1), (1, 3), (3, 2), (2, 0)])  3.2 us
    pallas_call x1, Pallas kernels, local(): call(functools.partial(last_body, unroll=16), (jax.ShapeDtypeStruct((bloc...  2.88 us
    ppermute x1, starting transfers between devices, relayed(): value = lax.ppermute(value, 'gx', [(0, 2), (1, 3), (2, 0), (3, 1)])  2.54 us
  transfers between devices with their start and end apart: 10, of which 1 were waited for; matrix products, arithmetic and copies ran while one was open for 0% of the time, Pallas kernels for 34%

profile of v3, /device:TPU:0, one launch (start us, length us, event | category | flops | bytes accessed | tf_op | source)
XLA Modules:
  0.0 37.4 jit_solution(17812561662408365723)
XLA Ops:
  0.0 0.0 copy-start
  0.0 0.0 copy-start.1
  0.0 3.3 %shard_map.64 = (bf16[4,128,256]{2,1,0:T(8,128)(2,1)S(1)}, bf16[4,128,256]{2,1,0:T(8,128)(2,1)S(1)}, bf16[32,12,128,128]{3,2,1,0:T(8,128)(2,1)S(1)}, bf16[48,128...) custom-call(s32[12,32]{1,0:T(8,128)} %bitcast.9, ...), custom_call_target="tpu_custom_call" | custom-call | flops 1 | bytes 1 | tf_op jit(solution)/shard_map/pallas_call | solution.py:331
  3.3 3.0 %collective-permute-start = (bf16[4,128,256]{2,1,0:T(8,128)(2,1)S(1)}, bf16[4,128,256]{2,1,0:T(8,128)(2,1)S(1)}, u32[]{:S(2)}, u32[]{:S(2)}) collective-permute-start(bf16[4,128,256]{2,1,0:T(8,128)(2,1)S(1)} %get-tuple-element.34), channel_id=1, source_target_pairs={{0,8},{1,9},{2,10},{3,11},{4,12},{5,13},{6,14},{7,15},{8,0},{9,1},... | collective-permute-start | bytes 786440 | tf_op jit(solution)/shard_map/ppermute | solution.py:300
  6.4 0.0 collective-permute-start.1
  6.4 0.0 copy-done
  6.4 0.0 copy-done.1
  6.4 5.6 %shard_map.65 = (bf16[32,12,128,128]{3,2,1,0:T(8,128)(2,1)S(1)}, bf16[48,128,256]{2,1,0:T(8,128)(2,1)S(1)}, f32[32,128,128]{2,1,0:T(8,128)S(1)}, bf16[32,128,256...) custom-call(s32[1,4,4]{2,1,0:T(4,128)S(4)} %get-tuple-element.26.lis, ...), custom_call_target="tpu_custom_call", output_to_operand_aliasing={{0}: (5, {}), {1}: (6, {}), {2}: (7, {})} | custom-call | flops 1 | bytes 1 | tf_op jit(solution)/shard_map/pallas_call | solution.py:348
  12.0 0.8 %collective-permute-start.2 = (bf16[4,128,256]{2,1,0:T(8,128)(2,1)S(1)}, bf16[4,128,256]{2,1,0:T(8,128)(2,1)S(1)}, u32[]{:S(2)}, u32[]{:S(2)}) collective-permute-start(bf16[4,128,256]{2,1,0:T(8,128)(2,1)S(1)} %get-tuple-element.36), channel_id=1, source_target_pairs={{0,1},{1,0},{2,3},{3,2},{4,5},{5,4},{6,7},{7,6},{8,9},{9,8},{10,11... | collective-permute-start | bytes 786440 | tf_op jit(solution)/shard_map/ppermute | solution.py:300
  12.8 1.2 %collective-permute-start.3 = (bf16[4,128,256]{2,1,0:T(8,128)(2,1)S(1)}, bf16[4,128,256]{2,1,0:T(8,128)(2,1)S(1)}, u32[]{:S(2)}, u32[]{:S(2)}) collective-permute-start(bf16[4,128,256]{2,1,0:T(8,128)(2,1)S(1)} %get-tuple-element.37), channel_id=1, source_target_pairs={{0,16},{1,2},{2,1},{3,4},{4,3},{5,6},{6,5},{7,23},{8,24},{9,10},{1... | collective-permute-start | bytes 786440 | tf_op jit(solution)/shard_map/ppermute | solution.py:300
  13.9 2.6 %shard_map.66.partial = f32[32,128,256]{2,1,0:T(8,128)S(1)} custom-call(s32[12,32]{1,0:T(8,128)S(4)} %get-tuple-element.25.columns, bf16[32,12,128,128]{3,2,1,0:T(8,128)(2,1)S(1)} %get-tuple-element.30.weights, bf16[48,128,256]{2,1,0:T(8,128)(2,1)S(1)} %get-tuple-element.31.extended.extended_in, f32[32,128,128]{2,1,0:T(8,128)S(1)} %get-tuple-element.32.scales, ...), custom_call_target="tpu_custom_call" | custom-call | flops 1 | bytes 1 | tf_op jit(solution)/shard_map/pallas_call | solution.py:366
  16.5 0.0 collective-permute-done.r0
  16.5 0.0 collective-permute-done.1.r1
  16.6 0.0 collective-permute-done.2.r2
  16.6 3.5 %collective-permute-done.3.r3 = bf16[4,128,256]{2,1,0:T(8,128)(2,1)S(1)} collective-permute-done((bf16[4,128,256]{2,1,0:T(8,128)(2,1)S(1)}, bf16[4,128,256]{2,1,0:T(8,128)(2,1)S(1)}, u32[]{:S(2)}, u32[]{:S(2)}) %collective-permute-start.3) | collective-permute-done | bytes 262176 | tf_op jit(solution)/shard_map/ppermute | solution.py:300
  20.1 1.0 %shard_map.67 = (bf16[4,128,256]{2,1,0:T(8,128)(2,1)S(1)}, bf16[2,128,256]{2,1,0:T(8,128)(2,1)S(1)}, bf16[2,128,256]{2,1,0:T(8,128)(2,1)S(1)}, bf16[4,128,256]{2...) custom-call(s32[12,32]{1,0:T(8,128)S(4)} %get-tuple-element.25.colum, ...), custom_call_target="tpu_custom_call", output_to_operand_aliasing={{5}: (3, {})} | custom-call | flops 1 | bytes 1 | tf_op jit(solution)/shard_map/pallas_call | solution.py:374
  21.0 2.5 %collective-permute-start.6 = (bf16[2,128,256]{2,1,0:T(8,128)(2,1)S(1)}, bf16[2,128,256]{2,1,0:T(8,128)(2,1)S(1)}, u32[]{:S(2)}, u32[]{:S(2)}) collective-permute-start(bf16[2,128,256]{2,1,0:T(8,128)(2,1)S(1)} %get-tuple-element.41), channel_id=1, source_target_pairs={{0,16},{8,24},{16,0},{24,8},{1,17},{9,25},{17,1},{25,9},{2,18},{10... | collective-permute-start | bytes 393224 | tf_op jit(solution)/shard_map/ppermute | solution.py:306
  23.6 1.3 %collective-permute-start.4 = (bf16[4,128,256]{2,1,0:T(8,128)(2,1)S(1)}, bf16[4,128,256]{2,1,0:T(8,128)(2,1)S(1)}, u32[]{:S(2)}, u32[]{:S(2)}) collective-permute-start(bf16[4,128,256]{2,1,0:T(8,128)(2,1)S(1)} %get-tuple-element.39), channel_id=1, source_target_pairs={{0,8},{1,9},{2,10},{3,11},{4,12},{5,13},{6,14},{7,15},{8,0},{9,1},... | collective-permute-start | bytes 786440 | tf_op jit(solution)/shard_map/ppermute | solution.py:300
  24.9 0.0 collective-permute-start.8
  24.9 1.9 %collective-permute-start.9 = (bf16[4,128,256]{2,1,0:T(8,128)(2,1)S(1)}, bf16[4,128,256]{2,1,0:T(8,128)(2,1)S(1)}, u32[]{:S(2)}, u32[]{:S(2)}) collective-permute-start(bf16[4,128,256]{2,1,0:T(8,128)(2,1)S(1)} %get-tuple-element.43), channel_id=1, source_target_pairs={{0,16},{1,2},{2,1},{3,4},{4,3},{5,6},{6,5},{7,23},{8,24},{9,10},{1... | collective-permute-start | bytes 786440 | tf_op jit(solution)/shard_map/ppermute | solution.py:300
  26.8 0.0 collective-permute-start.5
  26.8 0.0 collective-permute-done.6
  26.8 3.2 %collective-permute-start.7 = (bf16[2,128,256]{2,1,0:T(8,128)(2,1)S(1)}, bf16[2,128,256]{2,1,0:T(8,128)(2,1)S(1)}, u32[]{:S(2)}, u32[]{:S(2)}) collective-permute-start(bf16[2,128,256]{2,1,0:T(8,128)(2,1)S(1)} %collective-permute-done.6), channel_id=1, source_target_pairs={{0,8},{8,24},{24,16},{16,0},{1,9},{9,25},{25,17},{17,1},{2,10},{10... | collective-permute-start | bytes 393224 | tf_op jit(solution)/shard_map/ppermute | solution.py:307
  30.0 1.8 %shard_map.68.extended.extended_in = bf16[48,128,256]{2,1,0:T(8,128)(2,1)S(1)} custom-call(s32[12,32]{1,0:T(8,128)S(4)} %get-tuple-element.25.columns, bf16[32,12,128,128]{3,2,1,0:T(8,128)(2,1)S(1)} %get-tuple-element.30.weights, bf16[48,128,256]{2,1,0:T(8,128)(2,1)S(1)} %get-tuple-element.38.extended, f32[32,128,128]{2,1,0:T(8,128)S(1)} %get-tuple-element.32.scales, ...), custom_call_target="tpu_custom_call" | custom-call | flops 1 | bytes 1 | tf_op jit(solution)/shard_map/pallas_call | solution.py:384
  31.8 2.6 %shard_map.69.partial = f32[32,128,256]{2,1,0:T(8,128)S(1)} custom-call(s32[12,32]{1,0:T(8,128)S(4)} %get-tuple-element.25.columns, bf16[32,12,128,128]{3,2,1,0:T(8,128)(2,1)S(1)} %get-tuple-element.30.weights, bf16[48,128,256]{2,1,0:T(8,128)(2,1)S(1)} %shard_map.68.extended.extended_in, f32[32,128,128]{2,1,0:T(8,128)S(1)} %get-tuple-element.32.scales, ...), custom_call_target="tpu_custom_call" | custom-call | flops 1 | bytes 1 | tf_op jit(solution)/shard_map/pallas_call | solution.py:366
  34.4 0.0 collective-permute-done.5.r1
  34.4 0.0 collective-permute-done.7.r2
  34.5 0.0 collective-permute-done.4.r0
  34.5 0.0 collective-permute-done.8.r3
  34.5 0.0 collective-permute-done.9.r4
  34.5 2.9 %shard_map.70 = (f32[32,128,256]{2,1,0:T(8,128)}, bf16[48,128,256]{2,1,0:T(8,128)(2,1)S(1)}) custom-call(s32[12,32]{1,0:T(8,128)S(4)} %get-tuple-element.25.columns, bf16[32,12,128,128]{3,2,1,0:T(8,128)(2,1)S(1)} %get-tuple-element.30.weights, bf16[48,128,256]{2,1,0:T(8,128)(2,1)S(1)} %shard_map.68.extended.extended_in, ...), custom_call_target="tpu_custom_call", output_to_operand_aliasing={{1}: (2, {})} | custom-call | flops 1 | bytes 1 | tf_op jit(solution)/shard_map/pallas_call | solution.py:392
Async XLA Ops:
  0.0 6.4 %copy-start = (s32[256]{0:T(256)S(1)}, s32[256]{0:T(256)}, u32[]{:S(2)}) copy-start(s32[256]{0:T(256)} %param.10) | copy-start | bytes 3076
  0.0 6.4 %copy-start.1 = (s32[256]{0:T(256)S(1)}, s32[256]{0:T(256)}, u32[]{:S(2)}) copy-start(s32[256]{0:T(256)} %param.11) | copy-start | bytes 3076
  3.3 13.2 %collective-permute-start = (bf16[4,128,256]{2,1,0:T(8,128)(2,1)S(1)}, bf16[4,128,256]{2,1,0:T(8,128)(2,1)S(1)}, u32[]{:S(2)}, u32[]{:S(2)}) collective-permute-start(bf16[4,128,256]{2,1,0:T(8,128)(2,1)S(1)} %get-tuple-element.34), channel_id=1, source_target_pairs={{0,8},{1,9},{2,10},{3,11},{4,12},{5,13},{6,14},{7,15},{8,0},{9,1},... | collective-permute-start | bytes 786440 | tf_op jit(solution)/shard_map/ppermute | solution.py:300
  6.4 10.2 %collective-permute-start.1 = (bf16[4,128,256]{2,1,0:T(8,128)(2,1)S(1)}, bf16[4,128,256]{2,1,0:T(8,128)(2,1)S(1)}, u32[]{:S(2)}, u32[]{:S(2)}) collective-permute-start(bf16[4,128,256]{2,1,0:T(8,128)(2,1)S(1)} %get-tuple-element.35), channel_id=1, source_target_pairs={{0,1},{1,0},{2,3},{3,2},{4,5},{5,4},{6,7},{7,6},{8,16},{9,17},{10,... | collective-permute-start | bytes 786440 | tf_op jit(solution)/shard_map/ppermute | solution.py:300
  12.0 4.6 %collective-permute-start.2 = (bf16[4,128,256]{2,1,0:T(8,128)(2,1)S(1)}, bf16[4,128,256]{2,1,0:T(8,128)(2,1)S(1)}, u32[]{:S(2)}, u32[]{:S(2)}) collective-permute-start(bf16[4,128,256]{2,1,0:T(8,128)(2,1)S(1)} %get-tuple-element.36), channel_id=1, source_target_pairs={{0,1},{1,0},{2,3},{3,2},{4,5},{5,4},{6,7},{7,6},{8,9},{9,8},{10,11... | collective-permute-start | bytes 786440 | tf_op jit(solution)/shard_map/ppermute | solution.py:300
  12.8 7.3 %collective-permute-start.3 = (bf16[4,128,256]{2,1,0:T(8,128)(2,1)S(1)}, bf16[4,128,256]{2,1,0:T(8,128)(2,1)S(1)}, u32[]{:S(2)}, u32[]{:S(2)}) collective-permute-start(bf16[4,128,256]{2,1,0:T(8,128)(2,1)S(1)} %get-tuple-element.37), channel_id=1, source_target_pairs={{0,16},{1,2},{2,1},{3,4},{4,3},{5,6},{6,5},{7,23},{8,24},{9,10},{1... | collective-permute-start | bytes 786440 | tf_op jit(solution)/shard_map/ppermute | solution.py:300
  21.0 5.8 %collective-permute-start.6 = (bf16[2,128,256]{2,1,0:T(8,128)(2,1)S(1)}, bf16[2,128,256]{2,1,0:T(8,128)(2,1)S(1)}, u32[]{:S(2)}, u32[]{:S(2)}) collective-permute-start(bf16[2,128,256]{2,1,0:T(8,128)(2,1)S(1)} %get-tuple-element.41), channel_id=1, source_target_pairs={{0,16},{8,24},{16,0},{24,8},{1,17},{9,25},{17,1},{25,9},{2,18},{10... | collective-permute-start | bytes 393224 | tf_op jit(solution)/shard_map/ppermute | solution.py:306
  23.6 10.9 %collective-permute-start.4 = (bf16[4,128,256]{2,1,0:T(8,128)(2,1)S(1)}, bf16[4,128,256]{2,1,0:T(8,128)(2,1)S(1)}, u32[]{:S(2)}, u32[]{:S(2)}) collective-permute-start(bf16[4,128,256]{2,1,0:T(8,128)(2,1)S(1)} %get-tuple-element.39), channel_id=1, source_target_pairs={{0,8},{1,9},{2,10},{3,11},{4,12},{5,13},{6,14},{7,15},{8,0},{9,1},... | collective-permute-start | bytes 786440 | tf_op jit(solution)/shard_map/ppermute | solution.py:300
  24.9 9.6 %collective-permute-start.8 = (bf16[4,128,256]{2,1,0:T(8,128)(2,1)S(1)}, bf16[4,128,256]{2,1,0:T(8,128)(2,1)S(1)}, u32[]{:S(2)}, u32[]{:S(2)}) collective-permute-start(bf16[4,128,256]{2,1,0:T(8,128)(2,1)S(1)} %get-tuple-element.42), channel_id=1, source_target_pairs={{0,1},{1,0},{2,3},{3,2},{4,5},{5,4},{6,7},{7,6},{8,9},{9,8},{10,11... | collective-permute-start | bytes 786440 | tf_op jit(solution)/shard_map/ppermute | solution.py:300
  24.9 9.6 %collective-permute-start.9 = (bf16[4,128,256]{2,1,0:T(8,128)(2,1)S(1)}, bf16[4,128,256]{2,1,0:T(8,128)(2,1)S(1)}, u32[]{:S(2)}, u32[]{:S(2)}) collective-permute-start(bf16[4,128,256]{2,1,0:T(8,128)(2,1)S(1)} %get-tuple-element.43), channel_id=1, source_target_pairs={{0,16},{1,2},{2,1},{3,4},{4,3},{5,6},{6,5},{7,23},{8,24},{9,10},{1... | collective-permute-start | bytes 786440 | tf_op jit(solution)/shard_map/ppermute | solution.py:300
  26.8 7.6 %collective-permute-start.5 = (bf16[2,128,256]{2,1,0:T(8,128)(2,1)S(1)}, bf16[2,128,256]{2,1,0:T(8,128)(2,1)S(1)}, u32[]{:S(2)}, u32[]{:S(2)}) collective-permute-start(bf16[2,128,256]{2,1,0:T(8,128)(2,1)S(1)} %get-tuple-element.40), channel_id=1, source_target_pairs={{0,1},{1,0},{2,3},{3,2},{4,5},{5,4},{6,7},{7,6},{8,16},{9,17},{10,... | collective-permute-start | bytes 393224 | tf_op jit(solution)/shard_map/ppermute | solution.py:300
  26.8 7.6 %collective-permute-start.7 = (bf16[2,128,256]{2,1,0:T(8,128)(2,1)S(1)}, bf16[2,128,256]{2,1,0:T(8,128)(2,1)S(1)}, u32[]{:S(2)}, u32[]{:S(2)}) collective-permute-start(bf16[2,128,256]{2,1,0:T(8,128)(2,1)S(1)} %collective-permute-done.6), channel_id=1, source_target_pairs={{0,8},{8,24},{24,16},{16,0},{1,9},{9,25},{25,17},{17,1},{2,10},{10... | collective-permute-start | bytes 393224 | tf_op jit(solution)/shard_map/ppermute | solution.py:307

commit v4 on v3

--- a/solution.py
+++ b/solution.py
@@ -13,6 +13,7 @@
 GAIN = 1.0 / (1.0 - 0.99)
 SEED_WEIGHT = (1.0 - ALPHA) * GAIN
 
+EARLY = 4
 LOCAL = 8
 VMEM = pltpu.VMEM
 IN_VMEM = pl.BlockSpec(memory_space=pltpu.VMEM)
@@ -113,9 +114,15 @@
         seen[row] = 0
         return carry
 
+    sends = x_a.shape[0]
+    early = block.shape[0] - 2 * sends
+    for row in range(early):
+        for copy in row_copies(weights, labels, held, block, sem, row, 2 * sends + row):
+            copy.start()
     lax.fori_loop(0, blocks_dev, unseen, 0, unroll=8)
+    for row in range(early):
+        seen[row] = 1
     get_lists.wait()
-    sends = lists.shape[2]
     order = toward_x()
     rows = [sent_row(lists, order, sends, i) for i in range(len(order) * sends)]
     for i, row in enumerate(rows):
@@ -127,6 +134,11 @@
             for copy in row_copies(weights, labels, held, block, sem, row, i):
                 copy.start()
 
+    for row in range(early):
+        for copy in row_copies(weights, labels, held, block, sem, row, 2 * sends + row):
+            copy.wait()
+    for row in range(early):
+        scale_row(held, block, extended, scales, row, 2 * sends + row)
     for i, row in enumerate(rows):
 
         @pl.when(fresh[i] == 1)
@@ -154,6 +166,8 @@
     for direction in toward_x():
         for i in range(lists.shape[2]):
             seen[lists[0, direction, i]] = 1
+    for row in range(EARLY):
+        seen[row] = 1
 
     def fetch(row, number):
         @pl.when(seen[row] == 0)
@@ -195,13 +209,21 @@
     copy_out(extended, lists, toward_y(), (y_a, y_b))
 
 
+def pick_body(lists, source, out, *, number):
+    direction = toward_y()[number]
+    for i in range(out.shape[0]):
+        out[i] = source[lists[0, direction, i]]
+
+
 def near(weights, extended, columns, scales, counts, row):
     topics = extended.shape[2]
     product = weighted(weights, extended, columns, row, 0, LOCAL)
     return spread_over(ALPHA * scales[row], topics) * product + SEED_WEIGHT * counts[row].astype(jnp.float32)
 
 
-def near_body(columns, weights, extended, scales, counts, partial, *, unroll):
+def near_body(columns, weights, extended, scales, counts, *rest, unroll):
+    partial = rest[-1]
+
     def step(row, carry):
         partial[row] = near(weights, extended, columns, scales, counts, row)
         return carry
@@ -227,14 +249,14 @@
 
 
 def second_send_body(
-    columns, lists, weights, extended_in, scales, partial, r0, r1, r2, r3, x_a, x_b, x_c, y_a, y_b, extended
+    columns, lists, weights, extended_in, scales, partial, r0, r1, r2, r3, x_a, x_b, extended
 ):
     sends = lists.shape[2]
     topics = x_a.shape[2]
     arrivals((r0, r1, r2, r3), extended)
-    order = toward_x() + toward_y()
+    order = toward_x()
     i = 0
-    for out in (x_a, x_b, x_c, y_a, y_b):
+    for out in (x_a, x_b):
         for j in range(out.shape[0]):
             row = sent_row(lists, order, sends, i)
             value = finished(weights, extended, columns, scales, partial, row)
@@ -242,7 +264,7 @@
             i += 1
 
 
-def rest_body(columns, weights, extended, scales, partial, following, *, unroll):
+def rest_body(columns, lists, weights, extended, scales, partial, following, y_a, y_b, handed, *, unroll):
     blocks_dev, _, topics = partial.shape
 
     def finish(row, carry):
@@ -251,13 +273,14 @@
         return carry
 
     lax.fori_loop(0, blocks_dev, finish, 0, unroll=unroll)
+    copy_out(following, lists, toward_y(), (y_a, y_b))
 
 
 def last_body(
-    columns, weights, extended_in, scales, partial, r0, r1, r2, r3, r4, out, extended, block, sem, *, unroll
+    columns, weights, extended_in, scales, partial, r0, r1, r2, r3, out, extended, block, sem, *, unroll
 ):
     blocks_dev = partial.shape[0]
-    arrivals((r0, r1, r2, r3, r4), extended)
+    arrivals((r0, r1, r2, r3), extended)
 
     def leave(row):
         return pltpu.make_async_copy(block.at[row], out.at[row], sem.at[row])
@@ -276,35 +299,42 @@
     lax.fori_loop(0, blocks_dev, settle, 0)
 
 
-def swap_pairs(axis, first):
+ROUND = ((0, 1), (1, 3), (3, 2), (2, 0))
+
+
+def neighbours(count, first):
+    pairs = [p for low in range(first, count - 1, 2) for p in ((low, low + 1), (low + 1, low))]
+    return pairs, [place for place in range(count) if all(place != source for source, _ in pairs)]
+
+
+def permuted(value, pairs):
+    inner = lax.axis_size("gy")
+    return lax.ppermute(value, ("gx", "gy"), sorted((a * inner + b, c * inner + d) for (a, b), (c, d) in pairs))
+
+
+def along_x(line, pairs):
+    return [((source, line), (target, line)) for source, target in pairs]
+
+
+def along_y(line, pairs):
+    return [((line, source), (line, target)) for source, target in pairs]
+
+
+def x_swap(value, first):
     outer, inner = lax.axis_size("gx"), lax.axis_size("gy")
-    count, other = (outer, inner) if axis == "gx" else (inner, outer)
-    lines = []
-    for low in range(first, count - 1, 2):
-        lines += [((low, line), (low + 1, line)) for line in range(other)]
-    alone = [place for place in range(count) if all(place not in (p[0], q[0]) for p, q in lines)]
-    half = 1 if axis == "gx" else other // 2
-    for place in alone:
-        for line in range(other):
-            if line // half % 2 == 0 and line + half < other:
-                lines.append(((place, line), (place, line + half)))
-    number = (lambda place, line: place * inner + line) if axis == "gx" else (lambda place, line: line * inner + place)
-    pairs = []
-    for p, q in lines:
-        low, high = number(*p), number(*q)
-        pairs += [(low, high), (high, low)]
-    return sorted(pairs)
-
-
-def swapped(value, axis, first):
-    return lax.ppermute(value, ("gx", "gy"), swap_pairs(axis, first))
-
-
-def relayed(value):
-    if lax.axis_size("gx") != 4:
-        return swapped(value, "gx", 1)
-    value = lax.ppermute(value, "gx", [(0, 2), (1, 3), (2, 0), (3, 1)])
-    return lax.ppermute(value, "gx", [(0, 1), (1, 3), (3, 2), (2, 0)])
+    pairs, alone = neighbours(outer, first)
+    moves = [move for line in range(inner) for move in along_x(line, pairs)]
+    moves += [move for place in alone for move in along_y(place, neighbours(inner, 0)[0])]
+    return permuted(value, moves)
+
+
+def y_swap(value, first, whole=True):
+    outer, inner = lax.axis_size("gx"), lax.axis_size("gy")
+    pairs, alone = neighbours(inner, first)
+    moves = [move for line in range(outer) for move in along_y(line, pairs)]
+    if whole:
+        moves += [move for place in alone for move in along_x(place, ROUND if outer == 4 else neighbours(outer, 0)[0])]
+    return permuted(value, moves)
 
 
 def local(labels, weights, column_index, send_index, seed_doc, seed_topic):
@@ -318,10 +348,7 @@
     send_index = unmoved(send_index)
     seed_doc = seed_doc.reshape(1, seeds)
     seed_topic = seed_topic.reshape(1, seeds)
-    half = sends // 2
     whole = VMEM((sends, block_size, topics), jnp.bfloat16)
-    first_half = VMEM((half, block_size, topics), jnp.bfloat16)
-    second_half = VMEM((sends - half, block_size, topics), jnp.bfloat16)
     held_shape = VMEM(weights.shape, jnp.bfloat16)
     extended_shape = VMEM((blocks_dev + 4 * sends, block_size, topics), jnp.bfloat16)
     scale_shape = VMEM((blocks_dev, block_size, block_size), jnp.float32)
@@ -335,14 +362,14 @@
         (IN_VMEM,) * 5 + (IN_SMEM,) * 2,
         (ANYWHERE,) * 4,
         (
-            pltpu.VMEM((2 * sends, block_size, topics), jnp.float32),
+            pltpu.VMEM((2 * sends + EARLY, block_size, topics), jnp.float32),
             pltpu.SMEM((blocks_dev,), jnp.int32),
             pltpu.SMEM((2 * sends,), jnp.int32),
-            pltpu.SemaphoreType.DMA((2 * sends, 2)),
+            pltpu.SemaphoreType.DMA((2 * sends + EARLY, 2)),
             pltpu.SemaphoreType.DMA((2,)),
         ),
     )(unmoved(column_index.T), send_index, weights, labels)
-    x_a, x_b = swapped(x_a, "gx", 0), swapped(x_b, "gx", 1)
+    x_a, x_b = x_swap(x_a, 0), x_swap(x_b, 1)
     columns, lists = tabled(columns), tabled(lists)
 
     held, extended, scales, counts, y_a, y_b = call(
@@ -359,47 +386,49 @@
         ),
         aliases={5: 0, 6: 1, 7: 2},
     )(lists, seed_doc, seed_topic, weights, labels, pinned(held), pinned(extended), pinned(scales))
-    y_b, y_a = swapped(y_b, "gy", 1), swapped(y_a, "gy", 0)
+    y_a, y_b = y_swap(y_a, 0), y_swap(y_b, 1)
     held, scales, counts = pinned(held), pinned(scales), pinned(counts)
 
-    def started(extended):
+    def started(extended, *reused):
         return call(
             functools.partial(near_body, unroll=16),
             partial_shape,
             IN_VMEM,
-            (IN_SMEM,) + (IN_VMEM,) * 4,
-        )(columns, held, pinned(extended), scales, counts)
+            (IN_SMEM,) + (IN_VMEM,) * (4 + len(reused)),
+            aliases={4 + len(reused): 0} if reused else {},
+        )(columns, held, pinned(extended), scales, counts, *reused)
 
     partial = started(extended)
-    x_a, x_b, x_c, y_a, y_b, extended = call(
+    x_a, x_b, extended = call(
         second_send_body,
-        (whole, first_half, second_half, whole, whole, extended_shape),
-        (IN_VMEM,) * 6,
+        (whole, whole, extended_shape),
+        (IN_VMEM,) * 3,
         (IN_SMEM,) * 2 + (IN_VMEM,) * 8,
-        aliases={3: 5},
+        aliases={3: 2},
     )(columns, lists, held, pinned(extended), scales, pinned(partial), *map(pinned, (x_a, x_b, y_a, y_b)))
-    x_c, x_a, x_b = relayed(x_c), swapped(x_a, "gx", 0), swapped(x_b, "gx", 1)
-    y_b, y_a = swapped(y_b, "gy", 1), swapped(y_a, "gy", 0)
-
-    following = call(
+    x_a, x_b = x_swap(x_a, 0), x_swap(x_b, 1)
+
+    following, y_a, y_b, partial = call(
         functools.partial(rest_body, unroll=16),
-        extended_shape,
-        IN_VMEM,
-        (IN_SMEM,) + (IN_VMEM,) * 4,
-    )(columns, held, pinned(extended), scales, pinned(partial))
-    partial = started(following)
+        (extended_shape, whole, whole, partial_shape),
+        (IN_VMEM,) * 4,
+        (IN_SMEM,) * 2 + (IN_VMEM,) * 4,
+        aliases={5: 3},
+    )(columns, lists, held, pinned(extended), scales, pinned(partial))
+    y_a, y_b = y_swap(y_a, 0), y_swap(y_b, 1, whole=False)
+    partial = started(following, pinned(extended), pinned(partial))
 
     out, _ = call(
         functools.partial(last_body, unroll=16),
         (jax.ShapeDtypeStruct((blocks_dev, block_size, topics), jnp.float32), extended_shape),
         (ANYWHERE, IN_VMEM),
-        (IN_SMEM,) + (IN_VMEM,) * 9,
+        (IN_SMEM,) + (IN_VMEM,) * 8,
         (
             pltpu.VMEM((blocks_dev, block_size, topics), jnp.float32),
             pltpu.SemaphoreType.DMA((blocks_dev,)),
         ),
         aliases={2: 1},
-    )(columns, held, pinned(following), scales, pinned(partial), *map(pinned, (x_a, x_b, x_c, y_a, y_b)))
+    )(columns, held, pinned(following), scales, pinned(partial), *map(pinned, (x_a, x_b, y_a, y_b)))
     return out.reshape(documents, topics)
 
 

time: 37.5 us -> 35.3 us (0.941)
  the two profiles are of different devices: /device:TPU:0 before, /device:TPU:4 now
where the time goes in v4:
time: 35.3 us; the launch traced here: 35.1 us
  Pallas kernels  18.9 us (54%)
  waiting for transfers between devices  10.1 us (29%)
  starting transfers between devices  5.92 us (17%)
    ppermute x8, waiting for transfers between devices, permuted(): lax.ppermute(value, ('gx', 'gy'), sorted(((a * inner + b, c * inner + d)...  10.1 us
    ppermute x8, starting transfers between devices, permuted(): lax.ppermute(value, ('gx', 'gy'), sorted(((a * inner + b, c * inner + d)...  5.92 us
    pallas_call x2, Pallas kernels, started(): call(functools.partial(near_body, unroll=16), partial_shape, IN_VMEM, (IN...  5.22 us
    pallas_call x1, Pallas kernels, local(): call(functools.partial(degree_body, chunk=4), (held_shape, extended_shape...  5.21 us
    pallas_call x1, Pallas kernels, local(): call(first_send_body, (whole, whole, held_shape, extended_shape, scale_sh...  3.23 us
    pallas_call x1, Pallas kernels, local(): call(functools.partial(last_body, unroll=16), (jax.ShapeDtypeStruct((bloc...  2.88 us
    pallas_call x1, Pallas kernels, local(): call(functools.partial(rest_body, unroll=16), (extended_shape, whole, who...  1.81 us
  transfers between devices with their start and end apart: 8, of which 3 were waited for; matrix products, arithmetic and copies ran while one was open for 0% of the time, Pallas kernels for 35%

profile of v4, /device:TPU:4, one launch (start us, length us, event | category | flops | bytes accessed | tf_op | source)
XLA Modules:
  0.0 35.1 jit_solution(902298919593238796)
XLA Ops:
  0.0 0.0 copy-start
  0.0 0.0 copy-start.1
  0.0 3.2 %shard_map.64 = (bf16[4,128,256]{2,1,0:T(8,128)(2,1)S(1)}, bf16[4,128,256]{2,1,0:T(8,128)(2,1)S(1)}, bf16[32,12,128,128]{3,2,1,0:T(8,128)(2,1)S(1)}, bf16[48,128...) custom-call(s32[12,32]{1,0:T(8,128)} %bitcast.9, ...), custom_call_target="tpu_custom_call" | custom-call | flops 1 | bytes 1 | tf_op jit(solution)/shard_map/pallas_call | solution.py:358
  3.2 1.4 %collective-permute-start = (bf16[4,128,256]{2,1,0:T(8,128)(2,1)S(1)}, bf16[4,128,256]{2,1,0:T(8,128)(2,1)S(1)}, u32[]{:S(2)}, u32[]{:S(2)}) collective-permute-start(bf16[4,128,256]{2,1,0:T(8,128)(2,1)S(1)} %get-tuple-element.35), channel_id=1, source_target_pairs={{0,8},{1,9},{2,10},{3,11},{4,12},{5,13},{6,14},{7,15},{8,0},{9,1},... | collective-permute-start | bytes 786440 | tf_op jit(solution)/shard_map/ppermute | solution.py:312
  4.6 0.3 collective-permute-start.1
  5.0 0.0 copy-done
  5.0 0.0 copy-done.1
  5.0 5.2 %shard_map.65 = (bf16[32,12,128,128]{3,2,1,0:T(8,128)(2,1)S(1)}, bf16[48,128,256]{2,1,0:T(8,128)(2,1)S(1)}, f32[32,128,128]{2,1,0:T(8,128)S(1)}, bf16[32,128,256...) custom-call(s32[1,4,4]{2,1,0:T(4,128)S(4)} %get-tuple-element.27.lis, ...), custom_call_target="tpu_custom_call", output_to_operand_aliasing={{0}: (5, {}), {1}: (6, {}), {2}: (7, {})} | custom-call | flops 1 | bytes 1 | tf_op jit(solution)/shard_map/pallas_call | solution.py:375
  10.2 0.1 collective-permute-start.2
  10.3 0.7 %collective-permute-start.3 = (bf16[4,128,256]{2,1,0:T(8,128)(2,1)S(1)}, bf16[4,128,256]{2,1,0:T(8,128)(2,1)S(1)}, u32[]{:S(2)}, u32[]{:S(2)}) collective-permute-start(bf16[4,128,256]{2,1,0:T(8,128)(2,1)S(1)} %get-tuple-element.38), channel_id=1, source_target_pairs={{0,8},{1,2},{2,1},{3,4},{4,3},{5,6},{6,5},{7,15},{8,24},{9,10},{10... | collective-permute-start | bytes 786440 | tf_op jit(solution)/shard_map/ppermute | solution.py:312
  11.0 2.6 %shard_map.66.partial = f32[32,128,256]{2,1,0:T(8,128)S(1)} custom-call(s32[12,32]{1,0:T(8,128)S(4)} %get-tuple-element.26.columns, bf16[32,12,128,128]{3,2,1,0:T(8,128)(2,1)S(1)} %get-tuple-element.31.weights, bf16[48,128,256]{2,1,0:T(8,128)(2,1)S(1)} %get-tuple-element.32.extended.extended_in, f32[32,128,128]{2,1,0:T(8,128)S(1)} %get-tuple-element.33.scales, ...), custom_call_target="tpu_custom_call" | custom-call | flops 1 | bytes 1 | tf_op jit(solution)/shard_map/pallas_call | solution.py:393
  13.6 0.0 collective-permute-done.r0
  13.6 3.2 %collective-permute-done.1.r1 = bf16[4,128,256]{2,1,0:T(8,128)(2,1)S(1)} collective-permute-done((bf16[4,128,256]{2,1,0:T(8,128)(2,1)S(1)}, bf16[4,128,256]{2,1,0:T(8,128)(2,1)S(1)}, u32[]{:S(2)}, u32[]{:S(2)}) %collective-permute-start.1) | collective-permute-done | bytes 262176 | tf_op jit(solution)/shard_map/ppermute | solution.py:312
  16.8 0.0 collective-permute-done.2.r2
  16.8 0.0 collective-permute-done.3.r3
  16.8 0.6 %shard_map.67 = (bf16[4,128,256]{2,1,0:T(8,128)(2,1)S(1)}, bf16[4,128,256]{2,1,0:T(8,128)(2,1)S(1)}, bf16[48,128,256]{2,1,0:T(8,128)(2,1)S(1)}) custom-call(s32[12,32]{1,0:T(8,128)S(4)} %get-tuple-element.26.columns, s32[1,4,4]{2,1,0:T(4,128)S(4)} %get-tuple-element.27.lists, ...), custom_call_target="tpu_custom_call", output_to_operand_aliasing={{2}: (3, {})} | custom-call | flops 1 | bytes 1 | tf_op jit(solution)/shard_map/pallas_call | solution.py:402
  17.4 1.1 %collective-permute-start.4 = (bf16[4,128,256]{2,1,0:T(8,128)(2,1)S(1)}, bf16[4,128,256]{2,1,0:T(8,128)(2,1)S(1)}, u32[]{:S(2)}, u32[]{:S(2)}) collective-permute-start(bf16[4,128,256]{2,1,0:T(8,128)(2,1)S(1)} %get-tuple-element.42), channel_id=1, source_target_pairs={{0,8},{1,9},{2,10},{3,11},{4,12},{5,13},{6,14},{7,15},{8,0},{9,1},... | collective-permute-start | bytes 786440 | tf_op jit(solution)/shard_map/ppermute | solution.py:312
  18.5 1.6 %collective-permute-start.5 = (bf16[4,128,256]{2,1,0:T(8,128)(2,1)S(1)}, bf16[4,128,256]{2,1,0:T(8,128)(2,1)S(1)}, u32[]{:S(2)}, u32[]{:S(2)}) collective-permute-start(bf16[4,128,256]{2,1,0:T(8,128)(2,1)S(1)} %get-tuple-element.43), channel_id=1, source_target_pairs={{0,1},{1,0},{2,3},{3,2},{4,5},{5,4},{6,7},{7,6},{8,16},{9,17},{10,... | collective-permute-start | bytes 786440 | tf_op jit(solution)/shard_map/ppermute | solution.py:312
  20.1 1.8 %shard_map.68 = (bf16[48,128,256]{2,1,0:T(8,128)(2,1)S(1)}, bf16[4,128,256]{2,1,0:T(8,128)(2,1)S(1)}, bf16[4,128,256]{2,1,0:T(8,128)(2,1)S(1)}, f32[32,128,256]{2,1,0:T(8,128)S(1)}) custom-call(s32[12,32]{1,0:T(8,128)S(4)} %get-tuple-element.26.columns, s32[1,4,4]{2,1,0:T(4,128)S(4)} %get-tuple-element.27.lists, ...), custom_call_target="tpu_custom_call", output_to_operand_aliasing={{3}: (5, {})} | custom-call | flops 1 | bytes 1 | tf_op jit(solution)/shard_map/pallas_call | solution.py:411
  21.9 0.1 collective-permute-start.6
  22.0 0.7 %collective-permute-start.7 = (bf16[4,128,256]{2,1,0:T(8,128)(2,1)S(1)}, bf16[4,128,256]{2,1,0:T(8,128)(2,1)S(1)}, u32[]{:S(2)}, u32[]{:S(2)}) collective-permute-start(bf16[4,128,256]{2,1,0:T(8,128)(2,1)S(1)} %get-tuple-element.45), channel_id=1, source_target_pairs={{1,2},{2,1},{3,4},{4,3},{5,6},{6,5},{9,10},{10,9},{11,12},{12,11},... | collective-permute-start | bytes 786440 | tf_op jit(solution)/shard_map/ppermute | solution.py:312
  22.7 2.6 %shard_map.69.partial = f32[32,128,256]{2,1,0:T(8,128)S(1)} custom-call(s32[12,32]{1,0:T(8,128)S(4)} %get-tuple-element.26.columns, bf16[32,12,128,128]{3,2,1,0:T(8,128)(2,1)S(1)} %get-tuple-element.31.weights, bf16[48,128,256]{2,1,0:T(8,128)(2,1)S(1)} %get-tuple-element.40.extended.extended_in, ...), custom_call_target="tpu_custom_call", output_to_operand_aliasing={{}: (6, {})} | custom-call | flops 1 | bytes 1 | tf_op jit(solution)/shard_map/pallas_call | solution.py:393
  25.3 0.5 %collective-permute-done.4.r0 = bf16[4,128,256]{2,1,0:T(8,128)(2,1)S(1)} collective-permute-done((bf16[4,128,256]{2,1,0:T(8,128)(2,1)S(1)}, bf16[4,128,256]{2,1,0:T(8,128)(2,1)S(1)}, u32[]{:S(2)}, u32[]{:S(2)}) %collective-permute-start.4) | collective-permute-done | bytes 262176 | tf_op jit(solution)/shard_map/ppermute | solution.py:312
  25.8 6.4 %collective-permute-done.5.r1 = bf16[4,128,256]{2,1,0:T(8,128)(2,1)S(1)} collective-permute-done((bf16[4,128,256]{2,1,0:T(8,128)(2,1)S(1)}, bf16[4,128,256]{2,1,0:T(8,128)(2,1)S(1)}, u32[]{:S(2)}, u32[]{:S(2)}) %collective-permute-start.5) | collective-permute-done | bytes 262176 | tf_op jit(solution)/shard_map/ppermute | solution.py:312
  32.2 0.0 collective-permute-done.6.r2
  32.2 0.0 collective-permute-done.7.r3
  32.2 2.9 %shard_map.70 = (f32[32,128,256]{2,1,0:T(8,128)}, bf16[48,128,256]{2,1,0:T(8,128)(2,1)S(1)}) custom-call(s32[12,32]{1,0:T(8,128)S(4)} %get-tuple-element.26.columns, bf16[32,12,128,128]{3,2,1,0:T(8,128)(2,1)S(1)} %get-tuple-element.31.weights, bf16[48,128,256]{2,1,0:T(8,128)(2,1)S(1)} %get-tuple-element.40.extended.extended_in, ...), custom_call_target="tpu_custom_call", output_to_operand_aliasing={{1}: (2, {})} | custom-call | flops 1 | bytes 1 | tf_op jit(solution)/shard_map/pallas_call | solution.py:421
Async XLA Ops:
  0.0 5.0 %copy-start = (s32[256]{0:T(256)S(1)}, s32[256]{0:T(256)}, u32[]{:S(2)}) copy-start(s32[256]{0:T(256)} %param.10) | copy-start | bytes 3076
  0.0 5.0 %copy-start.1 = (s32[256]{0:T(256)S(1)}, s32[256]{0:T(256)}, u32[]{:S(2)}) copy-start(s32[256]{0:T(256)} %param.11) | copy-start | bytes 3076
  3.2 10.3 %collective-permute-start = (bf16[4,128,256]{2,1,0:T(8,128)(2,1)S(1)}, bf16[4,128,256]{2,1,0:T(8,128)(2,1)S(1)}, u32[]{:S(2)}, u32[]{:S(2)}) collective-permute-start(bf16[4,128,256]{2,1,0:T(8,128)(2,1)S(1)} %get-tuple-element.35), channel_id=1, source_target_pairs={{0,8},{1,9},{2,10},{3,11},{4,12},{5,13},{6,14},{7,15},{8,0},{9,1},... | collective-permute-start | bytes 786440 | tf_op jit(solution)/shard_map/ppermute | solution.py:312
  4.6 12.2 %collective-permute-start.1 = (bf16[4,128,256]{2,1,0:T(8,128)(2,1)S(1)}, bf16[4,128,256]{2,1,0:T(8,128)(2,1)S(1)}, u32[]{:S(2)}, u32[]{:S(2)}) collective-permute-start(bf16[4,128,256]{2,1,0:T(8,128)(2,1)S(1)} %get-tuple-element.36), channel_id=1, source_target_pairs={{0,1},{1,0},{2,3},{3,2},{4,5},{5,4},{6,7},{7,6},{8,16},{9,17},{10,... | collective-permute-start | bytes 786440 | tf_op jit(solution)/shard_map/ppermute | solution.py:312
  10.2 6.6 %collective-permute-start.2 = (bf16[4,128,256]{2,1,0:T(8,128)(2,1)S(1)}, bf16[4,128,256]{2,1,0:T(8,128)(2,1)S(1)}, u32[]{:S(2)}, u32[]{:S(2)}) collective-permute-start(bf16[4,128,256]{2,1,0:T(8,128)(2,1)S(1)} %get-tuple-element.37), channel_id=1, source_target_pairs={{0,1},{1,0},{2,3},{3,2},{4,5},{5,4},{6,7},{7,6},{8,9},{9,8},{10,11... | collective-permute-start | bytes 786440 | tf_op jit(solution)/shard_map/ppermute | solution.py:312
  10.3 6.5 %collective-permute-start.3 = (bf16[4,128,256]{2,1,0:T(8,128)(2,1)S(1)}, bf16[4,128,256]{2,1,0:T(8,128)(2,1)S(1)}, u32[]{:S(2)}, u32[]{:S(2)}) collective-permute-start(bf16[4,128,256]{2,1,0:T(8,128)(2,1)S(1)} %get-tuple-element.38), channel_id=1, source_target_pairs={{0,8},{1,2},{2,1},{3,4},{4,3},{5,6},{6,5},{7,15},{8,24},{9,10},{10... | collective-permute-start | bytes 786440 | tf_op jit(solution)/shard_map/ppermute | solution.py:312
  17.4 8.4 %collective-permute-start.4 = (bf16[4,128,256]{2,1,0:T(8,128)(2,1)S(1)}, bf16[4,128,256]{2,1,0:T(8,128)(2,1)S(1)}, u32[]{:S(2)}, u32[]{:S(2)}) collective-permute-start(bf16[4,128,256]{2,1,0:T(8,128)(2,1)S(1)} %get-tuple-element.42), channel_id=1, source_target_pairs={{0,8},{1,9},{2,10},{3,11},{4,12},{5,13},{6,14},{7,15},{8,0},{9,1},... | collective-permute-start | bytes 786440 | tf_op jit(solution)/shard_map/ppermute | solution.py:312
  18.5 13.7 %collective-permute-start.5 = (bf16[4,128,256]{2,1,0:T(8,128)(2,1)S(1)}, bf16[4,128,256]{2,1,0:T(8,128)(2,1)S(1)}, u32[]{:S(2)}, u32[]{:S(2)}) collective-permute-start(bf16[4,128,256]{2,1,0:T(8,128)(2,1)S(1)} %get-tuple-element.43), channel_id=1, source_target_pairs={{0,1},{1,0},{2,3},{3,2},{4,5},{5,4},{6,7},{7,6},{8,16},{9,17},{10,... | collective-permute-start | bytes 786440 | tf_op jit(solution)/shard_map/ppermute | solution.py:312
  21.9 10.3 %collective-permute-start.6 = (bf16[4,128,256]{2,1,0:T(8,128)(2,1)S(1)}, bf16[4,128,256]{2,1,0:T(8,128)(2,1)S(1)}, u32[]{:S(2)}, u32[]{:S(2)}) collective-permute-start(bf16[4,128,256]{2,1,0:T(8,128)(2,1)S(1)} %get-tuple-element.44), channel_id=1, source_target_pairs={{0,1},{1,0},{2,3},{3,2},{4,5},{5,4},{6,7},{7,6},{8,9},{9,8},{10,11... | collective-permute-start | bytes 786440 | tf_op jit(solution)/shard_map/ppermute | solution.py:312
  22.0 10.2 %collective-permute-start.7 = (bf16[4,128,256]{2,1,0:T(8,128)(2,1)S(1)}, bf16[4,128,256]{2,1,0:T(8,128)(2,1)S(1)}, u32[]{:S(2)}, u32[]{:S(2)}) collective-permute-start(bf16[4,128,256]{2,1,0:T(8,128)(2,1)S(1)} %get-tuple-element.45), channel_id=1, source_target_pairs={{1,2},{2,1},{3,4},{4,3},{5,6},{6,5},{9,10},{10,9},{11,12},{12,11},... | collective-permute-start | bytes 786440 | tf_op jit(solution)/shard_map/ppermute | solution.py:312

commit v5 on v4

--- a/solution.py
+++ b/solution.py
@@ -147,7 +147,8 @@
                 copy.wait()
             scale_row(held, block, extended, scales, row, i)
 
-    copy_out(extended, lists, order, (x_a, x_b))
+        out = x_a if i < sends else x_b
+        out[i % sends] = extended[row]
     get_columns.wait()
 
 
@@ -249,22 +250,20 @@
 
 
 def second_send_body(
-    columns, lists, weights, extended_in, scales, partial, r0, r1, r2, r3, x_a, x_b, extended
+    columns, lists, weights, extended_in, scales, partial, r0, r1, r2, r3, x_a, x_b, y_a, y_b, extended
 ):
     sends = lists.shape[2]
     topics = x_a.shape[2]
-    arrivals((r0, r1, r2, r3), extended)
-    order = toward_x()
-    i = 0
-    for out in (x_a, x_b):
-        for j in range(out.shape[0]):
-            row = sent_row(lists, order, sends, i)
+    arrivals((r1, r0, r3, r2), extended)
+    order = toward_x() + toward_y()
+    for number, out in ((1, x_b), (0, x_a), (3, y_b), (2, y_a)):
+        for i in range(sends):
+            row = lists[0, order[number], i]
             value = finished(weights, extended, columns, scales, partial, row)
-            out[j] = (spread_over(scales[row], topics) * value).astype(jnp.bfloat16)
-            i += 1
-
-
-def rest_body(columns, lists, weights, extended, scales, partial, following, y_a, y_b, handed, *, unroll):
+            out[i] = (spread_over(scales[row], topics) * value).astype(jnp.bfloat16)
+
+
+def rest_body(columns, weights, extended, scales, partial, following, handed, *, unroll):
     blocks_dev, _, topics = partial.shape
 
     def finish(row, carry):
@@ -273,7 +272,18 @@
         return carry
 
     lax.fori_loop(0, blocks_dev, finish, 0, unroll=unroll)
-    copy_out(following, lists, toward_y(), (y_a, y_b))
+
+
+def hand_on_body(direct, first_hop, out):
+    straight = lax.axis_index("gy") % 2 == 0
+
+    @pl.when(straight)
+    def _():
+        out[...] = direct[...]
+
+    @pl.when(jnp.logical_not(straight))
+    def _():
+        out[...] = first_hop[...]
 
 
 def last_body(
@@ -300,6 +310,15 @@
 
 
 ROUND = ((0, 1), (1, 3), (3, 2), (2, 0))
+ACROSS = ((0, 2), (2, 0), (1, 3), (3, 1))
+FIRST_HOP = (
+    ((1, 1), (3, 1)), ((3, 1), (3, 0)), ((3, 0), (1, 0)), ((1, 0), (1, 1)),
+    ((2, 1), (0, 1)), ((0, 1), (0, 0)), ((0, 0), (2, 0)), ((2, 0), (2, 1)),
+)
+SECOND_HOP = (
+    ((0, 1), (1, 1)), ((1, 1), (3, 0)), ((3, 0), (3, 1)), ((3, 1), (2, 1)), ((2, 1), (0, 0)), ((0, 0), (0, 1)),
+    ((1, 0), (2, 0)), ((2, 0), (1, 0)),
+)
 
 
 def neighbours(count, first):
@@ -328,13 +347,22 @@
     return permuted(value, moves)
 
 
-def y_swap(value, first, whole=True):
+def by_corner():
+    return lax.axis_size("gx") == 4 and lax.axis_size("gy") % 2 == 0
+
+
+def hop(value, moves):
+    lines = range(0, lax.axis_size("gy"), 2)
+    return permuted(value, [((a, low + p), (c, low + q)) for low in lines for (a, p), (c, q) in moves])
+
+
+def y_swap(value, first, idle=()):
     outer, inner = lax.axis_size("gx"), lax.axis_size("gy")
     pairs, alone = neighbours(inner, first)
     moves = [move for line in range(outer) for move in along_y(line, pairs)]
-    if whole:
-        moves += [move for place in alone for move in along_x(place, ROUND if outer == 4 else neighbours(outer, 0)[0])]
-    return permuted(value, moves)
+    if outer != 4:
+        idle = neighbours(outer, 0)[0]
+    return permuted(value, moves + [move for place in alone for move in along_x(place, idle)])
 
 
 def local(labels, weights, column_index, send_index, seed_doc, seed_topic):
@@ -369,7 +397,8 @@
             pltpu.SemaphoreType.DMA((2,)),
         ),
     )(unmoved(column_index.T), send_index, weights, labels)
-    x_a, x_b = x_swap(x_a, 0), x_swap(x_b, 1)
+    x_b = x_swap(x_b, 1)
+    x_a = x_swap(x_a, 0)
     columns, lists = tabled(columns), tabled(lists)
 
     held, extended, scales, counts, y_a, y_b = call(
@@ -386,7 +415,7 @@
         ),
         aliases={5: 0, 6: 1, 7: 2},
     )(lists, seed_doc, seed_topic, weights, labels, pinned(held), pinned(extended), pinned(scales))
-    y_a, y_b = y_swap(y_a, 0), y_swap(y_b, 1)
+    y_a, y_b = y_swap(y_a, 0), y_swap(y_b, 1, ROUND)
     held, scales, counts = pinned(held), pinned(scales), pinned(counts)
 
     def started(extended, *reused):
@@ -399,23 +428,29 @@
         )(columns, held, pinned(extended), scales, counts, *reused)
 
     partial = started(extended)
-    x_a, x_b, extended = call(
+    x_a, x_b, y_a, y_b, extended = call(
         second_send_body,
-        (whole, whole, extended_shape),
-        (IN_VMEM,) * 3,
+        (whole, whole, whole, whole, extended_shape),
+        (IN_VMEM,) * 5,
         (IN_SMEM,) * 2 + (IN_VMEM,) * 8,
-        aliases={3: 2},
-    )(columns, lists, held, pinned(extended), scales, pinned(partial), *map(pinned, (x_a, x_b, y_a, y_b)))
-    x_a, x_b = x_swap(x_a, 0), x_swap(x_b, 1)
-
-    following, y_a, y_b, partial = call(
+        aliases={3: 4},
+    )(columns, lists, held, pinned(extended), scales, pinned(partial), *map(pinned, (x_b, x_a, y_b, y_a)))
+    x_a = x_swap(x_a, 0)
+    if by_corner():
+        first_hop = hop(x_b, FIRST_HOP)
+        x_b = call(hand_on_body, whole, IN_VMEM, (IN_VMEM,) * 2)(*map(pinned, (x_b, first_hop)))
+        x_b = hop(x_b, SECOND_HOP)
+    else:
+        x_b = x_swap(x_b, 1)
+    y_a, y_b = y_swap(y_a, 0), y_swap(y_b, 1)
+
+    following, partial = call(
         functools.partial(rest_body, unroll=16),
-        (extended_shape, whole, whole, partial_shape),
-        (IN_VMEM,) * 4,
-        (IN_SMEM,) * 2 + (IN_VMEM,) * 4,
-        aliases={5: 3},
-    )(columns, lists, held, pinned(extended), scales, pinned(partial))
-    y_a, y_b = y_swap(y_a, 0), y_swap(y_b, 1, whole=False)
+        (extended_shape, partial_shape),
+        (IN_VMEM,) * 2,
+        (IN_SMEM,) + (IN_VMEM,) * 4,
+        aliases={4: 1},
+    )(columns, held, pinned(extended), scales, pinned(partial))
     partial = started(following, pinned(extended), pinned(partial))
 
     out, _ = call(

time: 35.3 us -> 34.6 us (0.980)
  waiting for transfers between devices: 10.1 us -> 6.54 us
  starting transfers between devices: 5.92 us -> 8.32 us
  Pallas kernels: 18.9 us -> 19.4 us
    ppermute x8 -> x9, waiting for transfers between devices: 10.1 us -> 6.54 us  [permuted(): lax.ppermute(value, ('gx', 'gy'), sorted(((a * inner + b, c * inner + d)...]
    ppermute x8 -> x9, starting transfers between devices: 5.92 us -> 8.32 us  [permuted(): lax.ppermute(value, ('gx', 'gy'), sorted(((a * inner + b, c * inner + d)...]
    pallas_call x2 -> x3, Pallas kernels: 2.41 us -> 2.76 us  [the longest x1 1.78 us: local(): call(functools.partial(rest_body, unroll=16), (extended_shape, partial_sh...]
  transfers between devices with their start and end apart: 8 -> 9, of which waited for: 3 -> 4; matrix products, arithmetic and copies ran while one was open for 0% -> 0% of each run, Pallas kernels for 35% -> 35%
where the time goes in v5:
time: 34.6 us; the launch traced here: 34.4 us
  Pallas kernels  19.4 us (56%)
  starting transfers between devices  8.32 us (24%)
  waiting for transfers between devices  6.54 us (19%)
    ppermute x9, starting transfers between devices, permuted(): lax.ppermute(value, ('gx', 'gy'), sorted(((a * inner + b, c * inner + d)...  8.32 us
    ppermute x9, waiting for transfers between devices, permuted(): lax.ppermute(value, ('gx', 'gy'), sorted(((a * inner + b, c * inner + d)...  6.54 us
    pallas_call x2, Pallas kernels, started(): call(functools.partial(near_body, unroll=16), partial_shape, IN_VMEM, (IN...  5.22 us
    pallas_call x1, Pallas kernels, local(): call(functools.partial(degree_body, chunk=4), (held_shape, extended_shape...  5.04 us
    pallas_call x1, Pallas kernels, local(): call(first_send_body, (whole, whole, held_shape, extended_shape, scale_sh...  3.5 us
    pallas_call x1, Pallas kernels, local(): call(functools.partial(last_body, unroll=16), (jax.ShapeDtypeStruct((bloc...  2.87 us
    pallas_call x1, Pallas kernels, local(): call(functools.partial(rest_body, unroll=16), (extended_shape, partial_sh...  1.78 us
    pallas_call x1, Pallas kernels, local(): call(second_send_body, (whole, whole, whole, whole, extended_shape), (IN_...  0.96 us
  transfers between devices with their start and end apart: 9, of which 4 were waited for; matrix products, arithmetic and copies ran while one was open for 0% of the time, Pallas kernels for 35%

profile of v5, /device:TPU:4, one launch (start us, length us, event | category | flops | bytes accessed | tf_op | source)
XLA Modules:
  0.0 34.4 jit_solution(17966058476183071239)
XLA Ops:
  0.0 0.0 copy-start
  0.0 0.0 copy-start.1
  0.0 3.5 %shard_map.64 = (bf16[4,128,256]{2,1,0:T(8,128)(2,1)S(1)}, bf16[4,128,256]{2,1,0:T(8,128)(2,1)S(1)}, bf16[32,12,128,128]{3,2,1,0:T(8,128)(2,1)S(1)}, bf16[48,128...) custom-call(s32[12,32]{1,0:T(8,128)} %bitcast.9, ...), custom_call_target="tpu_custom_call" | custom-call | flops 1 | bytes 1 | tf_op jit(solution)/shard_map/pallas_call | solution.py:386
  3.5 1.5 %collective-permute-start = (bf16[4,128,256]{2,1,0:T(8,128)(2,1)S(1)}, bf16[4,128,256]{2,1,0:T(8,128)(2,1)S(1)}, u32[]{:S(2)}, u32[]{:S(2)}) collective-permute-start(bf16[4,128,256]{2,1,0:T(8,128)(2,1)S(1)} %get-tuple-element.35), channel_id=1, source_target_pairs={{0,1},{1,0},{2,3},{3,2},{4,5},{5,4},{6,7},{7,6},{8,16},{9,17},{10,... | collective-permute-start | bytes 786440 | tf_op jit(solution)/shard_map/ppermute | solution.py:331
  5.0 0.0 collective-permute-start.1
  5.0 0.0 copy-done
  5.0 0.0 copy-done.1
  5.0 5.0 %shard_map.65 = (bf16[32,12,128,128]{3,2,1,0:T(8,128)(2,1)S(1)}, bf16[48,128,256]{2,1,0:T(8,128)(2,1)S(1)}, f32[32,128,128]{2,1,0:T(8,128)S(1)}, bf16[32,128,256...) custom-call(s32[1,4,4]{2,1,0:T(4,128)S(4)} %get-tuple-element.27.lis, ...), custom_call_target="tpu_custom_call", output_to_operand_aliasing={{0}: (5, {}), {1}: (6, {}), {2}: (7, {})} | custom-call | flops 1 | bytes 1 | tf_op jit(solution)/shard_map/pallas_call | solution.py:404
  10.1 2.3 %collective-permute-start.2 = (bf16[4,128,256]{2,1,0:T(8,128)(2,1)S(1)}, bf16[4,128,256]{2,1,0:T(8,128)(2,1)S(1)}, u32[]{:S(2)}, u32[]{:S(2)}) collective-permute-start(bf16[4,128,256]{2,1,0:T(8,128)(2,1)S(1)} %get-tuple-element.37), channel_id=1, source_target_pairs={{0,8},{1,2},{2,1},{3,4},{4,3},{5,6},{6,5},{7,15},{8,24},{9,10},{10... | collective-permute-start | bytes 786440 | tf_op jit(solution)/shard_map/ppermute | solution.py:331
  12.4 0.0 collective-permute-start.3
  12.4 2.6 %shard_map.66.partial = f32[32,128,256]{2,1,0:T(8,128)S(1)} custom-call(s32[12,32]{1,0:T(8,128)S(4)} %get-tuple-element.26.columns, bf16[32,12,128,128]{3,2,1,0:T(8,128)(2,1)S(1)} %get-tuple-element.31.weights, bf16[48,128,256]{2,1,0:T(8,128)(2,1)S(1)} %get-tuple-element.32.extended.extended_in, f32[32,128,128]{2,1,0:T(8,128)S(1)} %get-tuple-element.33.scales, ...), custom_call_target="tpu_custom_call" | custom-call | flops 1 | bytes 1 | tf_op jit(solution)/shard_map/pallas_call | solution.py:422
  15.0 0.0 collective-permute-done.r0
  15.0 1.2 %collective-permute-done.1.r1 = bf16[4,128,256]{2,1,0:T(8,128)(2,1)S(1)} collective-permute-done((bf16[4,128,256]{2,1,0:T(8,128)(2,1)S(1)}, bf16[4,128,256]{2,1,0:T(8,128)(2,1)S(1)}, u32[]{:S(2)}, u32[]{:S(2)}) %collective-permute-start.1) | collective-permute-done | bytes 262176 | tf_op jit(solution)/shard_map/ppermute | solution.py:331
  16.2 0.5 %collective-permute-done.2.r2 = bf16[4,128,256]{2,1,0:T(8,128)(2,1)S(1)} collective-permute-done((bf16[4,128,256]{2,1,0:T(8,128)(2,1)S(1)}, bf16[4,128,256]{2,1,0:T(8,128)(2,1)S(1)}, u32[]{:S(2)}, u32[]{:S(2)}) %collective-permute-start.2) | collective-permute-done | bytes 262176 | tf_op jit(solution)/shard_map/ppermute | solution.py:331
  16.7 0.0 collective-permute-done.3.r3
  16.7 1.0 %shard_map.67 = (bf16[4,128,256]{2,1,0:T(8,128)(2,1)S(1)}, bf16[4,128,256]{2,1,0:T(8,128)(2,1)S(1)}, bf16[4,128,256]{2,1,0:T(8,128)(2,1)S(1)}, bf16[4,128,256]{2,1,0:T(8,128)(2,1)S(1)}, bf16[48,128,256]{2,1,0:T(8,128)(2,1)S(1)}) custom-call(s32[12,32]{1,0:T(8,128)S(4)} %get-tuple-element.26.columns, ...), custom_call_target="tpu_custom_call", output_to_operand_aliasing={{4}: (3, {})} | custom-call | flops 1 | bytes 1 | tf_op jit(solution)/shard_map/pallas_call | solution.py:431
  17.6 0.1 collective-permute-start.5
  17.7 2.1 %collective-permute-start.4 = (bf16[4,128,256]{2,1,0:T(8,128)(2,1)S(1)}, bf16[4,128,256]{2,1,0:T(8,128)(2,1)S(1)}, u32[]{:S(2)}, u32[]{:S(2)}) collective-permute-start(bf16[4,128,256]{2,1,0:T(8,128)(2,1)S(1)} %get-tuple-element.42), channel_id=1, source_target_pairs={{0,8},{1,9},{2,10},{3,11},{4,12},{5,13},{6,14},{7,15},{8,0},{9,1},... | collective-permute-start | bytes 786440 | tf_op jit(solution)/shard_map/ppermute | solution.py:331
  19.8 0.2 collective-permute-start.7
  20.0 0.7 %collective-permute-start.8 = (bf16[4,128,256]{2,1,0:T(8,128)(2,1)S(1)}, bf16[4,128,256]{2,1,0:T(8,128)(2,1)S(1)}, u32[]{:S(2)}, u32[]{:S(2)}) collective-permute-start(bf16[4,128,256]{2,1,0:T(8,128)(2,1)S(1)} %get-tuple-element.45), channel_id=1, source_target_pairs={{1,2},{2,1},{3,4},{4,3},{5,6},{6,5},{9,10},{10,9},{11,12},{12,11},... | collective-permute-start | bytes 786440 | tf_op jit(solution)/shard_map/ppermute | solution.py:331
  20.6 3.5 %collective-permute-done.5.first_hop = bf16[4,128,256]{2,1,0:T(8,128)(2,1)S(1)} collective-permute-done((bf16[4,128,256]{2,1,0:T(8,128)(2,1)S(1)}, bf16[4,128,256]{2,1,0:T(8,128)(2,1)S(1)}, u32[]{:S(2)}, u32[]{:S(2)}) %collective-permute-start.5) | collective-permute-done | bytes 262176 | tf_op jit(solution)/shard_map/ppermute | solution.py:331
  24.2 1.5 %collective-permute-start.6 = (bf16[4,128,256]{2,1,0:T(8,128)(2,1)S(1)}, bf16[4,128,256]{2,1,0:T(8,128)(2,1)S(1)}, u32[]{:S(2)}, u32[]{:S(2)}) collective-permute-start(bf16[4,128,256]{2,1,0:T(8,128)(2,1)S(1)} %shard_map.70), channel_id=1, source_target_pairs={{0,1},{1,9},{2,3},{3,11},{4,5},{5,13},{6,7},{7,15},{8,16},{9,24},{... | collective-permute-start | bytes 786440 | tf_op jit(solution)/shard_map/ppermute | solution.py:331
  25.7 1.8 %shard_map.68 = (bf16[48,128,256]{2,1,0:T(8,128)(2,1)S(1)}, f32[32,128,256]{2,1,0:T(8,128)S(1)}) custom-call(s32[12,32]{1,0:T(8,128)S(4)} %get-tuple-element.26.columns, bf16[32,12,128,128]{3,2,1,0:T(8,128)(2,1)S(1)} %get-tuple-element.31.weights, bf16[48,128,256]{2,1,0:T(8,128)(2,1)S(1)} %get-tuple-element.39.extended.rest_0_, ...), custom_call_target="tpu_custom_call", output_to_operand_aliasing={{1}: (4, {})} | custom-call | flops 1 | bytes 1 | tf_op jit(solution)/shard_map/pallas_call | solution.py:447
  27.5 2.6 %shard_map.69.partial = f32[32,128,256]{2,1,0:T(8,128)S(1)} custom-call(s32[12,32]{1,0:T(8,128)S(4)} %get-tuple-element.26.columns, bf16[32,12,128,128]{3,2,1,0:T(8,128)(2,1)S(1)} %get-tuple-element.31.weights, bf16[48,128,256]{2,1,0:T(8,128)(2,1)S(1)} %get-tuple-element.40.extended.extended_in, ...), custom_call_target="tpu_custom_call", output_to_operand_aliasing={{}: (6, {})} | custom-call | flops 1 | bytes 1 | tf_op jit(solution)/shard_map/pallas_call | solution.py:422
  30.1 0.0 collective-permute-done.4.r0
  30.1 0.0 collective-permute-done.7.r2
  30.1 0.0 collective-permute-done.8.r3
  30.1 1.4 %collective-permute-done.6.r1 = bf16[4,128,256]{2,1,0:T(8,128)(2,1)S(1)} collective-permute-done((bf16[4,128,256]{2,1,0:T(8,128)(2,1)S(1)}, bf16[4,128,256]{2,1,0:T(8,128)(2,1)S(1)}, u32[]{:S(2)}, u32[]{:S(2)}) %collective-permute-start.6) | collective-permute-done | bytes 262176 | tf_op jit(solution)/shard_map/ppermute | solution.py:331
  31.5 2.9 %shard_map.71 = (f32[32,128,256]{2,1,0:T(8,128)}, bf16[48,128,256]{2,1,0:T(8,128)(2,1)S(1)}) custom-call(s32[12,32]{1,0:T(8,128)S(4)} %get-tuple-element.26.columns, bf16[32,12,128,128]{3,2,1,0:T(8,128)(2,1)S(1)} %get-tuple-element.31.weights, bf16[48,128,256]{2,1,0:T(8,128)(2,1)S(1)} %get-tuple-element.40.extended.extended_in, ...), custom_call_target="tpu_custom_call", output_to_operand_aliasing={{1}: (2, {})} | custom-call | flops 1 | bytes 1 | tf_op jit(solution)/shard_map/pallas_call | solution.py:456
  (1 shorter events, 0.0 us)
Async XLA Ops:
  0.0 5.0 %copy-start = (s32[256]{0:T(256)S(1)}, s32[256]{0:T(256)}, u32[]{:S(2)}) copy-start(s32[256]{0:T(256)} %param.10) | copy-start | bytes 3076
  0.0 5.0 %copy-start.1 = (s32[256]{0:T(256)S(1)}, s32[256]{0:T(256)}, u32[]{:S(2)}) copy-start(s32[256]{0:T(256)} %param.11) | copy-start | bytes 3076
  3.5 11.5 %collective-permute-start = (bf16[4,128,256]{2,1,0:T(8,128)(2,1)S(1)}, bf16[4,128,256]{2,1,0:T(8,128)(2,1)S(1)}, u32[]{:S(2)}, u32[]{:S(2)}) collective-permute-start(bf16[4,128,256]{2,1,0:T(8,128)(2,1)S(1)} %get-tuple-element.35), channel_id=1, source_target_pairs={{0,1},{1,0},{2,3},{3,2},{4,5},{5,4},{6,7},{7,6},{8,16},{9,17},{10,... | collective-permute-start | bytes 786440 | tf_op jit(solution)/shard_map/ppermute | solution.py:331
  5.0 11.2 %collective-permute-start.1 = (bf16[4,128,256]{2,1,0:T(8,128)(2,1)S(1)}, bf16[4,128,256]{2,1,0:T(8,128)(2,1)S(1)}, u32[]{:S(2)}, u32[]{:S(2)}) collective-permute-start(bf16[4,128,256]{2,1,0:T(8,128)(2,1)S(1)} %get-tuple-element.36), channel_id=1, source_target_pairs={{0,8},{1,9},{2,10},{3,11},{4,12},{5,13},{6,14},{7,15},{8,0},{9,1},... | collective-permute-start | bytes 786440 | tf_op jit(solution)/shard_map/ppermute | solution.py:331
  10.1 6.6 %collective-permute-start.2 = (bf16[4,128,256]{2,1,0:T(8,128)(2,1)S(1)}, bf16[4,128,256]{2,1,0:T(8,128)(2,1)S(1)}, u32[]{:S(2)}, u32[]{:S(2)}) collective-permute-start(bf16[4,128,256]{2,1,0:T(8,128)(2,1)S(1)} %get-tuple-element.37), channel_id=1, source_target_pairs={{0,8},{1,2},{2,1},{3,4},{4,3},{5,6},{6,5},{7,15},{8,24},{9,10},{10... | collective-permute-start | bytes 786440 | tf_op jit(solution)/shard_map/ppermute | solution.py:331
  12.4 4.3 %collective-permute-start.3 = (bf16[4,128,256]{2,1,0:T(8,128)(2,1)S(1)}, bf16[4,128,256]{2,1,0:T(8,128)(2,1)S(1)}, u32[]{:S(2)}, u32[]{:S(2)}) collective-permute-start(bf16[4,128,256]{2,1,0:T(8,128)(2,1)S(1)} %get-tuple-element.38), channel_id=1, source_target_pairs={{0,1},{1,0},{2,3},{3,2},{4,5},{5,4},{6,7},{7,6},{8,9},{9,8},{10,11... | collective-permute-start | bytes 786440 | tf_op jit(solution)/shard_map/ppermute | solution.py:331
  17.6 6.5 %collective-permute-start.5 = (bf16[4,128,256]{2,1,0:T(8,128)(2,1)S(1)}, bf16[4,128,256]{2,1,0:T(8,128)(2,1)S(1)}, u32[]{:S(2)}, u32[]{:S(2)}) collective-permute-start(bf16[4,128,256]{2,1,0:T(8,128)(2,1)S(1)} %get-tuple-element.43.direct), channel_id=1, source_target_pairs={{0,16},{1,0},{2,18},{3,2},{4,20},{5,4},{6,22},{7,6},{8,9},{9,25},{... | collective-permute-start | bytes 786440 | tf_op jit(solution)/shard_map/ppermute | solution.py:331
  17.7 12.4 %collective-permute-start.4 = (bf16[4,128,256]{2,1,0:T(8,128)(2,1)S(1)}, bf16[4,128,256]{2,1,0:T(8,128)(2,1)S(1)}, u32[]{:S(2)}, u32[]{:S(2)}) collective-permute-start(bf16[4,128,256]{2,1,0:T(8,128)(2,1)S(1)} %get-tuple-element.42), channel_id=1, source_target_pairs={{0,8},{1,9},{2,10},{3,11},{4,12},{5,13},{6,14},{7,15},{8,0},{9,1},... | collective-permute-start | bytes 786440 | tf_op jit(solution)/shard_map/ppermute | solution.py:331
  19.8 10.3 %collective-permute-start.7 = (bf16[4,128,256]{2,1,0:T(8,128)(2,1)S(1)}, bf16[4,128,256]{2,1,0:T(8,128)(2,1)S(1)}, u32[]{:S(2)}, u32[]{:S(2)}) collective-permute-start(bf16[4,128,256]{2,1,0:T(8,128)(2,1)S(1)} %get-tuple-element.44), channel_id=1, source_target_pairs={{0,1},{1,0},{2,3},{3,2},{4,5},{5,4},{6,7},{7,6},{8,9},{9,8},{10,11... | collective-permute-start | bytes 786440 | tf_op jit(solution)/shard_map/ppermute | solution.py:331
  20.0 10.2 %collective-permute-start.8 = (bf16[4,128,256]{2,1,0:T(8,128)(2,1)S(1)}, bf16[4,128,256]{2,1,0:T(8,128)(2,1)S(1)}, u32[]{:S(2)}, u32[]{:S(2)}) collective-permute-start(bf16[4,128,256]{2,1,0:T(8,128)(2,1)S(1)} %get-tuple-element.45), channel_id=1, source_target_pairs={{1,2},{2,1},{3,4},{4,3},{5,6},{6,5},{9,10},{10,9},{11,12},{12,11},... | collective-permute-start | bytes 786440 | tf_op jit(solution)/shard_map/ppermute | solution.py:331
  24.2 7.3 %collective-permute-start.6 = (bf16[4,128,256]{2,1,0:T(8,128)(2,1)S(1)}, bf16[4,128,256]{2,1,0:T(8,128)(2,1)S(1)}, u32[]{:S(2)}, u32[]{:S(2)}) collective-permute-start(bf16[4,128,256]{2,1,0:T(8,128)(2,1)S(1)} %shard_map.70), channel_id=1, source_target_pairs={{0,1},{1,9},{2,3},{3,11},{4,5},{5,13},{6,7},{7,15},{8,16},{9,24},{... | collective-permute-start | bytes 786440 | tf_op jit(solution)/shard_map/ppermute | solution.py:331

commit v6 on v5

--- a/solution.py
+++ b/solution.py
@@ -249,18 +249,25 @@
     return partial[row] + spread_over(ALPHA * scales[row], topics) * product
 
 
-def second_send_body(
-    columns, lists, weights, extended_in, scales, partial, r0, r1, r2, r3, x_a, x_b, y_a, y_b, extended
-):
-    sends = lists.shape[2]
-    topics = x_a.shape[2]
+def corner_send_body(columns, lists, weights, extended_in, scales, partial, r0, r1, r2, r3, x_b, extended):
     arrivals((r1, r0, r3, r2), extended)
-    order = toward_x() + toward_y()
-    for number, out in ((1, x_b), (0, x_a), (3, y_b), (2, y_a)):
-        for i in range(sends):
-            row = lists[0, order[number], i]
-            value = finished(weights, extended, columns, scales, partial, row)
-            out[i] = (spread_over(scales[row], topics) * value).astype(jnp.bfloat16)
+    send(columns, lists, weights, extended, scales, partial, toward_x()[1], x_b)
+
+
+def send_body(columns, lists, weights, extended, scales, partial, out, *, number):
+    send(columns, lists, weights, extended, scales, partial, (toward_x() + toward_y())[number], out)
+
+
+def y_send_body(columns, lists, weights, extended, scales, partial, y_a, y_b):
+    for direction, out in zip(toward_y(), (y_a, y_b)):
+        send(columns, lists, weights, extended, scales, partial, direction, out)
+
+
+def send(columns, lists, weights, extended, scales, partial, direction, out):
+    for i in range(out.shape[0]):
+        row = lists[0, direction, i]
+        value = finished(weights, extended, columns, scales, partial, row)
+        out[i] = (spread_over(scales[row], out.shape[2]) * value).astype(jnp.bfloat16)
 
 
 def rest_body(columns, weights, extended, scales, partial, following, handed, *, unroll):
@@ -428,13 +435,19 @@
         )(columns, held, pinned(extended), scales, counts, *reused)
 
     partial = started(extended)
-    x_a, x_b, y_a, y_b, extended = call(
-        second_send_body,
-        (whole, whole, whole, whole, extended_shape),
-        (IN_VMEM,) * 5,
+    x_b, extended = call(
+        corner_send_body,
+        (whole, extended_shape),
+        (IN_VMEM,) * 2,
         (IN_SMEM,) * 2 + (IN_VMEM,) * 8,
-        aliases={3: 4},
+        aliases={3: 1},
     )(columns, lists, held, pinned(extended), scales, pinned(partial), *map(pinned, (x_b, x_a, y_b, y_a)))
+    x_a = call(functools.partial(send_body, number=0), whole, IN_VMEM, (IN_SMEM,) * 2 + (IN_VMEM,) * 4)(
+        columns, lists, held, pinned(extended), scales, pinned(partial)
+    )
+    y_a, y_b = call(y_send_body, (whole, whole), (IN_VMEM,) * 2, (IN_SMEM,) * 2 + (IN_VMEM,) * 4)(
+        columns, lists, held, pinned(extended), scales, pinned(partial)
+    )
     x_a = x_swap(x_a, 0)
     if by_corner():
         first_hop = hop(x_b, FIRST_HOP)

time: 34.6 us -> 34.1 us (0.986)
  waiting for transfers between devices: 6.54 us -> 5.73 us
    ppermute x9, waiting for transfers between devices: 6.54 us -> 5.73 us  [permuted(): lax.ppermute(value, ('gx', 'gy'), sorted(((a * inner + b, c * inner + d)...]
    pallas_call x1 -> x3, Pallas kernels: 0.96 us -> 1.24 us  [the longest x1 0.53 us: local(): call(y_send_body, (whole, whole), (IN_VMEM,) * 2, (IN_SMEM,) * 2 + (IN_VM...]
  transfers between devices with their start and end apart: 9 -> 9, of which waited for: 4 -> 4; matrix products, arithmetic and copies ran while one was open for 0% -> 0% of each run, Pallas kernels for 35% -> 39%
where the time goes in v6:
time: 34.1 us; the launch traced here: 33.6 us
  Pallas kernels  19.7 us (58%)
  starting transfers between devices  8.03 us (24%)
  waiting for transfers between devices  5.73 us (17%)
    ppermute x9, starting transfers between devices, permuted(): lax.ppermute(value, ('gx', 'gy'), sorted(((a * inner + b, c * inner + d)...  8.03 us
    ppermute x9, waiting for transfers between devices, permuted(): lax.ppermute(value, ('gx', 'gy'), sorted(((a * inner + b, c * inner + d)...  5.73 us
    pallas_call x1, Pallas kernels, local(): call(functools.partial(degree_body, chunk=4), (held_shape, extended_shape...  5.21 us
    pallas_call x2, Pallas kernels, started(): call(functools.partial(near_body, unroll=16), partial_shape, IN_VMEM, (IN...  5.21 us
    pallas_call x1, Pallas kernels, local(): call(first_send_body, (whole, whole, held_shape, extended_shape, scale_sh...  3.35 us
    pallas_call x1, Pallas kernels, local(): call(functools.partial(last_body, unroll=16), (jax.ShapeDtypeStruct((bloc...  2.87 us
    pallas_call x1, Pallas kernels, local(): call(functools.partial(rest_body, unroll=16), (extended_shape, partial_sh...  1.77 us
  transfers between devices with their start and end apart: 9, of which 4 were waited for; matrix products, arithmetic and copies ran while one was open for 0% of the time, Pallas kernels for 39%

profile of v6, /device:TPU:4, one launch (start us, length us, event | category | flops | bytes accessed | tf_op | source)
XLA Modules:
  0.0 33.6 jit_solution(17285140038125936745)
XLA Ops:
  0.0 0.0 copy-start
  0.0 0.0 copy-start.1
  0.0 3.4 %shard_map.64 = (bf16[4,128,256]{2,1,0:T(8,128)(2,1)S(1)}, bf16[4,128,256]{2,1,0:T(8,128)(2,1)S(1)}, bf16[32,12,128,128]{3,2,1,0:T(8,128)(2,1)S(1)}, bf16[48,128...) custom-call(s32[12,32]{1,0:T(8,128)} %bitcast.9, ...), custom_call_target="tpu_custom_call" | custom-call | flops 1 | bytes 1 | tf_op jit(solution)/shard_map/pallas_call | solution.py:393
  3.4 1.3 %collective-permute-start = (bf16[4,128,256]{2,1,0:T(8,128)(2,1)S(1)}, bf16[4,128,256]{2,1,0:T(8,128)(2,1)S(1)}, u32[]{:S(2)}, u32[]{:S(2)}) collective-permute-start(bf16[4,128,256]{2,1,0:T(8,128)(2,1)S(1)} %get-tuple-element.34), channel_id=1, source_target_pairs={{0,1},{1,0},{2,3},{3,2},{4,5},{5,4},{6,7},{7,6},{8,16},{9,17},{10,... | collective-permute-start | bytes 786440 | tf_op jit(solution)/shard_map/ppermute | solution.py:338
  4.7 0.1 collective-permute-start.1
  4.9 0.0 copy-done
  4.9 0.0 copy-done.1
  4.9 5.2 %shard_map.65 = (bf16[32,12,128,128]{3,2,1,0:T(8,128)(2,1)S(1)}, bf16[48,128,256]{2,1,0:T(8,128)(2,1)S(1)}, f32[32,128,128]{2,1,0:T(8,128)S(1)}, bf16[32,128,256...) custom-call(s32[1,4,4]{2,1,0:T(4,128)S(4)} %get-tuple-element.26.lis, ...), custom_call_target="tpu_custom_call", output_to_operand_aliasing={{0}: (5, {}), {1}: (6, {}), {2}: (7, {})} | custom-call | flops 1 | bytes 1 | tf_op jit(solution)/shard_map/pallas_call | solution.py:411
  10.1 1.8 %collective-permute-start.2 = (bf16[4,128,256]{2,1,0:T(8,128)(2,1)S(1)}, bf16[4,128,256]{2,1,0:T(8,128)(2,1)S(1)}, u32[]{:S(2)}, u32[]{:S(2)}) collective-permute-start(bf16[4,128,256]{2,1,0:T(8,128)(2,1)S(1)} %get-tuple-element.36), channel_id=1, source_target_pairs={{0,8},{1,2},{2,1},{3,4},{4,3},{5,6},{6,5},{7,15},{8,24},{9,10},{10... | collective-permute-start | bytes 786440 | tf_op jit(solution)/shard_map/ppermute | solution.py:338
  11.9 0.0 collective-permute-start.3
  11.9 2.6 %shard_map.66.partial = f32[32,128,256]{2,1,0:T(8,128)S(1)} custom-call(s32[12,32]{1,0:T(8,128)S(4)} %get-tuple-element.25.columns, bf16[32,12,128,128]{3,2,1,0:T(8,128)(2,1)S(1)} %get-tuple-element.30.weights, bf16[48,128,256]{2,1,0:T(8,128)(2,1)S(1)} %get-tuple-element.31.extended.extended_in, f32[32,128,128]{2,1,0:T(8,128)S(1)} %get-tuple-element.32.scales, ...), custom_call_target="tpu_custom_call" | custom-call | flops 1 | bytes 1 | tf_op jit(solution)/shard_map/pallas_call | solution.py:429
  14.5 0.0 collective-permute-done.r0
  14.5 1.2 %collective-permute-done.1.r1 = bf16[4,128,256]{2,1,0:T(8,128)(2,1)S(1)} collective-permute-done((bf16[4,128,256]{2,1,0:T(8,128)(2,1)S(1)}, bf16[4,128,256]{2,1,0:T(8,128)(2,1)S(1)}, u32[]{:S(2)}, u32[]{:S(2)}) %collective-permute-start.1) | collective-permute-done | bytes 262176 | tf_op jit(solution)/shard_map/ppermute | solution.py:338
  15.7 0.8 %collective-permute-done.2.r2 = bf16[4,128,256]{2,1,0:T(8,128)(2,1)S(1)} collective-permute-done((bf16[4,128,256]{2,1,0:T(8,128)(2,1)S(1)}, bf16[4,128,256]{2,1,0:T(8,128)(2,1)S(1)}, u32[]{:S(2)}, u32[]{:S(2)}) %collective-permute-start.2) | collective-permute-done | bytes 262176 | tf_op jit(solution)/shard_map/ppermute | solution.py:338
  16.5 0.0 collective-permute-done.3.r3
  16.5 0.4 %shard_map.67 = (bf16[4,128,256]{2,1,0:T(8,128)(2,1)S(1)}, bf16[48,128,256]{2,1,0:T(8,128)(2,1)S(1)}) custom-call(s32[12,32]{1,0:T(8,128)S(4)} %get-tuple-element.25.columns, s32[1,4,4]{2,1,0:T(4,128)S(4)} %get-tuple-element.26.lists, bf16[32,12,128,128]{3,2,1,0:T(8,128)(2,1)S(1)} %get-tuple-element.30.weights, ...), custom_call_target="tpu_custom_call", output_to_operand_aliasing={{1}: (3, {})} | custom-call | flops 1 | bytes 1 | tf_op jit(solution)/shard_map/pallas_call | solution.py:438
  16.9 0.2 collective-permute-start.5
  17.1 0.3 shard_map.70
  17.4 0.5 %shard_map.72 = (bf16[4,128,256]{2,1,0:T(8,128)(2,1)S(1)}, bf16[4,128,256]{2,1,0:T(8,128)(2,1)S(1)}) custom-call(s32[12,32]{1,0:T(8,128)S(4)} %get-tuple-element.25.columns, s32[1,4,4]{2,1,0:T(4,128)S(4)} %get-tuple-element.26.lists, bf16[32,12,128,128]{3,2,1,0:T(8,128)(2,1)S(1)} %get-tuple-element.30.weights, ...), custom_call_target="tpu_custom_call" | custom-call | flops 1 | bytes 1 | tf_op jit(solution)/shard_map/pallas_call | solution.py:448
  17.9 2.2 %collective-permute-start.4 = (bf16[4,128,256]{2,1,0:T(8,128)(2,1)S(1)}, bf16[4,128,256]{2,1,0:T(8,128)(2,1)S(1)}, u32[]{:S(2)}, u32[]{:S(2)}) collective-permute-start(bf16[4,128,256]{2,1,0:T(8,128)(2,1)S(1)} %shard_map.70), channel_id=1, source_target_pairs={{0,8},{1,9},{2,10},{3,11},{4,12},{5,13},{6,14},{7,15},{8,0},{9,1},... | collective-permute-start | bytes 786440 | tf_op jit(solution)/shard_map/ppermute | solution.py:338
  20.1 0.0 collective-permute-start.7
  20.1 0.7 %collective-permute-start.8 = (bf16[4,128,256]{2,1,0:T(8,128)(2,1)S(1)}, bf16[4,128,256]{2,1,0:T(8,128)(2,1)S(1)}, u32[]{:S(2)}, u32[]{:S(2)}) collective-permute-start(bf16[4,128,256]{2,1,0:T(8,128)(2,1)S(1)} %get-tuple-element.43), channel_id=1, source_target_pairs={{1,2},{2,1},{3,4},{4,3},{5,6},{6,5},{9,10},{10,9},{11,12},{12,11},... | collective-permute-start | bytes 786440 | tf_op jit(solution)/shard_map/ppermute | solution.py:338
  20.8 2.6 %collective-permute-done.5.first_hop = bf16[4,128,256]{2,1,0:T(8,128)(2,1)S(1)} collective-permute-done((bf16[4,128,256]{2,1,0:T(8,128)(2,1)S(1)}, bf16[4,128,256]{2,1,0:T(8,128)(2,1)S(1)}, u32[]{:S(2)}, u32[]{:S(2)}) %collective-permute-start.5) | collective-permute-done | bytes 262176 | tf_op jit(solution)/shard_map/ppermute | solution.py:338
  23.4 1.7 %collective-permute-start.6 = (bf16[4,128,256]{2,1,0:T(8,128)(2,1)S(1)}, bf16[4,128,256]{2,1,0:T(8,128)(2,1)S(1)}, u32[]{:S(2)}, u32[]{:S(2)}) collective-permute-start(bf16[4,128,256]{2,1,0:T(8,128)(2,1)S(1)} %shard_map.71), channel_id=1, source_target_pairs={{0,1},{1,9},{2,3},{3,11},{4,5},{5,13},{6,7},{7,15},{8,16},{9,24},{... | collective-permute-start | bytes 786440 | tf_op jit(solution)/shard_map/ppermute | solution.py:338
  25.1 1.8 %shard_map.68 = (bf16[48,128,256]{2,1,0:T(8,128)(2,1)S(1)}, f32[32,128,256]{2,1,0:T(8,128)S(1)}) custom-call(s32[12,32]{1,0:T(8,128)S(4)} %get-tuple-element.25.columns, bf16[32,12,128,128]{3,2,1,0:T(8,128)(2,1)S(1)} %get-tuple-element.30.weights, bf16[48,128,256]{2,1,0:T(8,128)(2,1)S(1)} %get-tuple-element.38.extended.rest_0_, ...), custom_call_target="tpu_custom_call", output_to_operand_aliasing={{1}: (4, {})} | custom-call | flops 1 | bytes 1 | tf_op jit(solution)/shard_map/pallas_call | solution.py:460
  26.9 2.6 %shard_map.69.partial = f32[32,128,256]{2,1,0:T(8,128)S(1)} custom-call(s32[12,32]{1,0:T(8,128)S(4)} %get-tuple-element.25.columns, bf16[32,12,128,128]{3,2,1,0:T(8,128)(2,1)S(1)} %get-tuple-element.30.weights, bf16[48,128,256]{2,1,0:T(8,128)(2,1)S(1)} %get-tuple-element.39.extended.extended_in, ...), custom_call_target="tpu_custom_call", output_to_operand_aliasing={{}: (6, {})} | custom-call | flops 1 | bytes 1 | tf_op jit(solution)/shard_map/pallas_call | solution.py:429
  29.5 0.0 collective-permute-done.4.r0
  29.5 0.0 collective-permute-done.7.r2
  29.5 0.0 collective-permute-done.8.r3
  29.5 1.2 %collective-permute-done.6.r1 = bf16[4,128,256]{2,1,0:T(8,128)(2,1)S(1)} collective-permute-done((bf16[4,128,256]{2,1,0:T(8,128)(2,1)S(1)}, bf16[4,128,256]{2,1,0:T(8,128)(2,1)S(1)}, u32[]{:S(2)}, u32[]{:S(2)}) %collective-permute-start.6) | collective-permute-done | bytes 262176 | tf_op jit(solution)/shard_map/ppermute | solution.py:338
  30.7 2.9 %shard_map.73 = (f32[32,128,256]{2,1,0:T(8,128)}, bf16[48,128,256]{2,1,0:T(8,128)(2,1)S(1)}) custom-call(s32[12,32]{1,0:T(8,128)S(4)} %get-tuple-element.25.columns, bf16[32,12,128,128]{3,2,1,0:T(8,128)(2,1)S(1)} %get-tuple-element.30.weights, bf16[48,128,256]{2,1,0:T(8,128)(2,1)S(1)} %get-tuple-element.39.extended.extended_in, ...), custom_call_target="tpu_custom_call", output_to_operand_aliasing={{1}: (2, {})} | custom-call | flops 1 | bytes 1 | tf_op jit(solution)/shard_map/pallas_call | solution.py:469
  (1 shorter events, 0.0 us)
Async XLA Ops:
  0.0 4.9 %copy-start = (s32[256]{0:T(256)S(1)}, s32[256]{0:T(256)}, u32[]{:S(2)}) copy-start(s32[256]{0:T(256)} %param.10) | copy-start | bytes 3076
  0.0 4.9 %copy-start.1 = (s32[256]{0:T(256)S(1)}, s32[256]{0:T(256)}, u32[]{:S(2)}) copy-start(s32[256]{0:T(256)} %param.11) | copy-start | bytes 3076
  3.4 11.2 %collective-permute-start = (bf16[4,128,256]{2,1,0:T(8,128)(2,1)S(1)}, bf16[4,128,256]{2,1,0:T(8,128)(2,1)S(1)}, u32[]{:S(2)}, u32[]{:S(2)}) collective-permute-start(bf16[4,128,256]{2,1,0:T(8,128)(2,1)S(1)} %get-tuple-element.34), channel_id=1, source_target_pairs={{0,1},{1,0},{2,3},{3,2},{4,5},{5,4},{6,7},{7,6},{8,16},{9,17},{10,... | collective-permute-start | bytes 786440 | tf_op jit(solution)/shard_map/ppermute | solution.py:338
  4.7 11.0 %collective-permute-start.1 = (bf16[4,128,256]{2,1,0:T(8,128)(2,1)S(1)}, bf16[4,128,256]{2,1,0:T(8,128)(2,1)S(1)}, u32[]{:S(2)}, u32[]{:S(2)}) collective-permute-start(bf16[4,128,256]{2,1,0:T(8,128)(2,1)S(1)} %get-tuple-element.35), channel_id=1, source_target_pairs={{0,8},{1,9},{2,10},{3,11},{4,12},{5,13},{6,14},{7,15},{8,0},{9,1},... | collective-permute-start | bytes 786440 | tf_op jit(solution)/shard_map/ppermute | solution.py:338
  10.1 6.4 %collective-permute-start.2 = (bf16[4,128,256]{2,1,0:T(8,128)(2,1)S(1)}, bf16[4,128,256]{2,1,0:T(8,128)(2,1)S(1)}, u32[]{:S(2)}, u32[]{:S(2)}) collective-permute-start(bf16[4,128,256]{2,1,0:T(8,128)(2,1)S(1)} %get-tuple-element.36), channel_id=1, source_target_pairs={{0,8},{1,2},{2,1},{3,4},{4,3},{5,6},{6,5},{7,15},{8,24},{9,10},{10... | collective-permute-start | bytes 786440 | tf_op jit(solution)/shard_map/ppermute | solution.py:338
  11.9 4.6 %collective-permute-start.3 = (bf16[4,128,256]{2,1,0:T(8,128)(2,1)S(1)}, bf16[4,128,256]{2,1,0:T(8,128)(2,1)S(1)}, u32[]{:S(2)}, u32[]{:S(2)}) collective-permute-start(bf16[4,128,256]{2,1,0:T(8,128)(2,1)S(1)} %get-tuple-element.37), channel_id=1, source_target_pairs={{0,1},{1,0},{2,3},{3,2},{4,5},{5,4},{6,7},{7,6},{8,9},{9,8},{10,11... | collective-permute-start | bytes 786440 | tf_op jit(solution)/shard_map/ppermute | solution.py:338
  16.9 6.4 %collective-permute-start.5 = (bf16[4,128,256]{2,1,0:T(8,128)(2,1)S(1)}, bf16[4,128,256]{2,1,0:T(8,128)(2,1)S(1)}, u32[]{:S(2)}, u32[]{:S(2)}) collective-permute-start(bf16[4,128,256]{2,1,0:T(8,128)(2,1)S(1)} %get-tuple-element.41.direct), channel_id=1, source_target_pairs={{0,16},{1,0},{2,18},{3,2},{4,20},{5,4},{6,22},{7,6},{8,9},{9,25},{... | collective-permute-start | bytes 786440 | tf_op jit(solution)/shard_map/ppermute | solution.py:338
  17.9 11.6 %collective-permute-start.4 = (bf16[4,128,256]{2,1,0:T(8,128)(2,1)S(1)}, bf16[4,128,256]{2,1,0:T(8,128)(2,1)S(1)}, u32[]{:S(2)}, u32[]{:S(2)}) collective-permute-start(bf16[4,128,256]{2,1,0:T(8,128)(2,1)S(1)} %shard_map.70), channel_id=1, source_target_pairs={{0,8},{1,9},{2,10},{3,11},{4,12},{5,13},{6,14},{7,15},{8,0},{9,1},... | collective-permute-start | bytes 786440 | tf_op jit(solution)/shard_map/ppermute | solution.py:338
  20.1 9.4 %collective-permute-start.7 = (bf16[4,128,256]{2,1,0:T(8,128)(2,1)S(1)}, bf16[4,128,256]{2,1,0:T(8,128)(2,1)S(1)}, u32[]{:S(2)}, u32[]{:S(2)}) collective-permute-start(bf16[4,128,256]{2,1,0:T(8,128)(2,1)S(1)} %get-tuple-element.42), channel_id=1, source_target_pairs={{0,1},{1,0},{2,3},{3,2},{4,5},{5,4},{6,7},{7,6},{8,9},{9,8},{10,11... | collective-permute-start | bytes 786440 | tf_op jit(solution)/shard_map/ppermute | solution.py:338
  20.1 9.4 %collective-permute-start.8 = (bf16[4,128,256]{2,1,0:T(8,128)(2,1)S(1)}, bf16[4,128,256]{2,1,0:T(8,128)(2,1)S(1)}, u32[]{:S(2)}, u32[]{:S(2)}) collective-permute-start(bf16[4,128,256]{2,1,0:T(8,128)(2,1)S(1)} %get-tuple-element.43), channel_id=1, source_target_pairs={{1,2},{2,1},{3,4},{4,3},{5,6},{6,5},{9,10},{10,9},{11,12},{12,11},... | collective-permute-start | bytes 786440 | tf_op jit(solution)/shard_map/ppermute | solution.py:338
  23.4 7.3 %collective-permute-start.6 = (bf16[4,128,256]{2,1,0:T(8,128)(2,1)S(1)}, bf16[4,128,256]{2,1,0:T(8,128)(2,1)S(1)}, u32[]{:S(2)}, u32[]{:S(2)}) collective-permute-start(bf16[4,128,256]{2,1,0:T(8,128)(2,1)S(1)} %shard_map.71), channel_id=1, source_target_pairs={{0,1},{1,9},{2,3},{3,11},{4,5},{5,13},{6,7},{7,15},{8,16},{9,24},{... | collective-permute-start | bytes 786440 | tf_op jit(solution)/shard_map/ppermute | solution.py:338

commit v7 on v6

--- a/solution.py
+++ b/solution.py
@@ -258,7 +258,7 @@
     send(columns, lists, weights, extended, scales, partial, (toward_x() + toward_y())[number], out)
 
 
-def y_send_body(columns, lists, weights, extended, scales, partial, y_a, y_b):
+def y_send_body(columns, lists, weights, extended, scales, partial, behind, y_a, y_b):
     for direction, out in zip(toward_y(), (y_a, y_b)):
         send(columns, lists, weights, extended, scales, partial, direction, out)
 
@@ -445,8 +445,8 @@
     x_a = call(functools.partial(send_body, number=0), whole, IN_VMEM, (IN_SMEM,) * 2 + (IN_VMEM,) * 4)(
         columns, lists, held, pinned(extended), scales, pinned(partial)
     )
-    y_a, y_b = call(y_send_body, (whole, whole), (IN_VMEM,) * 2, (IN_SMEM,) * 2 + (IN_VMEM,) * 4)(
-        columns, lists, held, pinned(extended), scales, pinned(partial)
+    y_a, y_b = call(y_send_body, (whole, whole), (IN_VMEM,) * 2, (IN_SMEM,) * 2 + (IN_VMEM,) * 5)(
+        columns, lists, held, pinned(extended), scales, pinned(partial), pinned(x_a)
     )
     x_a = x_swap(x_a, 0)
     if by_corner():
@@ -467,7 +467,7 @@
     partial = started(following, pinned(extended), pinned(partial))
 
     out, _ = call(
-        functools.partial(last_body, unroll=16),
+        functools.partial(last_body, unroll=32),
         (jax.ShapeDtypeStruct((blocks_dev, block_size, topics), jnp.float32), extended_shape),
         (ANYWHERE, IN_VMEM),
         (IN_SMEM,) + (IN_VMEM,) * 8,

time: 34.1 us -> 33.9 us (level)
  no operation moved by 1% of the time
where the time goes in v7:
time: 33.9 us; the launch traced here: 33.5 us
  Pallas kernels  19.5 us (58%)
  starting transfers between devices  8.11 us (24%)
  waiting for transfers between devices  5.82 us (17%)
    ppermute x9, starting transfers between devices, permuted(): lax.ppermute(value, ('gx', 'gy'), sorted(((a * inner + b, c * inner + d)...  8.11 us
    ppermute x9, waiting for transfers between devices, permuted(): lax.ppermute(value, ('gx', 'gy'), sorted(((a * inner + b, c * inner + d)...  5.82 us
    pallas_call x1, Pallas kernels, local(): call(functools.partial(degree_body, chunk=4), (held_shape, extended_shape...  5.22 us
    pallas_call x2, Pallas kernels, started(): call(functools.partial(near_body, unroll=16), partial_shape, IN_VMEM, (IN...  5.22 us
    pallas_call x1, Pallas kernels, local(): call(first_send_body, (whole, whole, held_shape, extended_shape, scale_sh...  3.2 us
    pallas_call x1, Pallas kernels, local(): call(functools.partial(last_body, unroll=32), (jax.ShapeDtypeStruct((bloc...  2.79 us
    pallas_call x1, Pallas kernels, local(): call(functools.partial(rest_body, unroll=16), (extended_shape, partial_sh...  1.78 us
  transfers between devices with their start and end apart: 9, of which 4 were waited for; matrix products, arithmetic and copies ran while one was open for 0% of the time, Pallas kernels for 39%

profile of v7, /device:TPU:4, one launch (start us, length us, event | category | flops | bytes accessed | tf_op | source)
XLA Modules:
  0.0 33.5 jit_solution(15477985391250958662)
XLA Ops:
  0.0 0.0 copy-start
  0.0 0.0 copy-start.1
  0.0 3.2 %shard_map.64 = (bf16[4,128,256]{2,1,0:T(8,128)(2,1)S(1)}, bf16[4,128,256]{2,1,0:T(8,128)(2,1)S(1)}, bf16[32,12,128,128]{3,2,1,0:T(8,128)(2,1)S(1)}, bf16[48,128...) custom-call(s32[12,32]{1,0:T(8,128)} %bitcast.9, ...), custom_call_target="tpu_custom_call" | custom-call | flops 1 | bytes 1 | tf_op jit(solution)/shard_map/pallas_call | solution.py:393
  3.2 1.5 %collective-permute-start = (bf16[4,128,256]{2,1,0:T(8,128)(2,1)S(1)}, bf16[4,128,256]{2,1,0:T(8,128)(2,1)S(1)}, u32[]{:S(2)}, u32[]{:S(2)}) collective-permute-start(bf16[4,128,256]{2,1,0:T(8,128)(2,1)S(1)} %get-tuple-element.34), channel_id=1, source_target_pairs={{0,1},{1,0},{2,3},{3,2},{4,5},{5,4},{6,7},{7,6},{8,16},{9,17},{10,... | collective-permute-start | bytes 786440 | tf_op jit(solution)/shard_map/ppermute | solution.py:338
  4.7 0.1 collective-permute-start.1
  4.8 0.0 copy-done
  4.8 0.0 copy-done.1
  4.9 5.2 %shard_map.65 = (bf16[32,12,128,128]{3,2,1,0:T(8,128)(2,1)S(1)}, bf16[48,128,256]{2,1,0:T(8,128)(2,1)S(1)}, f32[32,128,128]{2,1,0:T(8,128)S(1)}, bf16[32,128,256...) custom-call(s32[1,4,4]{2,1,0:T(4,128)S(4)} %get-tuple-element.26.lis, ...), custom_call_target="tpu_custom_call", output_to_operand_aliasing={{0}: (5, {}), {1}: (6, {}), {2}: (7, {})} | custom-call | flops 1 | bytes 1 | tf_op jit(solution)/shard_map/pallas_call | solution.py:411
  10.1 1.9 %collective-permute-start.2 = (bf16[4,128,256]{2,1,0:T(8,128)(2,1)S(1)}, bf16[4,128,256]{2,1,0:T(8,128)(2,1)S(1)}, u32[]{:S(2)}, u32[]{:S(2)}) collective-permute-start(bf16[4,128,256]{2,1,0:T(8,128)(2,1)S(1)} %get-tuple-element.36), channel_id=1, source_target_pairs={{0,8},{1,2},{2,1},{3,4},{4,3},{5,6},{6,5},{7,15},{8,24},{9,10},{10... | collective-permute-start | bytes 786440 | tf_op jit(solution)/shard_map/ppermute | solution.py:338
  12.0 0.1 collective-permute-start.3
  12.1 2.6 %shard_map.66.partial = f32[32,128,256]{2,1,0:T(8,128)S(1)} custom-call(s32[12,32]{1,0:T(8,128)S(4)} %get-tuple-element.25.columns, bf16[32,12,128,128]{3,2,1,0:T(8,128)(2,1)S(1)} %get-tuple-element.30.weights, bf16[48,128,256]{2,1,0:T(8,128)(2,1)S(1)} %get-tuple-element.31.extended.extended_in, f32[32,128,128]{2,1,0:T(8,128)S(1)} %get-tuple-element.32.scales, ...), custom_call_target="tpu_custom_call" | custom-call | flops 1 | bytes 1 | tf_op jit(solution)/shard_map/pallas_call | solution.py:429
  14.7 0.0 collective-permute-done.r0
  14.7 1.1 %collective-permute-done.1.r1 = bf16[4,128,256]{2,1,0:T(8,128)(2,1)S(1)} collective-permute-done((bf16[4,128,256]{2,1,0:T(8,128)(2,1)S(1)}, bf16[4,128,256]{2,1,0:T(8,128)(2,1)S(1)}, u32[]{:S(2)}, u32[]{:S(2)}) %collective-permute-start.1) | collective-permute-done | bytes 262176 | tf_op jit(solution)/shard_map/ppermute | solution.py:338
  15.9 0.6 %collective-permute-done.2.r2 = bf16[4,128,256]{2,1,0:T(8,128)(2,1)S(1)} collective-permute-done((bf16[4,128,256]{2,1,0:T(8,128)(2,1)S(1)}, bf16[4,128,256]{2,1,0:T(8,128)(2,1)S(1)}, u32[]{:S(2)}, u32[]{:S(2)}) %collective-permute-start.2) | collective-permute-done | bytes 262176 | tf_op jit(solution)/shard_map/ppermute | solution.py:338
  16.5 0.0 collective-permute-done.3.r3
  16.5 0.4 %shard_map.67 = (bf16[4,128,256]{2,1,0:T(8,128)(2,1)S(1)}, bf16[48,128,256]{2,1,0:T(8,128)(2,1)S(1)}) custom-call(s32[12,32]{1,0:T(8,128)S(4)} %get-tuple-element.25.columns, s32[1,4,4]{2,1,0:T(4,128)S(4)} %get-tuple-element.26.lists, bf16[32,12,128,128]{3,2,1,0:T(8,128)(2,1)S(1)} %get-tuple-element.30.weights, ...), custom_call_target="tpu_custom_call", output_to_operand_aliasing={{1}: (3, {})} | custom-call | flops 1 | bytes 1 | tf_op jit(solution)/shard_map/pallas_call | solution.py:438
  16.9 0.1 collective-permute-start.5
  17.0 0.3 %shard_map.70.behind = bf16[4,128,256]{2,1,0:T(8,128)(2,1)S(1)} custom-call(s32[12,32]{1,0:T(8,128)S(4)} %get-tuple-element.25.columns, s32[1,4,4]{2,1,0:T(4,128)S(4)} %get-tuple-element.26.lists, bf16[32,12,128,128]{3,2,1,0:T(8,128)(2,1)S(1)} %get-tuple-element.30.weights, bf16[48,128,256]{2,1,0:T(8,128)(2,1)S(1)} %get-tuple-element.38.extended.rest_0_, ...), custom_call_target="tpu_custom_call" | custom-call | flops 1 | bytes 1 | tf_op jit(solution)/shard_map/pallas_call | solution.py:445
  17.3 2.1 %collective-permute-start.4 = (bf16[4,128,256]{2,1,0:T(8,128)(2,1)S(1)}, bf16[4,128,256]{2,1,0:T(8,128)(2,1)S(1)}, u32[]{:S(2)}, u32[]{:S(2)}) collective-permute-start(bf16[4,128,256]{2,1,0:T(8,128)(2,1)S(1)} %shard_map.70.behind), channel_id=1, source_target_pairs={{0,8},{1,9},{2,10},{3,11},{4,12},{5,13},{6,14},{7,15},{8,0},{9,1},... | collective-permute-start | bytes 786440 | tf_op jit(solution)/shard_map/ppermute | solution.py:338
  19.4 0.5 %shard_map.72 = (bf16[4,128,256]{2,1,0:T(8,128)(2,1)S(1)}, bf16[4,128,256]{2,1,0:T(8,128)(2,1)S(1)}) custom-call(s32[12,32]{1,0:T(8,128)S(4)} %get-tuple-element.25.columns, s32[1,4,4]{2,1,0:T(4,128)S(4)} %get-tuple-element.26.lists, bf16[32,12,128,128]{3,2,1,0:T(8,128)(2,1)S(1)} %get-tuple-element.30.weights, ...), custom_call_target="tpu_custom_call" | custom-call | flops 1 | bytes 1 | tf_op jit(solution)/shard_map/pallas_call | solution.py:448
  19.9 0.1 collective-permute-start.7
  20.1 0.7 %collective-permute-start.8 = (bf16[4,128,256]{2,1,0:T(8,128)(2,1)S(1)}, bf16[4,128,256]{2,1,0:T(8,128)(2,1)S(1)}, u32[]{:S(2)}, u32[]{:S(2)}) collective-permute-start(bf16[4,128,256]{2,1,0:T(8,128)(2,1)S(1)} %get-tuple-element.43), channel_id=1, source_target_pairs={{1,2},{2,1},{3,4},{4,3},{5,6},{6,5},{9,10},{10,9},{11,12},{12,11},... | collective-permute-start | bytes 786440 | tf_op jit(solution)/shard_map/ppermute | solution.py:338
  20.7 2.7 %collective-permute-done.5.first_hop = bf16[4,128,256]{2,1,0:T(8,128)(2,1)S(1)} collective-permute-done((bf16[4,128,256]{2,1,0:T(8,128)(2,1)S(1)}, bf16[4,128,256]{2,1,0:T(8,128)(2,1)S(1)}, u32[]{:S(2)}, u32[]{:S(2)}) %collective-permute-start.5) | collective-permute-done | bytes 262176 | tf_op jit(solution)/shard_map/ppermute | solution.py:338
  23.4 1.5 %collective-permute-start.6 = (bf16[4,128,256]{2,1,0:T(8,128)(2,1)S(1)}, bf16[4,128,256]{2,1,0:T(8,128)(2,1)S(1)}, u32[]{:S(2)}, u32[]{:S(2)}) collective-permute-start(bf16[4,128,256]{2,1,0:T(8,128)(2,1)S(1)} %shard_map.71), channel_id=1, source_target_pairs={{0,1},{1,9},{2,3},{3,11},{4,5},{5,13},{6,7},{7,15},{8,16},{9,24},{... | collective-permute-start | bytes 786440 | tf_op jit(solution)/shard_map/ppermute | solution.py:338
  24.9 1.8 %shard_map.68 = (bf16[48,128,256]{2,1,0:T(8,128)(2,1)S(1)}, f32[32,128,256]{2,1,0:T(8,128)S(1)}) custom-call(s32[12,32]{1,0:T(8,128)S(4)} %get-tuple-element.25.columns, bf16[32,12,128,128]{3,2,1,0:T(8,128)(2,1)S(1)} %get-tuple-element.30.weights, bf16[48,128,256]{2,1,0:T(8,128)(2,1)S(1)} %get-tuple-element.38.extended.rest_0_, ...), custom_call_target="tpu_custom_call", output_to_operand_aliasing={{1}: (4, {})} | custom-call | flops 1 | bytes 1 | tf_op jit(solution)/shard_map/pallas_call | solution.py:460
  26.7 2.6 %shard_map.69.partial = f32[32,128,256]{2,1,0:T(8,128)S(1)} custom-call(s32[12,32]{1,0:T(8,128)S(4)} %get-tuple-element.25.columns, bf16[32,12,128,128]{3,2,1,0:T(8,128)(2,1)S(1)} %get-tuple-element.30.weights, bf16[48,128,256]{2,1,0:T(8,128)(2,1)S(1)} %get-tuple-element.39.extended.extended_in, ...), custom_call_target="tpu_custom_call", output_to_operand_aliasing={{}: (6, {})} | custom-call | flops 1 | bytes 1 | tf_op jit(solution)/shard_map/pallas_call | solution.py:429
  29.3 0.0 collective-permute-done.4.r0
  29.3 0.0 collective-permute-done.7.r2
  29.3 0.0 collective-permute-done.8.r3
  29.4 1.4 %collective-permute-done.6.r1 = bf16[4,128,256]{2,1,0:T(8,128)(2,1)S(1)} collective-permute-done((bf16[4,128,256]{2,1,0:T(8,128)(2,1)S(1)}, bf16[4,128,256]{2,1,0:T(8,128)(2,1)S(1)}, u32[]{:S(2)}, u32[]{:S(2)}) %collective-permute-start.6) | collective-permute-done | bytes 262176 | tf_op jit(solution)/shard_map/ppermute | solution.py:338
  30.7 2.8 %shard_map.73 = (f32[32,128,256]{2,1,0:T(8,128)}, bf16[48,128,256]{2,1,0:T(8,128)(2,1)S(1)}) custom-call(s32[12,32]{1,0:T(8,128)S(4)} %get-tuple-element.25.columns, bf16[32,12,128,128]{3,2,1,0:T(8,128)(2,1)S(1)} %get-tuple-element.30.weights, bf16[48,128,256]{2,1,0:T(8,128)(2,1)S(1)} %get-tuple-element.39.extended.extended_in, ...), custom_call_target="tpu_custom_call", output_to_operand_aliasing={{1}: (2, {})} | custom-call | flops 1 | bytes 1 | tf_op jit(solution)/shard_map/pallas_call | solution.py:469
  (1 shorter events, 0.0 us)
Async XLA Ops:
  0.0 4.8 %copy-start = (s32[256]{0:T(256)S(1)}, s32[256]{0:T(256)}, u32[]{:S(2)}) copy-start(s32[256]{0:T(256)} %param.10) | copy-start | bytes 3076
  0.0 4.8 %copy-start.1 = (s32[256]{0:T(256)S(1)}, s32[256]{0:T(256)}, u32[]{:S(2)}) copy-start(s32[256]{0:T(256)} %param.11) | copy-start | bytes 3076
  3.2 11.5 %collective-permute-start = (bf16[4,128,256]{2,1,0:T(8,128)(2,1)S(1)}, bf16[4,128,256]{2,1,0:T(8,128)(2,1)S(1)}, u32[]{:S(2)}, u32[]{:S(2)}) collective-permute-start(bf16[4,128,256]{2,1,0:T(8,128)(2,1)S(1)} %get-tuple-element.34), channel_id=1, source_target_pairs={{0,1},{1,0},{2,3},{3,2},{4,5},{5,4},{6,7},{7,6},{8,16},{9,17},{10,... | collective-permute-start | bytes 786440 | tf_op jit(solution)/shard_map/ppermute | solution.py:338
  4.7 11.2 %collective-permute-start.1 = (bf16[4,128,256]{2,1,0:T(8,128)(2,1)S(1)}, bf16[4,128,256]{2,1,0:T(8,128)(2,1)S(1)}, u32[]{:S(2)}, u32[]{:S(2)}) collective-permute-start(bf16[4,128,256]{2,1,0:T(8,128)(2,1)S(1)} %get-tuple-element.35), channel_id=1, source_target_pairs={{0,8},{1,9},{2,10},{3,11},{4,12},{5,13},{6,14},{7,15},{8,0},{9,1},... | collective-permute-start | bytes 786440 | tf_op jit(solution)/shard_map/ppermute | solution.py:338
  10.1 6.4 %collective-permute-start.2 = (bf16[4,128,256]{2,1,0:T(8,128)(2,1)S(1)}, bf16[4,128,256]{2,1,0:T(8,128)(2,1)S(1)}, u32[]{:S(2)}, u32[]{:S(2)}) collective-permute-start(bf16[4,128,256]{2,1,0:T(8,128)(2,1)S(1)} %get-tuple-element.36), channel_id=1, source_target_pairs={{0,8},{1,2},{2,1},{3,4},{4,3},{5,6},{6,5},{7,15},{8,24},{9,10},{10... | collective-permute-start | bytes 786440 | tf_op jit(solution)/shard_map/ppermute | solution.py:338
  12.0 4.5 %collective-permute-start.3 = (bf16[4,128,256]{2,1,0:T(8,128)(2,1)S(1)}, bf16[4,128,256]{2,1,0:T(8,128)(2,1)S(1)}, u32[]{:S(2)}, u32[]{:S(2)}) collective-permute-start(bf16[4,128,256]{2,1,0:T(8,128)(2,1)S(1)} %get-tuple-element.37), channel_id=1, source_target_pairs={{0,1},{1,0},{2,3},{3,2},{4,5},{5,4},{6,7},{7,6},{8,9},{9,8},{10,11... | collective-permute-start | bytes 786440 | tf_op jit(solution)/shard_map/ppermute | solution.py:338
  16.9 6.5 %collective-permute-start.5 = (bf16[4,128,256]{2,1,0:T(8,128)(2,1)S(1)}, bf16[4,128,256]{2,1,0:T(8,128)(2,1)S(1)}, u32[]{:S(2)}, u32[]{:S(2)}) collective-permute-start(bf16[4,128,256]{2,1,0:T(8,128)(2,1)S(1)} %get-tuple-element.41.direct), channel_id=1, source_target_pairs={{0,16},{1,0},{2,18},{3,2},{4,20},{5,4},{6,22},{7,6},{8,9},{9,25},{... | collective-permute-start | bytes 786440 | tf_op jit(solution)/shard_map/ppermute | solution.py:338
  17.3 12.0 %collective-permute-start.4 = (bf16[4,128,256]{2,1,0:T(8,128)(2,1)S(1)}, bf16[4,128,256]{2,1,0:T(8,128)(2,1)S(1)}, u32[]{:S(2)}, u32[]{:S(2)}) collective-permute-start(bf16[4,128,256]{2,1,0:T(8,128)(2,1)S(1)} %shard_map.70.behind), channel_id=1, source_target_pairs={{0,8},{1,9},{2,10},{3,11},{4,12},{5,13},{6,14},{7,15},{8,0},{9,1},... | collective-permute-start | bytes 786440 | tf_op jit(solution)/shard_map/ppermute | solution.py:338
  19.9 9.4 %collective-permute-start.7 = (bf16[4,128,256]{2,1,0:T(8,128)(2,1)S(1)}, bf16[4,128,256]{2,1,0:T(8,128)(2,1)S(1)}, u32[]{:S(2)}, u32[]{:S(2)}) collective-permute-start(bf16[4,128,256]{2,1,0:T(8,128)(2,1)S(1)} %get-tuple-element.42), channel_id=1, source_target_pairs={{0,1},{1,0},{2,3},{3,2},{4,5},{5,4},{6,7},{7,6},{8,9},{9,8},{10,11... | collective-permute-start | bytes 786440 | tf_op jit(solution)/shard_map/ppermute | solution.py:338
  20.1 9.3 %collective-permute-start.8 = (bf16[4,128,256]{2,1,0:T(8,128)(2,1)S(1)}, bf16[4,128,256]{2,1,0:T(8,128)(2,1)S(1)}, u32[]{:S(2)}, u32[]{:S(2)}) collective-permute-start(bf16[4,128,256]{2,1,0:T(8,128)(2,1)S(1)} %get-tuple-element.43), channel_id=1, source_target_pairs={{1,2},{2,1},{3,4},{4,3},{5,6},{6,5},{9,10},{10,9},{11,12},{12,11},... | collective-permute-start | bytes 786440 | tf_op jit(solution)/shard_map/ppermute | solution.py:338
  23.4 7.3 %collective-permute-start.6 = (bf16[4,128,256]{2,1,0:T(8,128)(2,1)S(1)}, bf16[4,128,256]{2,1,0:T(8,128)(2,1)S(1)}, u32[]{:S(2)}, u32[]{:S(2)}) collective-permute-start(bf16[4,128,256]{2,1,0:T(8,128)(2,1)S(1)} %shard_map.71), channel_id=1, source_target_pairs={{0,1},{1,9},{2,3},{3,11},{4,5},{5,13},{6,7},{7,15},{8,16},{9,24},{... | collective-permute-start | bytes 786440 | tf_op jit(solution)/shard_map/ppermute | solution.py:338

commit v8 on v7

--- a/solution.py
+++ b/solution.py
@@ -13,7 +13,7 @@
 GAIN = 1.0 / (1.0 - 0.99)
 SEED_WEIGHT = (1.0 - ALPHA) * GAIN
 
-EARLY = 4
+EARLY = 2
 LOCAL = 8
 VMEM = pltpu.VMEM
 IN_VMEM = pl.BlockSpec(memory_space=pltpu.VMEM)

time: 33.9 us -> 34 us (level)
    pallas_call x1, Pallas kernels: 5.22 us -> 5.62 us  [local(): call(functools.partial(degree_body, chunk=4), (held_shape, extended_shape...]
  transfers between devices with their start and end apart: 9 -> 9, of which waited for: 4 -> 4; matrix products, arithmetic and copies ran while one was open for 0% -> 0% of each run, Pallas kernels for 39% -> 40%
where the time goes in v8:
time: 34 us; the launch traced here: 33.9 us
  Pallas kernels  19.7 us (58%)
  starting transfers between devices  8.28 us (24%)
  waiting for transfers between devices  5.69 us (17%)
    ppermute x9, starting transfers between devices, permuted(): lax.ppermute(value, ('gx', 'gy'), sorted(((a * inner + b, c * inner + d)...  8.28 us
    ppermute x9, waiting for transfers between devices, permuted(): lax.ppermute(value, ('gx', 'gy'), sorted(((a * inner + b, c * inner + d)...  5.69 us
    pallas_call x1, Pallas kernels, local(): call(functools.partial(degree_body, chunk=4), (held_shape, extended_shape...  5.62 us
    pallas_call x2, Pallas kernels, started(): call(functools.partial(near_body, unroll=16), partial_shape, IN_VMEM, (IN...  5.21 us
    pallas_call x1, Pallas kernels, local(): call(first_send_body, (whole, whole, held_shape, extended_shape, scale_sh...  3.08 us
    pallas_call x1, Pallas kernels, local(): call(functools.partial(last_body, unroll=32), (jax.ShapeDtypeStruct((bloc...  2.79 us
    pallas_call x1, Pallas kernels, local(): call(functools.partial(rest_body, unroll=16), (extended_shape, partial_sh...  1.78 us
  transfers between devices with their start and end apart: 9, of which 4 were waited for; matrix products, arithmetic and copies ran while one was open for 0% of the time, Pallas kernels for 40%

profile of v8, /device:TPU:4, one launch (start us, length us, event | category | flops | bytes accessed | tf_op | source)
XLA Modules:
  0.0 33.9 jit_solution(72561303991600433)
XLA Ops:
  0.0 0.0 copy-start
  0.0 0.0 copy-start.1
  0.0 3.1 %shard_map.64 = (bf16[4,128,256]{2,1,0:T(8,128)(2,1)S(1)}, bf16[4,128,256]{2,1,0:T(8,128)(2,1)S(1)}, bf16[32,12,128,128]{3,2,1,0:T(8,128)(2,1)S(1)}, bf16[48,128...) custom-call(s32[12,32]{1,0:T(8,128)} %bitcast.9, ...), custom_call_target="tpu_custom_call" | custom-call | flops 1 | bytes 1 | tf_op jit(solution)/shard_map/pallas_call | solution.py:393
  3.1 1.7 %collective-permute-start = (bf16[4,128,256]{2,1,0:T(8,128)(2,1)S(1)}, bf16[4,128,256]{2,1,0:T(8,128)(2,1)S(1)}, u32[]{:S(2)}, u32[]{:S(2)}) collective-permute-start(bf16[4,128,256]{2,1,0:T(8,128)(2,1)S(1)} %get-tuple-element.34), channel_id=1, source_target_pairs={{0,1},{1,0},{2,3},{3,2},{4,5},{5,4},{6,7},{7,6},{8,16},{9,17},{10,... | collective-permute-start | bytes 786440 | tf_op jit(solution)/shard_map/ppermute | solution.py:338
  4.8 0.0 collective-permute-start.1
  4.8 0.0 copy-done
  4.8 0.0 copy-done.1
  4.8 5.6 %shard_map.65 = (bf16[32,12,128,128]{3,2,1,0:T(8,128)(2,1)S(1)}, bf16[48,128,256]{2,1,0:T(8,128)(2,1)S(1)}, f32[32,128,128]{2,1,0:T(8,128)S(1)}, bf16[32,128,256...) custom-call(s32[1,4,4]{2,1,0:T(4,128)S(4)} %get-tuple-element.26.lis, ...), custom_call_target="tpu_custom_call", output_to_operand_aliasing={{0}: (5, {}), {1}: (6, {}), {2}: (7, {})} | custom-call | flops 1 | bytes 1 | tf_op jit(solution)/shard_map/pallas_call | solution.py:411
  10.4 2.1 %collective-permute-start.2 = (bf16[4,128,256]{2,1,0:T(8,128)(2,1)S(1)}, bf16[4,128,256]{2,1,0:T(8,128)(2,1)S(1)}, u32[]{:S(2)}, u32[]{:S(2)}) collective-permute-start(bf16[4,128,256]{2,1,0:T(8,128)(2,1)S(1)} %get-tuple-element.36), channel_id=1, source_target_pairs={{0,8},{1,2},{2,1},{3,4},{4,3},{5,6},{6,5},{7,15},{8,24},{9,10},{10... | collective-permute-start | bytes 786440 | tf_op jit(solution)/shard_map/ppermute | solution.py:338
  12.5 0.0 collective-permute-start.3
  12.5 2.6 %shard_map.66.partial = f32[32,128,256]{2,1,0:T(8,128)S(1)} custom-call(s32[12,32]{1,0:T(8,128)S(4)} %get-tuple-element.25.columns, bf16[32,12,128,128]{3,2,1,0:T(8,128)(2,1)S(1)} %get-tuple-element.30.weights, bf16[48,128,256]{2,1,0:T(8,128)(2,1)S(1)} %get-tuple-element.31.extended.extended_in, f32[32,128,128]{2,1,0:T(8,128)S(1)} %get-tuple-element.32.scales, ...), custom_call_target="tpu_custom_call" | custom-call | flops 1 | bytes 1 | tf_op jit(solution)/shard_map/pallas_call | solution.py:429
  15.1 0.0 collective-permute-done.r0
  15.1 1.0 %collective-permute-done.1.r1 = bf16[4,128,256]{2,1,0:T(8,128)(2,1)S(1)} collective-permute-done((bf16[4,128,256]{2,1,0:T(8,128)(2,1)S(1)}, bf16[4,128,256]{2,1,0:T(8,128)(2,1)S(1)}, u32[]{:S(2)}, u32[]{:S(2)}) %collective-permute-start.1) | collective-permute-done | bytes 262176 | tf_op jit(solution)/shard_map/ppermute | solution.py:338
  16.1 0.7 %collective-permute-done.2.r2 = bf16[4,128,256]{2,1,0:T(8,128)(2,1)S(1)} collective-permute-done((bf16[4,128,256]{2,1,0:T(8,128)(2,1)S(1)}, bf16[4,128,256]{2,1,0:T(8,128)(2,1)S(1)}, u32[]{:S(2)}, u32[]{:S(2)}) %collective-permute-start.2) | collective-permute-done | bytes 262176 | tf_op jit(solution)/shard_map/ppermute | solution.py:338
  16.8 0.0 collective-permute-done.3.r3
  16.8 0.4 %shard_map.67 = (bf16[4,128,256]{2,1,0:T(8,128)(2,1)S(1)}, bf16[48,128,256]{2,1,0:T(8,128)(2,1)S(1)}) custom-call(s32[12,32]{1,0:T(8,128)S(4)} %get-tuple-element.25.columns, s32[1,4,4]{2,1,0:T(4,128)S(4)} %get-tuple-element.26.lists, bf16[32,12,128,128]{3,2,1,0:T(8,128)(2,1)S(1)} %get-tuple-element.30.weights, ...), custom_call_target="tpu_custom_call", output_to_operand_aliasing={{1}: (3, {})} | custom-call | flops 1 | bytes 1 | tf_op jit(solution)/shard_map/pallas_call | solution.py:438
  17.2 0.1 collective-permute-start.5
  17.3 0.3 %shard_map.70.behind = bf16[4,128,256]{2,1,0:T(8,128)(2,1)S(1)} custom-call(s32[12,32]{1,0:T(8,128)S(4)} %get-tuple-element.25.columns, s32[1,4,4]{2,1,0:T(4,128)S(4)} %get-tuple-element.26.lists, bf16[32,12,128,128]{3,2,1,0:T(8,128)(2,1)S(1)} %get-tuple-element.30.weights, bf16[48,128,256]{2,1,0:T(8,128)(2,1)S(1)} %get-tuple-element.38.extended.rest_0_, ...), custom_call_target="tpu_custom_call" | custom-call | flops 1 | bytes 1 | tf_op jit(solution)/shard_map/pallas_call | solution.py:445
  17.6 2.1 %collective-permute-start.4 = (bf16[4,128,256]{2,1,0:T(8,128)(2,1)S(1)}, bf16[4,128,256]{2,1,0:T(8,128)(2,1)S(1)}, u32[]{:S(2)}, u32[]{:S(2)}) collective-permute-start(bf16[4,128,256]{2,1,0:T(8,128)(2,1)S(1)} %shard_map.70.behind), channel_id=1, source_target_pairs={{0,8},{1,9},{2,10},{3,11},{4,12},{5,13},{6,14},{7,15},{8,0},{9,1},... | collective-permute-start | bytes 786440 | tf_op jit(solution)/shard_map/ppermute | solution.py:338
  19.7 0.5 %shard_map.72 = (bf16[4,128,256]{2,1,0:T(8,128)(2,1)S(1)}, bf16[4,128,256]{2,1,0:T(8,128)(2,1)S(1)}) custom-call(s32[12,32]{1,0:T(8,128)S(4)} %get-tuple-element.25.columns, s32[1,4,4]{2,1,0:T(4,128)S(4)} %get-tuple-element.26.lists, bf16[32,12,128,128]{3,2,1,0:T(8,128)(2,1)S(1)} %get-tuple-element.30.weights, ...), custom_call_target="tpu_custom_call" | custom-call | flops 1 | bytes 1 | tf_op jit(solution)/shard_map/pallas_call | solution.py:448
  20.3 0.1 collective-permute-start.7
  20.4 0.7 %collective-permute-start.8 = (bf16[4,128,256]{2,1,0:T(8,128)(2,1)S(1)}, bf16[4,128,256]{2,1,0:T(8,128)(2,1)S(1)}, u32[]{:S(2)}, u32[]{:S(2)}) collective-permute-start(bf16[4,128,256]{2,1,0:T(8,128)(2,1)S(1)} %get-tuple-element.43), channel_id=1, source_target_pairs={{1,2},{2,1},{3,4},{4,3},{5,6},{6,5},{9,10},{10,9},{11,12},{12,11},... | collective-permute-start | bytes 786440 | tf_op jit(solution)/shard_map/ppermute | solution.py:338
  21.1 2.6 %collective-permute-done.5.first_hop = bf16[4,128,256]{2,1,0:T(8,128)(2,1)S(1)} collective-permute-done((bf16[4,128,256]{2,1,0:T(8,128)(2,1)S(1)}, bf16[4,128,256]{2,1,0:T(8,128)(2,1)S(1)}, u32[]{:S(2)}, u32[]{:S(2)}) %collective-permute-start.5) | collective-permute-done | bytes 262176 | tf_op jit(solution)/shard_map/ppermute | solution.py:338
  23.7 1.5 %collective-permute-start.6 = (bf16[4,128,256]{2,1,0:T(8,128)(2,1)S(1)}, bf16[4,128,256]{2,1,0:T(8,128)(2,1)S(1)}, u32[]{:S(2)}, u32[]{:S(2)}) collective-permute-start(bf16[4,128,256]{2,1,0:T(8,128)(2,1)S(1)} %shard_map.71), channel_id=1, source_target_pairs={{0,1},{1,9},{2,3},{3,11},{4,5},{5,13},{6,7},{7,15},{8,16},{9,24},{... | collective-permute-start | bytes 786440 | tf_op jit(solution)/shard_map/ppermute | solution.py:338
  25.3 1.8 %shard_map.68 = (bf16[48,128,256]{2,1,0:T(8,128)(2,1)S(1)}, f32[32,128,256]{2,1,0:T(8,128)S(1)}) custom-call(s32[12,32]{1,0:T(8,128)S(4)} %get-tuple-element.25.columns, bf16[32,12,128,128]{3,2,1,0:T(8,128)(2,1)S(1)} %get-tuple-element.30.weights, bf16[48,128,256]{2,1,0:T(8,128)(2,1)S(1)} %get-tuple-element.38.extended.rest_0_, ...), custom_call_target="tpu_custom_call", output_to_operand_aliasing={{1}: (4, {})} | custom-call | flops 1 | bytes 1 | tf_op jit(solution)/shard_map/pallas_call | solution.py:460
  27.0 2.6 %shard_map.69.partial = f32[32,128,256]{2,1,0:T(8,128)S(1)} custom-call(s32[12,32]{1,0:T(8,128)S(4)} %get-tuple-element.25.columns, bf16[32,12,128,128]{3,2,1,0:T(8,128)(2,1)S(1)} %get-tuple-element.30.weights, bf16[48,128,256]{2,1,0:T(8,128)(2,1)S(1)} %get-tuple-element.39.extended.extended_in, ...), custom_call_target="tpu_custom_call", output_to_operand_aliasing={{}: (6, {})} | custom-call | flops 1 | bytes 1 | tf_op jit(solution)/shard_map/pallas_call | solution.py:429
  29.7 0.0 collective-permute-done.4.r0
  29.7 0.0 collective-permute-done.7.r2
  29.7 0.0 collective-permute-done.8.r3
  29.7 1.4 %collective-permute-done.6.r1 = bf16[4,128,256]{2,1,0:T(8,128)(2,1)S(1)} collective-permute-done((bf16[4,128,256]{2,1,0:T(8,128)(2,1)S(1)}, bf16[4,128,256]{2,1,0:T(8,128)(2,1)S(1)}, u32[]{:S(2)}, u32[]{:S(2)}) %collective-permute-start.6) | collective-permute-done | bytes 262176 | tf_op jit(solution)/shard_map/ppermute | solution.py:338
  31.1 2.8 %shard_map.73 = (f32[32,128,256]{2,1,0:T(8,128)}, bf16[48,128,256]{2,1,0:T(8,128)(2,1)S(1)}) custom-call(s32[12,32]{1,0:T(8,128)S(4)} %get-tuple-element.25.columns, bf16[32,12,128,128]{3,2,1,0:T(8,128)(2,1)S(1)} %get-tuple-element.30.weights, bf16[48,128,256]{2,1,0:T(8,128)(2,1)S(1)} %get-tuple-element.39.extended.extended_in, ...), custom_call_target="tpu_custom_call", output_to_operand_aliasing={{1}: (2, {})} | custom-call | flops 1 | bytes 1 | tf_op jit(solution)/shard_map/pallas_call | solution.py:469
  (1 shorter events, 0.0 us)
Async XLA Ops:
  0.0 4.8 %copy-start = (s32[256]{0:T(256)S(1)}, s32[256]{0:T(256)}, u32[]{:S(2)}) copy-start(s32[256]{0:T(256)} %param.10) | copy-start | bytes 3076
  0.0 4.8 %copy-start.1 = (s32[256]{0:T(256)S(1)}, s32[256]{0:T(256)}, u32[]{:S(2)}) copy-start(s32[256]{0:T(256)} %param.11) | copy-start | bytes 3076
  3.1 12.0 %collective-permute-start = (bf16[4,128,256]{2,1,0:T(8,128)(2,1)S(1)}, bf16[4,128,256]{2,1,0:T(8,128)(2,1)S(1)}, u32[]{:S(2)}, u32[]{:S(2)}) collective-permute-start(bf16[4,128,256]{2,1,0:T(8,128)(2,1)S(1)} %get-tuple-element.34), channel_id=1, source_target_pairs={{0,1},{1,0},{2,3},{3,2},{4,5},{5,4},{6,7},{7,6},{8,16},{9,17},{10,... | collective-permute-start | bytes 786440 | tf_op jit(solution)/shard_map/ppermute | solution.py:338
  4.8 11.3 %collective-permute-start.1 = (bf16[4,128,256]{2,1,0:T(8,128)(2,1)S(1)}, bf16[4,128,256]{2,1,0:T(8,128)(2,1)S(1)}, u32[]{:S(2)}, u32[]{:S(2)}) collective-permute-start(bf16[4,128,256]{2,1,0:T(8,128)(2,1)S(1)} %get-tuple-element.35), channel_id=1, source_target_pairs={{0,8},{1,9},{2,10},{3,11},{4,12},{5,13},{6,14},{7,15},{8,0},{9,1},... | collective-permute-start | bytes 786440 | tf_op jit(solution)/shard_map/ppermute | solution.py:338
  10.4 6.4 %collective-permute-start.2 = (bf16[4,128,256]{2,1,0:T(8,128)(2,1)S(1)}, bf16[4,128,256]{2,1,0:T(8,128)(2,1)S(1)}, u32[]{:S(2)}, u32[]{:S(2)}) collective-permute-start(bf16[4,128,256]{2,1,0:T(8,128)(2,1)S(1)} %get-tuple-element.36), channel_id=1, source_target_pairs={{0,8},{1,2},{2,1},{3,4},{4,3},{5,6},{6,5},{7,15},{8,24},{9,10},{10... | collective-permute-start | bytes 786440 | tf_op jit(solution)/shard_map/ppermute | solution.py:338
  12.5 4.3 %collective-permute-start.3 = (bf16[4,128,256]{2,1,0:T(8,128)(2,1)S(1)}, bf16[4,128,256]{2,1,0:T(8,128)(2,1)S(1)}, u32[]{:S(2)}, u32[]{:S(2)}) collective-permute-start(bf16[4,128,256]{2,1,0:T(8,128)(2,1)S(1)} %get-tuple-element.37), channel_id=1, source_target_pairs={{0,1},{1,0},{2,3},{3,2},{4,5},{5,4},{6,7},{7,6},{8,9},{9,8},{10,11... | collective-permute-start | bytes 786440 | tf_op jit(solution)/shard_map/ppermute | solution.py:338
  17.2 6.5 %collective-permute-start.5 = (bf16[4,128,256]{2,1,0:T(8,128)(2,1)S(1)}, bf16[4,128,256]{2,1,0:T(8,128)(2,1)S(1)}, u32[]{:S(2)}, u32[]{:S(2)}) collective-permute-start(bf16[4,128,256]{2,1,0:T(8,128)(2,1)S(1)} %get-tuple-element.41.direct), channel_id=1, source_target_pairs={{0,16},{1,0},{2,18},{3,2},{4,20},{5,4},{6,22},{7,6},{8,9},{9,25},{... | collective-permute-start | bytes 786440 | tf_op jit(solution)/shard_map/ppermute | solution.py:338
  17.6 12.0 %collective-permute-start.4 = (bf16[4,128,256]{2,1,0:T(8,128)(2,1)S(1)}, bf16[4,128,256]{2,1,0:T(8,128)(2,1)S(1)}, u32[]{:S(2)}, u32[]{:S(2)}) collective-permute-start(bf16[4,128,256]{2,1,0:T(8,128)(2,1)S(1)} %shard_map.70.behind), channel_id=1, source_target_pairs={{0,8},{1,9},{2,10},{3,11},{4,12},{5,13},{6,14},{7,15},{8,0},{9,1},... | collective-permute-start | bytes 786440 | tf_op jit(solution)/shard_map/ppermute | solution.py:338
  20.3 9.4 %collective-permute-start.7 = (bf16[4,128,256]{2,1,0:T(8,128)(2,1)S(1)}, bf16[4,128,256]{2,1,0:T(8,128)(2,1)S(1)}, u32[]{:S(2)}, u32[]{:S(2)}) collective-permute-start(bf16[4,128,256]{2,1,0:T(8,128)(2,1)S(1)} %get-tuple-element.42), channel_id=1, source_target_pairs={{0,1},{1,0},{2,3},{3,2},{4,5},{5,4},{6,7},{7,6},{8,9},{9,8},{10,11... | collective-permute-start | bytes 786440 | tf_op jit(solution)/shard_map/ppermute | solution.py:338
  20.4 9.3 %collective-permute-start.8 = (bf16[4,128,256]{2,1,0:T(8,128)(2,1)S(1)}, bf16[4,128,256]{2,1,0:T(8,128)(2,1)S(1)}, u32[]{:S(2)}, u32[]{:S(2)}) collective-permute-start(bf16[4,128,256]{2,1,0:T(8,128)(2,1)S(1)} %get-tuple-element.43), channel_id=1, source_target_pairs={{1,2},{2,1},{3,4},{4,3},{5,6},{6,5},{9,10},{10,9},{11,12},{12,11},... | collective-permute-start | bytes 786440 | tf_op jit(solution)/shard_map/ppermute | solution.py:338
  23.7 7.3 %collective-permute-start.6 = (bf16[4,128,256]{2,1,0:T(8,128)(2,1)S(1)}, bf16[4,128,256]{2,1,0:T(8,128)(2,1)S(1)}, u32[]{:S(2)}, u32[]{:S(2)}) collective-permute-start(bf16[4,128,256]{2,1,0:T(8,128)(2,1)S(1)} %shard_map.71), channel_id=1, source_target_pairs={{0,1},{1,9},{2,3},{3,11},{4,5},{5,13},{6,7},{7,15},{8,16},{9,24},{... | collective-permute-start | bytes 786440 | tf_op jit(solution)/shard_map/ppermute | solution.py:338
